TPU v7x, 128 devices: a whole 4x4x4 slice. The times are simulated.
128 devices in a mesh: section: 16 (over x, y), tp: 8 (over z, core).
Axes of the slice: x: 4, y: 4, z: 4, core: 2. Of those that a mesh axis runs over, the one named last changes fastest.
Arguments:
- queries: bfloat16 [4096, 4096], P(('section', 'tp')), may hold values from -256 to 256
- keys: bfloat16 [4096, 4096], P(('section', 'tp')), may hold values from -8 to 8
- values: bfloat16 [4096, 4096], P(('section', 'tp')), may hold values from -72 to 72
- out_grad: bfloat16 [4096, 4096], P(('section', 'tp')), may hold values from -6 to 6
- lam: float32 [16], P('tp'), may hold values from 0.2 to 0.9
- lengths: int32 [16], replicated, may hold values from 128 to 256, as said below
Outputs:
- query_grad: bfloat16 [4096, 4096], P(('section', 'tp'))
- key_grad: bfloat16 [4096, 4096], P(('section', 'tp'))
- value_grad: bfloat16 [4096, 4096], P(('section', 'tp'))
Inputs may be any that keep to these rules, and one draw needn't show every extreme that they name: `lengths`: each slice holds 128 to 256 live tokens, never more in a later slice than in an earlier one; the first slice is full.
All inputs are finite; a program needn't handle non-finite values.
Results may differ from a plain program's by a relative error of at most 0.017.
Values may be sent and summed in bfloat16 or wider, within the bound.
No kernel may reach another device: no remote copies, remote signals or barrier semaphores. Data moves between devices by JAX's collectives and lax.ppermute only.
A program may use at most 128 MiB of HBM per device.

v0:
```python
import jax
import jax.numpy as jnp
from jax import lax
from jax.sharding import PartitionSpec as P

EPSILON = 1e-05
NEGATIVE = -1e30


def slice_live(pos, lengths, slots):
    owners = jnp.arange(lengths.shape[0], dtype=jnp.int32)
    length = jnp.sum(
        jnp.where((pos // slots)[:, None] == owners[None, :], lengths[None, :], 0), axis=1
    )
    return pos % slots < length


def masked_scores(qpart, kpart, visible, scale):
    scores = jnp.einsum("qd,kd->qk", qpart, kpart, preferred_element_type=jnp.float32) * scale
    return jnp.where(visible, scores, NEGATIVE)


def softmax_parts(scores):
    top = jnp.max(scores, axis=1, keepdims=True)
    total = jnp.sum(jnp.exp(scores - top), axis=1, keepdims=True)
    return (top, total)


def head_forward(qh, kh, vh, gh, weight, visible, scale, half):
    s_one = masked_scores(qh[:, :half], kh[:, :half], visible, scale)
    s_two = masked_scores(qh[:, half:], kh[:, half:], visible, scale)
    m_one, l_one = softmax_parts(s_one)
    m_two, l_two = softmax_parts(s_two)
    p_one = jnp.exp(s_one - m_one) / l_one
    p_two = jnp.exp(s_two - m_two) / l_two
    mixed = (p_one - weight * p_two).astype(jnp.bfloat16)
    output = jnp.dot(mixed, vh, preferred_element_type=jnp.float32)
    factor = lax.rsqrt(jnp.mean(output * output, axis=1, keepdims=True) + EPSILON)
    normed = output * factor
    d_out = (factor * (gh - normed * jnp.mean(gh * normed, axis=1, keepdims=True))).astype(
        jnp.bfloat16
    )
    d_mix = jnp.einsum("qe,ke->qk", d_out, vh, preferred_element_type=jnp.float32)
    e_one = jnp.sum(d_mix * p_one, axis=1, keepdims=True)
    e_two = jnp.sum(d_mix * p_two, axis=1, keepdims=True)
    t_one = (scale * p_one * (d_mix - e_one)).astype(jnp.bfloat16)
    t_two = (-scale * weight * p_two * (d_mix - e_two)).astype(jnp.bfloat16)
    d_query = jnp.concatenate(
        [
            jnp.dot(t_one, kh[:, :half], preferred_element_type=jnp.float32),
            jnp.dot(t_two, kh[:, half:], preferred_element_type=jnp.float32),
        ],
        axis=1,
    )
    stats = jnp.concatenate([m_one, l_one, m_two, l_two, e_one, e_two], axis=1)
    return (d_query, mixed, d_out, t_one, t_two, stats)


def key_terms(t_one, t_two, mixed, d_out, qh, half):
    d_key = jnp.concatenate(
        [
            jnp.einsum("qk,qd->kd", t_one, qh[:, :half], preferred_element_type=jnp.float32),
            jnp.einsum("qk,qd->kd", t_two, qh[:, half:], preferred_element_type=jnp.float32),
        ],
        axis=1,
    )
    d_value = jnp.einsum("qk,qe->ke", mixed, d_out, preferred_element_type=jnp.float32)
    return (d_key, d_value)


def shards(queries, keys, values, out_grad, lam, lengths):
    q_loc, k_loc, v_loc, g_loc = (
        lax.all_to_all(queries, "tp", split_axis=1, concat_axis=0, tiled=True),
        lax.all_to_all(keys, "tp", split_axis=1, concat_axis=0, tiled=True),
        lax.all_to_all(values, "tp", split_axis=1, concat_axis=0, tiled=True),
        lax.all_to_all(out_grad, "tp", split_axis=1, concat_axis=0, tiled=True),
    )
    k_all, v_all = (
        lax.all_gather(k_loc, "section", axis=0, tiled=True),
        lax.all_gather(v_loc, "section", axis=0, tiled=True),
    )
    slots = q_loc.shape[0]
    heads = lam.shape[0]
    width = q_loc.shape[1] // heads
    half = width // 2
    total = k_all.shape[0]
    scale = half ** (-0.5)
    section = lax.axis_index("section")
    q_pos = section * slots + jnp.arange(slots, dtype=jnp.int32)
    own_live = slice_live(q_pos, lengths, slots)
    q_mask = own_live.astype(jnp.float32)[:, None]
    k_pos = jnp.arange(total, dtype=jnp.int32)
    visible = (k_pos[None, :] <= q_pos[:, None]) & slice_live(k_pos, lengths, slots)[None, :]
    g_masked = g_loc.astype(jnp.float32) * q_mask

    def columns(source, head):
        return lax.dynamic_slice_in_dim(source, head * width, width, 1)

    def place(buffer, piece, head):
        return lax.dynamic_update_slice_in_dim(buffer, piece, head * width, 1)

    dq_init = jnp.zeros((slots, heads * width), jnp.bfloat16)

    def head_step(head, carry):
        dq_buf, dk_buf, dv_buf = carry
        q_head = columns(q_loc, head)
        d_query, mixed, d_out, t_one, t_two, stats = head_forward(
            q_head,
            columns(k_all, head),
            columns(v_all, head),
            columns(g_masked, head),
            lam[head],
            visible,
            scale,
            half,
        )
        d_key, d_value = key_terms(t_one, t_two, mixed, d_out, q_head, half)
        return (
            place(dq_buf, d_query.astype(jnp.bfloat16), head),
            place(dk_buf, d_key, head),
            place(dv_buf, d_value, head),
        )

    acc_init = jnp.zeros((total, heads * width), jnp.float32)
    dq_all, dk_terms, dv_terms = lax.fori_loop(0, heads, head_step, (dq_init, acc_init, acc_init))
    dk_sum, dv_sum = (
        lax.psum_scatter(
            dk_terms.astype(jnp.bfloat16), "section", scatter_dimension=0, tiled=True
        ).astype(jnp.float32),
        lax.psum_scatter(
            dv_terms.astype(jnp.bfloat16), "section", scatter_dimension=0, tiled=True
        ).astype(jnp.float32),
    )
    dq_rows, dk_rows, dv_rows = (
        lax.all_to_all(dq_all, "tp", split_axis=0, concat_axis=1, tiled=True),
        lax.all_to_all(dk_sum.astype(jnp.bfloat16), "tp", split_axis=0, concat_axis=1, tiled=True),
        lax.all_to_all(dv_sum.astype(jnp.bfloat16), "tp", split_axis=0, concat_axis=1, tiled=True),
    )
    return (dq_rows, dk_rows, dv_rows)


def solution(mesh):
    in_specs = (
        P(("section", "tp"), None),
        P(("section", "tp"), None),
        P(("section", "tp"), None),
        P(("section", "tp"), None),
        P("tp"),
        P(),
    )
    out_specs = (P(("section", "tp"), None), P(("section", "tp"), None), P(("section", "tp"), None))
    return jax.shard_map(shards, mesh=mesh, in_specs=in_specs, out_specs=out_specs, check_vma=False)
```

profile of v0, /device:TPU:0, one launch (start us, length us, event | category | flops | bytes accessed | tf_op | source)
XLA Modules:
  0.0 363.1 jit_solution(8596101106910417713)
XLA Ops:
  7.2 1.0 copy.86
  8.2 12.8 %all_to_all.127 = bf16[32,8,512]{2,0,1:T(8,128)(2,1)} all-to-all(bf16[32,8,512]{2,0,1:T(8,128)(2,1)S(1)} %bitcast.75), channel_id=1, replica_groups=mesh['section'=16,'tp'=8] {'tp'}, dimensions={1} | all-to-all | bytes 524288 | tf_op jit(solution)/shard_map/all_to_all | solution.py:74
  21.1 1.0 copy.85
  22.1 10.6 %all_to_all.128 = bf16[32,8,512]{2,0,1:T(8,128)(2,1)} all-to-all(bf16[32,8,512]{2,0,1:T(8,128)(2,1)S(1)} %bitcast.76), channel_id=1, replica_groups=mesh['section'=16,'tp'=8] {'tp'}, dimensions={1} | all-to-all | bytes 524288 | tf_op jit(solution)/shard_map/all_to_all | solution.py:75
  32.7 1.7 copy.84
  34.4 3.4 all-to-all-start.3
  37.8 0.7 select_reduce_fusion.1
  38.6 0.8 select_reduce_fusion
  39.4 1.7 copy.87
  41.1 4.2 %all-to-all-done.3 = bf16[32,8,512]{2,0,1:T(8,128)(2,1)S(1)} async-done(((bf16[32,8,512]{2,0,1:T(8,128)(2,1)}), bf16[32,8,512]{2,0,1:T(8,128)(2,1)S(1)}, u32[]{:S(2)}, u32[]{:S(2)}) %all-to-all-start.3) | async-done | bytes 262176 | tf_op jit(solution)/shard_map/all_to_all | solution.py:76
  45.3 3.4 all-to-all-start
  48.7 0.1 bitcast_multiply_fusion
  48.8 7.3 %all-to-all-done = bf16[32,8,512]{2,0,1:T(8,128)(2,1)S(1)} async-done(((bf16[32,8,512]{2,0,1:T(8,128)(2,1)}), bf16[32,8,512]{2,0,1:T(8,128)(2,1)S(1)}, u32[]{:S(2)}, u32[]{:S(2)}) %all-to-all-start) | async-done | bytes 262176 | tf_op jit(solution)/shard_map/all_to_all | solution.py:73
  56.1 16.0 %all-gather.3.cloned.1.call-done = bf16[4096,512]{1,0:T(8,128)(2,1)} async-done(((bf16[256,512]{1,0:T(8,128)(2,1)}), bf16[4096,512]{1,0:T(8,128)(2,1)}) %all-gather.3.cloned.1.call-update) | async-done | bytes 4194320 | tf_op jit(solution)/shard_map/all_gather | solution.py:79
  72.1 53.3 %all-gather.5.cloned.1.call-done = bf16[4096,512]{1,0:T(8,128)(2,1)} async-done(((bf16[256,512]{1,0:T(8,128)(2,1)}), bf16[4096,512]{1,0:T(8,128)(2,1)}) %all-gather.5.cloned.1.call-update) | async-done | bytes 4194320 | tf_op jit(solution)/shard_map/all_gather | solution.py:80
  125.4 2.2 broadcast_in_dim.74.clone2
  127.7 2.2 broadcast_in_dim.74.clone
  129.9 56.1 %while.18 = (s32[]{:T(128)}, bf16[256,512]{1,0:T(8,128)(2,1)S(1)}, bf16[4096,512]{1,0:T(8,128)(2,1)}, bf16[4096,512]{1,0:T(8,128)(2,1)}, bf16[256,512]{1,0:T(8,1...) while((s32[]{:T(128)}, bf16[256,512]{1,0:T(8,128)(2,1)S(1)}, ...), condition=%wide.region_11.12_spmd.clone, body=%wide.region_2.11_spmd.clone.sunk | while | flops 3269393152 | bytes 133999936 | solution.py:125
  129.9 0.6 dynamic_slice.56
  131.2 0.1 copy.91
  131.3 2.8 fusion.77
  134.2 1.5 fusion.78
  135.7 1.3 fusion.79
  136.9 2.9 subtract_convert_fusion.2
  139.8 1.0 multiply_reduce_fusion.7
  141.0 2.1 convolution_dynamic-update-slice_fusion.2
  143.2 2.5 multiply_reduce_fusion.9
  145.6 3.1 multiply_convert_fusion.6
  148.8 0.9 convolution_convert_fusion.4
  149.6 0.5 fusion.80
  150.1 0.8 convolution_convert_fusion.5
  151.0 0.5 fusion.81
  151.5 1.6 pad_maximum_fusion.5
  153.0 3.3 copy.93
  156.3 0.1 copy.92
  156.5 1.5 constant_dynamic-update-slice_fusion.5
  158.0 0.6 dynamic_slice.56
  159.3 0.1 copy.91
  159.4 2.8 fusion.77
  162.3 1.5 fusion.78
  163.8 1.3 fusion.79
  165.0 2.9 subtract_convert_fusion.2
  167.9 1.0 multiply_reduce_fusion.7
  169.1 2.1 convolution_dynamic-update-slice_fusion.2
  171.2 2.5 multiply_reduce_fusion.9
  173.7 3.1 multiply_convert_fusion.6
  176.8 0.9 convolution_convert_fusion.4
  177.7 0.5 fusion.80
  178.2 0.9 convolution_convert_fusion.5
  179.1 0.5 fusion.81
  179.6 1.6 pad_maximum_fusion.5
  181.1 3.3 copy.93
  184.4 0.1 copy.92
  184.6 1.5 constant_dynamic-update-slice_fusion.5
  186.1 0.5 reduce-scatter.5.cloned.1.call-update
  186.7 11.8 %all_to_all.129 = bf16[8,32,512]{2,1,0:T(8,128)(2,1)S(1)} all-to-all(bf16[8,32,512]{2,1,0:T(8,128)(2,1)S(1)} %bitcast.74), channel_id=1, replica_groups=mesh['section'=16,'tp'=8] {'tp'}, dimensions={0} | all-to-all | bytes 524288 | tf_op jit(solution)/shard_map/all_to_all | solution.py:135
  198.4 65.0 %reduce-scatter.3.cloned.1.call-done = bf16[256,512]{1,0:T(8,128)(2,1)} async-done(((bf16[4096,512]{1,0:T(8,128)(2,1)}), bf16[256,512]{1,0:T(8,128)(2,1)}) %reduce-scatter.3.cloned.1.call-update) | async-done | bytes 262160 | tf_op jit(solution)/shard_map/reduce_scatter | solution.py:127
  263.4 4.4 %all-to-all-start.5 = ((bf16[8,32,512]{2,1,0:T(8,128)(2,1)}), bf16[8,32,512]{2,1,0:T(8,128)(2,1)S(1)}, u32[]{:S(2)}, u32[]{:S(2)}) async-start(bf16[8,32,512]{2,1,0:T(8,128)(2,1)} %bitcast.82), calls=%async_computation.6 | async-start | bytes 524288 | tf_op jit(solution)/shard_map/all_to_all | solution.py:136
  267.9 76.0 %reduce-scatter.5.cloned.1.call-done = bf16[256,512]{1,0:T(8,128)(2,1)} async-done(((bf16[4096,512]{1,0:T(8,128)(2,1)}), bf16[256,512]{1,0:T(8,128)(2,1)}) %reduce-scatter.5.cloned.1.call-update) | async-done | bytes 262160 | tf_op jit(solution)/shard_map/reduce_scatter | solution.py:130
  343.9 4.4 %all-to-all-start.6 = ((bf16[8,32,512]{2,1,0:T(8,128)(2,1)}), bf16[8,32,512]{2,1,0:T(8,128)(2,1)S(1)}, u32[]{:S(2)}, u32[]{:S(2)}) async-start(bf16[8,32,512]{2,1,0:T(8,128)(2,1)} %bitcast.81), calls=%async_computation.8 | async-start | bytes 524288 | tf_op jit(solution)/shard_map/all_to_all | solution.py:137
  348.3 0.7 copy.77
  349.1 0.7 copy.78
  349.8 6.1 %all-to-all-done.6 = bf16[8,32,512]{2,1,0:T(8,128)(2,1)S(1)} async-done(((bf16[8,32,512]{2,1,0:T(8,128)(2,1)}), bf16[8,32,512]{2,1,0:T(8,128)(2,1)S(1)}, u32[]{:S(2)}, u32[]{:S(2)}) %all-to-all-start.6) | async-done | bytes 262176 | tf_op jit(solution)/shard_map/all_to_all | solution.py:137
  355.9 0.7 copy.79
  (38 shorter events, 0.7 us)
Async XLA Ops:
  7.2 64.9 %all-gather.3.cloned.1.call-start = ((), (), s32[]{:S(2)}) async-start(), calls=%async_computation.9 | async-start | bytes 4456448 | tf_op jit(solution)/shard_map/all_gather | solution.py:79
  21.0 104.3 %all-gather.5.cloned.1.call-start = ((), (), s32[]{:S(2)}) async-start(), calls=%async_computation.10 | async-start | bytes 4456448 | tf_op jit(solution)/shard_map/all_gather | solution.py:80
  34.4 10.9 %all-to-all-start.3 = ((bf16[32,8,512]{2,0,1:T(8,128)(2,1)}), bf16[32,8,512]{2,0,1:T(8,128)(2,1)S(1)}, u32[]{:S(2)}, u32[]{:S(2)}) async-start(bf16[32,8,512]{2,0,1:T(8,128)(2,1)} %bitcast.46), calls=%async_computation.3 | async-start | bytes 524288 | tf_op jit(solution)/shard_map/all_to_all | solution.py:76
  45.3 10.9 %all-to-all-start = ((bf16[32,8,512]{2,0,1:T(8,128)(2,1)}), bf16[32,8,512]{2,0,1:T(8,128)(2,1)S(1)}, u32[]{:S(2)}, u32[]{:S(2)}) async-start(bf16[32,8,512]{2,0,1:T(8,128)(2,1)} %bitcast.49), calls=%async_computation | async-start | bytes 524288 | tf_op jit(solution)/shard_map/all_to_all | solution.py:73
  48.7 214.8 %reduce-scatter.3.cloned.1.call-start = ((), (), s32[]{:S(2)}) async-start(), calls=%async_computation.11 | async-start | bytes 4456448 | tf_op jit(solution)/shard_map/reduce_scatter | solution.py:127
  125.4 4.5 %copy-start.2 = (f32[2]{0:T(128)S(1)}, f32[2]{0:T(128)}, u32[]{:S(2)}) copy-start(f32[2]{0:T(128)} %param.12) | copy-start | bytes 28
  131.3 2.8 copy-start
  136.9 2.9 copy-start.1
  159.4 2.9 copy-start
  165.0 2.9 copy-start.1
  186.1 157.8 %reduce-scatter.5.cloned.1.call-start = ((), (), s32[]{:S(2)}) async-start(), calls=%async_computation.12 | async-start | bytes 4456448 | tf_op jit(solution)/shard_map/reduce_scatter | solution.py:130
  263.4 80.5 %all-to-all-start.5 = ((bf16[8,32,512]{2,1,0:T(8,128)(2,1)}), bf16[8,32,512]{2,1,0:T(8,128)(2,1)S(1)}, u32[]{:S(2)}, u32[]{:S(2)}) async-start(bf16[8,32,512]{2,1,0:T(8,128)(2,1)} %bitcast.82), calls=%async_computation.6 | async-start | bytes 524288 | tf_op jit(solution)/shard_map/all_to_all | solution.py:136
  343.9 12.0 %all-to-all-start.6 = ((bf16[8,32,512]{2,1,0:T(8,128)(2,1)}), bf16[8,32,512]{2,1,0:T(8,128)(2,1)S(1)}, u32[]{:S(2)}, u32[]{:S(2)}) async-start(bf16[8,32,512]{2,1,0:T(8,128)(2,1)} %bitcast.81), calls=%async_computation.8 | async-start | bytes 524288 | tf_op jit(solution)/shard_map/all_to_all | solution.py:137
Sparse Core Ops, SparseCore 0:
  21.2 50.8 all-gather.2
  74.2 51.0 all-gather.4
  186.2 77.1 reduce-scatter.2
  267.0 76.8 reduce-scatter.4
where the time goes:
time: 364 us; the launch traced here: 363 us
  waiting for transfers between devices  228 us (63%)
  blocking collectives  35.2 us (10%)
  matrix products  25.3 us (7%)
  local copies, waits for them, and re-layouts  23.3 us (6%)
  other arithmetic  19.7 us (5%)
  starting transfers between devices  15.8 us (4%)
  between operations  13.8 us (4%)
    reduce_scatter x1, waiting for transfers between devices, shards(): lax.psum_scatter(dv_terms.astype(jnp.bfloat16), 'section', scatter_dimens...  76 us
    reduce_scatter x1, waiting for transfers between devices, shards(): lax.psum_scatter(dk_terms.astype(jnp.bfloat16), 'section', scatter_dimens...  65 us
    all_gather x1, waiting for transfers between devices, shards(): lax.all_gather(v_loc, 'section', axis=0, tiled=True)  53.3 us
    all_gather x1, waiting for transfers between devices, shards(): lax.all_gather(k_loc, 'section', axis=0, tiled=True)  16 us
    all_to_all x1, blocking collectives, shards(): lax.all_to_all(keys, 'tp', split_axis=1, concat_axis=0, tiled=True)  12.8 us
    all_to_all x1, blocking collectives, shards(): lax.all_to_all(dq_all, 'tp', split_axis=0, concat_axis=1, tiled=True)  11.8 us
    all_to_all x1, blocking collectives, shards(): lax.all_to_all(values, 'tp', split_axis=1, concat_axis=0, tiled=True)  10.6 us
    dynamic_update_slice x8, local copies, waits for them, and re-layouts, place(): return lax.dynamic_update_slice_in_dim(buffer, piece, head * width, 1)  9.79 us
  transfers between devices with their start and end apart: 8, of which 7 were waited for; matrix products, arithmetic and copies ran while one was open for 2% of the time, Pallas kernels for 0%

commit v1 on v0

v1 whole, which is shorter than its diff:
```python
import functools

import jax
import jax.numpy as jnp
from jax import lax
from jax.experimental import pallas as pl
from jax.experimental.pallas import tpu as pltpu
from jax.sharding import Mesh
from jax.sharding import PartitionSpec as P

EPSILON = 1e-05
NEGATIVE = -1e30
LOG2E = 1.4426950408889634

STRIPE = 32
SLICES = 16
PARTS = 8
WIDTH = 256
HALF = 128
TILE = 128
GROUPS = 4
CHUNK = PARTS * TILE
ROWS = GROUPS * TILE
SECTION = ("x", "y")
SCALE = HALF ** (-0.5)


def pack_kernel(a_ref, b_ref, out_ref):
    for head in range(SLICES):
        cols = slice(head * WIDTH, (head + 1) * WIDTH)
        out_ref[head, 0] = a_ref[:, cols]
        out_ref[head, 1] = b_ref[:, cols]


def pack(a, b):
    return pl.pallas_call(
        pack_kernel,
        out_shape=jax.ShapeDtypeStruct((SLICES, 2, STRIPE, WIDTH), a.dtype),
        in_specs=[pl.BlockSpec(memory_space=pltpu.VMEM)] * 2,
        out_specs=pl.BlockSpec(memory_space=pltpu.VMEM),
        name="pack",
    )(a, b)


def unpack_pair_kernel(in_ref, a_ref, b_ref):
    for head in range(SLICES):
        cols = slice(head * WIDTH, (head + 1) * WIDTH)
        a_ref[:, cols] = in_ref[head, 0]
        b_ref[:, cols] = in_ref[head, 1]


def unpack_pair(x):
    shape = jax.ShapeDtypeStruct((STRIPE, SLICES * WIDTH), x.dtype)
    return pl.pallas_call(
        unpack_pair_kernel,
        out_shape=(shape, shape),
        in_specs=[pl.BlockSpec(memory_space=pltpu.VMEM)],
        out_specs=(pl.BlockSpec(memory_space=pltpu.VMEM),) * 2,
        name="unpack_pair",
    )(x)


def unpack_one_kernel(in_ref, a_ref):
    for head in range(SLICES):
        a_ref[:, head * WIDTH : (head + 1) * WIDTH] = in_ref[head]


def unpack_one(x):
    return pl.pallas_call(
        unpack_one_kernel,
        out_shape=jax.ShapeDtypeStruct((STRIPE, SLICES * WIDTH), x.dtype),
        in_specs=[pl.BlockSpec(memory_space=pltpu.VMEM)],
        out_specs=pl.BlockSpec(memory_space=pltpu.VMEM),
        name="unpack_one",
    )(x)


def dot_nt(a, b):
    return lax.dot_general(a, b, (((1,), (1,)), ((), ())), preferred_element_type=jnp.float32)


def dot_nn(a, b):
    return lax.dot_general(a, b, (((1,), (0,)), ((), ())), preferred_element_type=jnp.float32)


def dot_tn(a, b):
    return lax.dot_general(a, b, (((0,), (0,)), ((), ())), preferred_element_type=jnp.float32)


def fold(op, x):
    out = x[:, :128]
    for c in range(1, CHUNK // 128):
        out = op(out, x[:, c * 128 : (c + 1) * 128])
    return out


def core_kernel(lengths, where, lam, qg, *refs):
    kv_parts = refs[:PARTS]
    dq_out, own_out, sib_out = refs[PARTS : PARTS + 3]
    ks, vs, p1s, p2s, das, mixs, t1s, t2s, key_pos, sems = refs[PARTS + 3 :]

    copies = []
    for u in range(PARTS):
        for kind, dst in ((0, ks), (1, vs)):
            for j in range(GROUPS):
                copy = pltpu.make_async_copy(
                    kv_parts[u].at[pl.ds(4 * j, 4), kind],
                    dst.at[j, u],
                    sems.at[(u * 2 + kind) * GROUPS + j],
                )
                copy.start()
                copies.append(copy)

    lane = lax.broadcasted_iota(jnp.int32, (1, TILE), 1)
    for j in range(GROUPS):
        length = jnp.full((1, TILE), lengths[4 * j], jnp.int32)
        for nl in range(1, 4):
            length = jnp.where(lane // STRIPE == nl, lengths[4 * j + nl], length)
        for u in range(PARTS):
            slot = where[u] * STRIPE + lane % STRIPE
            pos = 256 * (4 * j + lane // STRIPE) + slot
            key_pos[j, :, u * TILE : (u + 1) * TILE] = jnp.where(slot < length, pos, 1 << 30)

    for copy in copies:
        copy.wait()

    weight = lam[0]
    row = lax.broadcasted_iota(jnp.int32, (TILE, 1), 0)
    row_pos = 256 * (row // STRIPE) + where[0] * STRIPE + row % STRIPE
    row_slot = where[0] * STRIPE + row % STRIPE
    zero128 = jnp.zeros((TILE, 128), jnp.float32)

    def tile(i, _):
        rows = pl.ds(pl.multiple_of(i * TILE, TILE), TILE)
        q = qg[pl.ds(i * 4, 4), 0].reshape(TILE, WIDTH)
        q1, q2 = q[:, :HALF], q[:, HALF:]
        qpos = row_pos + 1024 * i

        def scores(j, carry):
            m1, m2 = carry
            k = ks[j].reshape(CHUNK, WIDTH)
            vis = key_pos[j] <= qpos
            s1 = jnp.where(vis, dot_nt(q1, k[:, :HALF]), NEGATIVE)
            s2 = jnp.where(vis, dot_nt(q2, k[:, HALF:]), NEGATIVE)
            p1s[j] = s1
            p2s[j] = s2
            return jnp.maximum(m1, fold(jnp.maximum, s1)), jnp.maximum(m2, fold(jnp.maximum, s2))

        lowest = jnp.full((TILE, 128), NEGATIVE, jnp.float32)
        m1, m2 = lax.fori_loop(0, i + 1, scores, (lowest, lowest))
        m1 = jnp.max(m1, axis=1, keepdims=True)
        m2 = jnp.max(m2, axis=1, keepdims=True)

        def exps(j, carry):
            l1, l2 = carry
            p1 = jnp.exp2((p1s[j] - m1) * (SCALE * LOG2E))
            p2 = jnp.exp2((p2s[j] - m2) * (SCALE * LOG2E))
            p1s[j] = p1
            p2s[j] = p2
            return l1 + fold(jnp.add, p1), l2 + fold(jnp.add, p2)

        l1, l2 = lax.fori_loop(0, i + 1, exps, (zero128, zero128))
        inv1 = 1.0 / jnp.sum(l1, axis=1, keepdims=True)
        inv2 = 1.0 / jnp.sum(l2, axis=1, keepdims=True)
        winv2 = weight * inv2

        def mix(j, o):
            a = (p1s[j] * inv1 - p2s[j] * winv2).astype(jnp.bfloat16)
            mixs[j, rows, :] = a
            return o + dot_nn(a, vs[j].reshape(CHUNK, WIDTH))

        o = lax.fori_loop(0, i + 1, mix, jnp.zeros((TILE, WIDTH), jnp.float32))
        factor = lax.rsqrt(jnp.mean(o * o, axis=1, keepdims=True) + EPSILON)
        y = o * factor
        length = jnp.full((TILE, 1), lengths[4 * i], jnp.int32)
        for nl in range(1, 4):
            length = jnp.where(row // STRIPE == nl, lengths[4 * i + nl], length)
        live = (row_slot < length).astype(jnp.float32)
        g = qg[pl.ds(i * 4, 4), 1].reshape(TILE, WIDTH).astype(jnp.float32) * live
        d_out = (factor * (g - y * jnp.mean(g * y, axis=1, keepdims=True))).astype(jnp.bfloat16)

        def mix_grad(j, carry):
            e1, e2 = carry
            da = dot_nt(d_out, vs[j].reshape(CHUNK, WIDTH))
            das[j] = da
            return e1 + fold(jnp.add, da * p1s[j]), e2 + fold(jnp.add, da * p2s[j])

        e1, e2 = lax.fori_loop(0, i + 1, mix_grad, (zero128, zero128))
        e1 = jnp.sum(e1, axis=1, keepdims=True) * inv1
        e2 = jnp.sum(e2, axis=1, keepdims=True) * inv2

        def score_grad(j, carry):
            dq1, dq2 = carry
            da = das[j]
            t1 = (p1s[j] * (inv1 * (da - e1))).astype(jnp.bfloat16)
            t2 = (p2s[j] * (inv2 * (da - e2))).astype(jnp.bfloat16)
            t1s[j, rows, :] = t1
            t2s[j, rows, :] = t2
            k = ks[j].reshape(CHUNK, WIDTH)
            return dq1 + dot_nn(t1, k[:, :HALF]), dq2 + dot_nn(t2, k[:, HALF:])

        dq1, dq2 = lax.fori_loop(0, i + 1, score_grad, (zero128, zero128))
        return d_out, jnp.concatenate([dq1 * SCALE, dq2 * (-SCALE * weight)], axis=1)

    d_outs = []
    for i in range(GROUPS):
        d_out, dq = tile(i, None)
        d_outs.append(d_out)
        dq_out[4 * i : 4 * i + 4] = dq.astype(jnp.bfloat16).reshape(4, STRIPE, WIDTH)

    d_all = jnp.concatenate(d_outs, axis=0)
    q_all = qg[:, 0].reshape(ROWS, WIDTH)
    for j in range(GROUPS):
        lo = j * TILE
        for u in range(PARTS):
            cols = slice(u * TILE, (u + 1) * TILE)
            out = own_out if u < 4 else sib_out
            dk1 = dot_tn(t1s[j, lo:, cols], q_all[lo:, :HALF]) * SCALE
            dk2 = dot_tn(t2s[j, lo:, cols], q_all[lo:, HALF:]) * (-SCALE * weight)
            dv = dot_tn(mixs[j, lo:, cols], d_all[lo:])
            dk = jnp.concatenate([dk1, dk2], axis=1).astype(jnp.bfloat16)
            out[u % 4, 4 * j : 4 * j + 4, 0] = dk.reshape(4, STRIPE, WIDTH)
            out[u % 4, 4 * j : 4 * j + 4, 1] = dv.astype(jnp.bfloat16).reshape(4, STRIPE, WIDTH)


def core(lengths, where, lam, qg, kv_parts):
    vmem = pl.BlockSpec(memory_space=pltpu.VMEM)
    smem = pl.BlockSpec(memory_space=pltpu.SMEM)
    hbm = pl.BlockSpec(memory_space=pl.ANY)
    b16, f32 = jnp.bfloat16, jnp.float32
    return pl.pallas_call(
        core_kernel,
        out_shape=(
            jax.ShapeDtypeStruct((SLICES, STRIPE, WIDTH), b16),
            jax.ShapeDtypeStruct((4, SLICES, 2, STRIPE, WIDTH), b16),
            jax.ShapeDtypeStruct((4, SLICES, 2, STRIPE, WIDTH), b16),
        ),
        in_specs=[smem, smem, smem, vmem] + [hbm] * PARTS,
        out_specs=(vmem, vmem, vmem),
        scratch_shapes=[
            pltpu.VMEM((GROUPS, PARTS, 4, STRIPE, WIDTH), b16),
            pltpu.VMEM((GROUPS, PARTS, 4, STRIPE, WIDTH), b16),
            pltpu.VMEM((GROUPS, TILE, CHUNK), f32),
            pltpu.VMEM((GROUPS, TILE, CHUNK), f32),
            pltpu.VMEM((GROUPS, TILE, CHUNK), f32),
            pltpu.VMEM((GROUPS, ROWS, CHUNK), b16),
            pltpu.VMEM((GROUPS, ROWS, CHUNK), b16),
            pltpu.VMEM((GROUPS, ROWS, CHUNK), b16),
            pltpu.VMEM((GROUPS, 1, CHUNK), jnp.int32),
            pltpu.SemaphoreType.DMA((PARTS * 2 * GROUPS,)),
        ],
        compiler_params=pltpu.CompilerParams(vmem_limit_bytes=56 * 1024 * 1024),
        name="attention",
    )(lengths, where, lam, qg, *kv_parts)


def along_z(x, d):
    return lax.ppermute(x, "z", [(i, (i + d) % 4) for i in range(4)])


def swap(x):
    return lax.ppermute(x, "core", [(0, 1), (1, 0)])


def shards(queries, keys, values, out_grad, lam, lengths):
    z, c = lax.axis_index("z"), lax.axis_index("core")
    section = lax.axis_index("x") * 4 + lax.axis_index("y")

    kv = lax.all_to_all(pack(keys, values), SECTION, 0, 0, tiled=True)
    kv, qg_packed, lam = lax.optimization_barrier((kv, pack(queries, out_grad), lam))
    near = [kv] + [along_z(kv, d) for d in (1, 2, 3)]
    parts = near + [swap(x) for x in near]
    qg = lax.all_to_all(qg_packed, SECTION, 0, 0, tiled=True)
    lam_pad = jnp.broadcast_to(lam[None], (1, 2))
    lam_near = [lam_pad] + [along_z(lam_pad, d) for d in (1, 2, 3)]
    lams = jnp.concatenate(lam_near + [swap(x) for x in lam_near], axis=0)

    where = jnp.stack(
        [2 * ((z - d) % 4) + c for d in range(4)] + [2 * ((z - d) % 4) + 1 - c for d in range(4)]
    ).astype(jnp.int32)
    weight = jnp.sum(jnp.where((where == section // 2)[:, None], lams, 0.0), axis=0)
    weight = jnp.where(section % 2 == 0, weight[0], weight[1])

    d_query, own, sib = core(lengths, where, weight[None], qg, parts)

    f32, b16 = jnp.float32, jnp.bfloat16
    merged = (own.astype(f32) + swap(sib).astype(f32)).astype(b16)
    back = [along_z(merged[d], -d) for d in (1, 2, 3)]
    total = merged[0].astype(f32)
    for x in back:
        total = total + x.astype(f32)
    dq = lax.all_to_all(d_query, SECTION, 0, 0, tiled=True)
    dkv = lax.all_to_all(total.astype(b16), SECTION, 0, 0, tiled=True)
    dk, dv = unpack_pair(dkv)
    return (unpack_one(dq), dk, dv)


def solution(mesh):
    fine = Mesh(mesh.devices.reshape(4, 4, 4, 2), ("x", "y", "z", "core"))
    rows = P(("x", "y", "z", "core"), None)
    return jax.shard_map(
        shards,
        mesh=fine,
        in_specs=(rows, rows, rows, rows, P(("z", "core")), P()),
        out_specs=(rows, rows, rows),
        check_vma=False,
    )
```

time: 364 us -> 158 us (0.43)
  waiting for transfers between devices: 228 us -> 78.3 us
  blocking collectives: 35.2 us -> 0 us
  Pallas kernels: 0 us -> 31.2 us
  matrix products: 25.3 us -> 0 us
  starting transfers between devices: 15.8 us -> 35.8 us
  local copies, waits for them, and re-layouts: 23.3 us -> 4.49 us
  other arithmetic: 19.7 us -> 4.87 us
  between operations: 13.8 us -> 2.22 us
    reduce_scatter x2 -> x0, waiting for transfers between devices: 141 us -> none  [the longest x1 76 us: shards(): lax.psum_scatter(dv_terms.astype(jnp.bfloat16), 'section', scatter_dimens...]
    all_gather x2 -> x0, waiting for transfers between devices: 69.3 us -> none  [the longest x1 53.3 us: shards(): lax.all_gather(v_loc, 'section', axis=0, tiled=True)]
    ppermute x0 -> x18, waiting for transfers between devices: none -> 59.6 us  [the longest x9 52 us: along_z(): return lax.ppermute(x, 'z', [(i, (i + d) % 4) for i in range(4)])]
    all_to_all x3 -> x0, blocking collectives: 35.2 us -> none  [the longest x1 12.8 us: shards(): lax.all_to_all(keys, 'tp', split_axis=1, concat_axis=0, tiled=True)]
    pallas_call x0 -> x5, Pallas kernels: none -> 31.2 us  [the longest x1 23.9 us: core(): pl.pallas_call(core_kernel, out_shape=(jax.ShapeDtypeStruct((SLICES, STRI...]
    dot_general x18 -> x0, matrix products: 25.3 us -> none  [the longest x4 8.64 us: masked_scores(): jnp.einsum('qd,kd->qk', qpart, kpart, preferred_element_type=jnp.float32)]
    ppermute x0 -> x18, starting transfers between devices: none -> 10.7 us  [the longest x9 9.14 us: along_z(): return lax.ppermute(x, 'z', [(i, (i + d) % 4) for i in range(4)])]
    dynamic_update_slice x8 -> x0, local copies, waits for them, and re-layouts: 9.79 us -> none  [place(): return lax.dynamic_update_slice_in_dim(buffer, piece, head * width, 1)]
  transfers between devices with their start and end apart: 8 -> 22, of which waited for: 7 -> 14; matrix products, arithmetic and copies ran while one was open for 2% -> 2% of each run, Pallas kernels for 0% -> 2%
where the time goes in v1:
time: 158 us; the launch traced here: 157 us
  waiting for transfers between devices  78.3 us (50%)
  starting transfers between devices  35.8 us (23%)
  Pallas kernels  31.2 us (20%)
  other arithmetic  4.87 us (3%)
  local copies, waits for them, and re-layouts  4.49 us (3%)
  between operations  2.22 us (1%)
    ppermute x9, waiting for transfers between devices, along_z(): return lax.ppermute(x, 'z', [(i, (i + d) % 4) for i in range(4)])  52 us
    pallas_call x1, Pallas kernels, core(): pl.pallas_call(core_kernel, out_shape=(jax.ShapeDtypeStruct((SLICES, STRI...  23.9 us
    all_to_all x1, waiting for transfers between devices, shards(): kv = lax.all_to_all(pack(keys, values), SECTION, 0, 0, tiled=True)  9.63 us
    ppermute x9, starting transfers between devices, along_z(): return lax.ppermute(x, 'z', [(i, (i + d) % 4) for i in range(4)])  9.14 us
    all_to_all x1, waiting for transfers between devices, shards(): dkv = lax.all_to_all(total.astype(b16), SECTION, 0, 0, tiled=True)  9.03 us
    ppermute x9, waiting for transfers between devices, swap(): return lax.ppermute(x, 'core', [(0, 1), (1, 0)])  7.67 us
    all_to_all x1, starting transfers between devices, shards(): dkv = lax.all_to_all(total.astype(b16), SECTION, 0, 0, tiled=True)  7.13 us
    all_to_all x1, starting transfers between devices, shards(): dq = lax.all_to_all(d_query, SECTION, 0, 0, tiled=True)  7.13 us
  transfers between devices with their start and end apart: 22, of which 14 were waited for; matrix products, arithmetic and copies ran while one was open for 2% of the time, Pallas kernels for 2%

profile of v1, /device:TPU:0, one launch (start us, length us, event | category | flops | bytes accessed | tf_op | source)
XLA Modules:
  0.0 156.9 jit_solution(15299798169593326794)
XLA Ops:
  0.6 1.9 %pack.2 = bf16[16,2,32,256]{3,2,1,0:T(8,128)(2,1)} custom-call(bf16[32,4096]{1,0:T(8,128)(2,1)} %a_ref.2, bf16[32,4096]{1,0:T(8,128)(2,1)} %b_ref.2), custom_call_target="tpu_custom_call" | custom-call | tf_op jit(solution)/shard_map/pack/pallas_call | solution.py:36
  2.5 7.1 %all-to-all-start = ((bf16[16,2,32,256]{3,2,1,0:T(8,128)(2,1)}), bf16[16,2,32,256]{3,2,1,0:T(8,128)(2,1)S(1)}, u32[]{:S(2)}, u32[]{:S(2)}) async-start(bf16[16,2,32,256]{3,2,1,0:T(8,128)(2,1)} %pack.2), calls=%async_computation | async-start | bytes 1048576 | tf_op jit(solution)/shard_map/all_to_all | solution.py:269
  9.6 1.9 %pack.3 = bf16[16,2,32,256]{3,2,1,0:T(8,128)(2,1)} custom-call(bf16[32,4096]{1,0:T(8,128)(2,1)} %a_ref.3, bf16[32,4096]{1,0:T(8,128)(2,1)} %b_ref.3), custom_call_target="tpu_custom_call" | custom-call | tf_op jit(solution)/shard_map/pack/pallas_call | solution.py:36
  11.5 9.6 %all-to-all-done.refs_0_ = bf16[16,2,32,256]{3,2,1,0:T(8,128)(2,1)S(1)} async-done(((bf16[16,2,32,256]{3,2,1,0:T(8,128)(2,1)}), bf16[16,2,32,256]{3,2,1,0:T(8,128)(2,1)S(1)}, u32[]{:S(2)}, u32[]{:S(2)}) %all-to-all-start) | async-done | bytes 524320 | tf_op jit(solution)/shard_map/all_to_all | solution.py:269
  21.1 4.0 %collective-permute-start.9 = (bf16[16,2,32,256]{3,2,1,0:T(8,128)(2,1)S(1)}, bf16[16,2,32,256]{3,2,1,0:T(8,128)(2,1)S(1)}, u32[]{:S(2)}, u32[]{:S(2)}) collective-permute-start(bf16[16,2,32,256]{3,2,1,0:T(8,128)(2,1)S(1)} %all-to-all-done.refs_0_), channel_id=1, source_target_pairs={{0,6},{2,0},{4,2},{6,4},{1,7},{3,1},{5,3},{7,5},{8,14},{10,8},{12,... | collective-permute-start | bytes 1572872 | tf_op jit(solution)/shard_map/ppermute | solution.py:258
  25.2 0.0 collective-permute-start.8
  25.2 1.3 collective-permute-start.7
  26.4 0.0 collective-permute-start.10
  26.4 19.7 %collective-permute-done.9.refs_3_ = bf16[16,2,32,256]{3,2,1,0:T(8,128)(2,1)S(1)} collective-permute-done((bf16[16,2,32,256]{3,2,1,0:T(8,128)(2,1)S(1)}, bf16[16,2,32,256]{3,2,1,0:T(8,128)(2,1)S(1)}, u32[]{:S(2)}, u32[]{:S(2)}) %collective-permute-start.9) | collective-permute-done | bytes 524320 | tf_op jit(solution)/shard_map/ppermute | solution.py:258
  46.1 0.0 collective-permute-start.13
  46.1 0.0 collective-permute-done.8.refs_2_
  46.1 0.5 collective-permute-start.12
  46.6 2.9 %collective-permute-done.7.refs_1_ = bf16[16,2,32,256]{3,2,1,0:T(8,128)(2,1)S(1)} collective-permute-done((bf16[16,2,32,256]{3,2,1,0:T(8,128)(2,1)S(1)}, bf16[16,2,32,256]{3,2,1,0:T(8,128)(2,1)S(1)}, u32[]{:S(2)}, u32[]{:S(2)}) %collective-permute-start.7) | collective-permute-done | bytes 524320 | tf_op jit(solution)/shard_map/ppermute | solution.py:258
  49.5 0.0 collective-permute-start.11
  49.5 3.8 %all-to-all-start.1 = ((bf16[16,2,32,256]{3,2,1,0:T(8,128)(2,1)}), bf16[16,2,32,256]{3,2,1,0:T(8,128)(2,1)S(1)}, u32[]{:S(2)}, u32[]{:S(2)}) async-start(bf16[16,2,32,256]{3,2,1,0:T(8,128)(2,1)} %pack.3), calls=%async_computation.1 | async-start | bytes 1048576 | tf_op jit(solution)/shard_map/all_to_all | solution.py:273
  53.4 0.1 stack.35.where
  53.5 0.1 copy.9
  53.6 0.3 collective-permute-start.3
  53.9 0.8 collective-permute-done.3
  54.7 0.9 collective-permute-start.2
  55.6 0.1 copy.13
  55.7 2.6 %collective-permute-done.2 = f32[1,2]{1,0:T(1,128)S(1)} collective-permute-done((f32[1,2]{1,0:T(1,128)S(1)}, f32[1,2]{1,0:T(1,128)S(1)}, u32[]{:S(2)}, u32[]{:S(2)}) %collective-permute-start.2) | collective-permute-done | bytes 40 | tf_op jit(solution)/shard_map/ppermute | solution.py:258
  58.3 0.6 collective-permute-start.1
  58.9 0.1 copy.12
  59.0 4.4 %collective-permute-done.1 = f32[1,2]{1,0:T(1,128)S(1)} collective-permute-done((f32[1,2]{1,0:T(1,128)S(1)}, f32[1,2]{1,0:T(1,128)S(1)}, u32[]{:S(2)}, u32[]{:S(2)}) %collective-permute-start.1) | collective-permute-done | bytes 40 | tf_op jit(solution)/shard_map/ppermute | solution.py:258
  63.3 0.0 collective-permute-start
  63.3 0.1 copy.11
  63.4 4.7 %collective-permute-done = f32[1,2]{1,0:T(1,128)S(1)} collective-permute-done((f32[1,2]{1,0:T(1,128)S(1)}, f32[1,2]{1,0:T(1,128)S(1)}, u32[]{:S(2)}, u32[]{:S(2)}) %collective-permute-start) | collective-permute-done | bytes 40 | tf_op jit(solution)/shard_map/ppermute | solution.py:258
  68.1 0.0 collective-permute-start.6
  68.1 0.1 copy.10
  68.2 1.0 collective-permute-done.6
  69.2 0.2 collective-permute-start.5
  69.4 0.1 copy.16
  69.5 0.8 collective-permute-done.5
  70.3 0.2 collective-permute-start.4
  70.5 0.1 copy.15
  70.6 0.8 collective-permute-done.4
  71.4 0.1 copy.14
  71.5 0.1 concatenate.7
  71.6 0.1 select_reduce_fusion
  71.7 0.6 fusion.3
  73.6 0.0 all-to-all-done.1.qg
  73.7 0.0 collective-permute-done.13.refs_7_
  73.7 0.0 collective-permute-done.12.refs_6_
  73.8 0.7 copy-done.2
  74.5 0.2 copy-done.7
  74.7 23.9 %attention.1 = (bf16[16,32,256]{2,1,0:T(8,128)(2,1)}, bf16[4,16,2,32,256]{4,3,2,1,0:T(8,128)(2,1)}, bf16[4,16,2,32,256]{4,3,2,1,0:T(8,128)(2,1)}) custom-call(s32[16]{0:T(128)} %lengths.1, s32[8]{0:T(128)} %copy-done.8, f32[1]{0:T(128)} %bitcast.11.lam, bf16[16,2,32,256]{3,2,1,0:T(8,128)(2,1)} %copy-done.2, bf16[16,2,32,256]{3,2,1,0:T(8,128)(2,1)} %copy-done.1, ...), custom_call_target="tpu_custom_call" | custom-call | tf_op jit(solution)/shard_map/attention/pallas_call | solution.py:231
  98.6 0.3 collective-permute-start.14
  98.9 4.2 %collective-permute-done.14 = bf16[4,16,2,32,256]{4,3,2,1,0:T(8,128)(2,1)S(1)} collective-permute-done((bf16[4,16,2,32,256]{4,3,2,1,0:T(8,128)(2,1)}, bf16[4,16,2,32,256]{4,3,2,1,0:T(8,128)(2,1)S(1)}, u32[]{:S(2)}, u32[]{:S(2)}) %collective-permute-start.14) | collective-permute-done | bytes 2097184 | tf_op jit(solution)/shard_map/ppermute | solution.py:262
  103.1 2.5 %add_convert_fusion = bf16[4,16,2,32,256]{4,3,2,1,0:T(8,128)(2,1)S(1)} fusion(bf16[4,16,2,32,256]{4,3,2,1,0:T(8,128)(2,1)S(1)} %collective-permute-done.14, bf16[4,16,2,32,256]{4,3,2,1,0:T(8,128)(2,1)} %get-tuple-element.15), kind=kLoop, calls=%fused_computation | loop fusion | flops 4194304 | bytes 6291456 | tf_op jit(solution)/shard_map/convert_element_type | solution.py:287
  105.6 1.2 slice_bitcast_fusion.2
  106.8 0.9 collective-permute-start.15
  107.7 1.1 collective-permute-start.17
  108.9 0.3 collective-permute-start.16
  109.2 7.1 %all-to-all-start.2 = ((bf16[16,32,256]{2,1,0:T(8,128)(2,1)}), bf16[16,32,256]{2,1,0:T(8,128)(2,1)S(1)}, u32[]{:S(2)}, u32[]{:S(2)}) async-start(bf16[16,32,256]{2,1,0:T(8,128)(2,1)} %get-tuple-element.14), calls=%async_computation.2 | async-start | bytes 524288 | tf_op jit(solution)/shard_map/all_to_all | solution.py:292
  116.3 5.5 %collective-permute-done.15 = bf16[16,2,32,256]{3,2,1,0:T(8,128)(2,1)S(1)} collective-permute-done((bf16[16,2,32,256]{3,2,1,0:T(8,128)(2,1)}, bf16[16,2,32,256]{3,2,1,0:T(8,128)(2,1)S(1)}, u32[]{:S(2)}, u32[]{:S(2)}) %collective-permute-start.15) | collective-permute-done | bytes 524320 | tf_op jit(solution)/shard_map/ppermute | solution.py:258
  121.8 12.3 %collective-permute-done.17 = bf16[16,2,32,256]{3,2,1,0:T(8,128)(2,1)S(1)} collective-permute-done((bf16[16,2,32,256]{3,2,1,0:T(8,128)(2,1)}, bf16[16,2,32,256]{3,2,1,0:T(8,128)(2,1)S(1)}, u32[]{:S(2)}, u32[]{:S(2)}) %collective-permute-start.17) | collective-permute-done | bytes 524320 | tf_op jit(solution)/shard_map/ppermute | solution.py:258
  134.1 2.2 %fusion.2 = bf16[16,2,32,256]{3,2,1,0:T(8,128)(2,1)} fusion(bf16[16,2,32,256]{3,2,1,0:T(8,128)(2,1)S(1)} %collective-permute-done.17, bf16[16,2,32,256]{3,2,1,0:T(8,128)(2,1)} %collective-permute-done.16, bf16[16,2,32,256]{3,2,1,0:T(8,128)(2,1)S(1)} %collective-permute-done.15, bf16[4,16,2,32,256]{4,3,2,1,0:T(8,128)(2,1)S(1)} %add_convert_fusion), kind=kLoop, calls=%fused_computation.4 | loop fusion | flops 2097152 | bytes 2621440 | tf_op jit(solution)/shard_map/convert_element_type | solution.py:293
  136.4 0.0 all-to-all-done.2.in_ref
  136.4 7.1 %all-to-all-start.3 = ((bf16[16,2,32,256]{3,2,1,0:T(8,128)(2,1)}), bf16[16,2,32,256]{3,2,1,0:T(8,128)(2,1)S(1)}, u32[]{:S(2)}, u32[]{:S(2)}) async-start(bf16[16,2,32,256]{3,2,1,0:T(8,128)(2,1)} %fusion.2), calls=%async_computation.3 | async-start | bytes 1048576 | tf_op jit(solution)/shard_map/all_to_all | solution.py:293
  143.5 1.7 %unpack_one.1 = bf16[32,4096]{1,0:T(8,128)(2,1)} custom-call(bf16[16,32,256]{2,1,0:T(8,128)(2,1)} %copy-done.3), custom_call_target="tpu_custom_call" | custom-call | tf_op jit(solution)/shard_map/unpack_one/pallas_call | solution.py:69
  145.2 9.0 %all-to-all-done.3.in_ref = bf16[16,2,32,256]{3,2,1,0:T(8,128)(2,1)S(1)} async-done(((bf16[16,2,32,256]{3,2,1,0:T(8,128)(2,1)}), bf16[16,2,32,256]{3,2,1,0:T(8,128)(2,1)S(1)}, u32[]{:S(2)}, u32[]{:S(2)}) %all-to-all-start.3) | async-done | bytes 524320 | tf_op jit(solution)/shard_map/all_to_all | solution.py:293
  154.2 0.8 copy-done
  155.0 1.9 %unpack_pair.1 = (bf16[32,4096]{1,0:T(8,128)(2,1)}, bf16[32,4096]{1,0:T(8,128)(2,1)}) custom-call(bf16[16,2,32,256]{3,2,1,0:T(8,128)(2,1)} %copy-done), custom_call_target="tpu_custom_call" | custom-call | tf_op jit(solution)/shard_map/unpack_pair/pallas_call | solution.py:54
  (21 shorter events, 0.0 us)
Async XLA Ops:
  0.6 52.9 %copy-start.9 = (f32[2]{0:T(128)S(1)}, f32[2]{0:T(128)}, u32[]{:S(2)}) copy-start(f32[2]{0:T(128)} %param.10) | copy-start | bytes 28
  2.5 18.6 %all-to-all-start = ((bf16[16,2,32,256]{3,2,1,0:T(8,128)(2,1)}), bf16[16,2,32,256]{3,2,1,0:T(8,128)(2,1)S(1)}, u32[]{:S(2)}, u32[]{:S(2)}) async-start(bf16[16,2,32,256]{3,2,1,0:T(8,128)(2,1)} %pack.2), calls=%async_computation | async-start | bytes 1048576 | tf_op jit(solution)/shard_map/all_to_all | solution.py:269
  21.1 52.6 %copy-start.1 = (bf16[16,2,32,256]{3,2,1,0:T(8,128)(2,1)}, bf16[16,2,32,256]{3,2,1,0:T(8,128)(2,1)S(1)}, u32[]{:S(2)}) copy-start(bf16[16,2,32,256]{3,2,1,0:T(8,128)(2,1)S(1)} %all-to-all-done.refs_0_) | copy-start | bytes 1572868
  21.1 25.0 %collective-permute-start.9 = (bf16[16,2,32,256]{3,2,1,0:T(8,128)(2,1)S(1)}, bf16[16,2,32,256]{3,2,1,0:T(8,128)(2,1)S(1)}, u32[]{:S(2)}, u32[]{:S(2)}) collective-permute-start(bf16[16,2,32,256]{3,2,1,0:T(8,128)(2,1)S(1)} %all-to-all-done.refs_0_), channel_id=1, source_target_pairs={{0,6},{2,0},{4,2},{6,4},{1,7},{3,1},{5,3},{7,5},{8,14},{10,8},{12,... | collective-permute-start | bytes 1572872 | tf_op jit(solution)/shard_map/ppermute | solution.py:258
  25.2 21.0 %collective-permute-start.8 = (bf16[16,2,32,256]{3,2,1,0:T(8,128)(2,1)S(1)}, bf16[16,2,32,256]{3,2,1,0:T(8,128)(2,1)S(1)}, u32[]{:S(2)}, u32[]{:S(2)}) collective-permute-start(bf16[16,2,32,256]{3,2,1,0:T(8,128)(2,1)S(1)} %all-to-all-done.refs_0_), channel_id=1, source_target_pairs={{0,4},{2,6},{4,0},{6,2},{1,5},{3,7},{5,1},{7,3},{8,12},{10,14},{12... | collective-permute-start | bytes 1572872 | tf_op jit(solution)/shard_map/ppermute | solution.py:258
  25.2 24.4 %collective-permute-start.7 = (bf16[16,2,32,256]{3,2,1,0:T(8,128)(2,1)S(1)}, bf16[16,2,32,256]{3,2,1,0:T(8,128)(2,1)S(1)}, u32[]{:S(2)}, u32[]{:S(2)}) collective-permute-start(bf16[16,2,32,256]{3,2,1,0:T(8,128)(2,1)S(1)} %all-to-all-done.refs_0_), channel_id=1, source_target_pairs={{0,2},{2,4},{4,6},{6,0},{1,3},{3,5},{5,7},{7,1},{8,10},{10,12},{12... | collective-permute-start | bytes 1572872 | tf_op jit(solution)/shard_map/ppermute | solution.py:258
  26.4 47.2 %collective-permute-start.10 = (bf16[16,2,32,256]{3,2,1,0:T(8,128)(2,1)S(1)}, bf16[16,2,32,256]{3,2,1,0:T(8,128)(2,1)S(1)}, u32[]{:S(2)}, u32[]{:S(2)}) collective-permute-start(bf16[16,2,32,256]{3,2,1,0:T(8,128)(2,1)S(1)} %all-to-all-done.refs_0_), channel_id=1, source_target_pairs={{0,1},{1,0},{2,3},{3,2},{4,5},{5,4},{6,7},{7,6},{8,9},{9,8},{10,11... | collective-permute-start | bytes 1572872 | tf_op jit(solution)/shard_map/ppermute | solution.py:262
  46.1 27.6 %copy-start.4 = (bf16[16,2,32,256]{3,2,1,0:T(8,128)(2,1)}, bf16[16,2,32,256]{3,2,1,0:T(8,128)(2,1)S(1)}, u32[]{:S(2)}) copy-start(bf16[16,2,32,256]{3,2,1,0:T(8,128)(2,1)S(1)} %collective-permute-done.9.refs_3_) | copy-start | bytes 1572868
  46.1 27.6 %collective-permute-start.13 = (bf16[16,2,32,256]{3,2,1,0:T(8,128)(2,1)S(1)}, bf16[16,2,32,256]{3,2,1,0:T(8,128)(2,1)}, u32[]{:S(2)}, u32[]{:S(2)}) collective-permute-start(bf16[16,2,32,256]{3,2,1,0:T(8,128)(2,1)S(1)} %collective-permute-done.9.refs_3_), channel_id=1, source_target_pairs={{0,1},{1,0},{2,3},{3,2},{4,5},{5,4},{6,7},{7,6},{8,9},{9,8},{10,11... | collective-permute-start | bytes 1572872 | tf_op jit(solution)/shard_map/ppermute | solution.py:262
  46.1 27.6 %copy-start.5 = (bf16[16,2,32,256]{3,2,1,0:T(8,128)(2,1)}, bf16[16,2,32,256]{3,2,1,0:T(8,128)(2,1)S(1)}, u32[]{:S(2)}) copy-start(bf16[16,2,32,256]{3,2,1,0:T(8,128)(2,1)S(1)} %collective-permute-done.8.refs_2_) | copy-start | bytes 1572868
  46.1 27.6 %collective-permute-start.12 = (bf16[16,2,32,256]{3,2,1,0:T(8,128)(2,1)S(1)}, bf16[16,2,32,256]{3,2,1,0:T(8,128)(2,1)}, u32[]{:S(2)}, u32[]{:S(2)}) collective-permute-start(bf16[16,2,32,256]{3,2,1,0:T(8,128)(2,1)S(1)} %collective-permute-done.8.refs_2_), channel_id=1, source_target_pairs={{0,1},{1,0},{2,3},{3,2},{4,5},{5,4},{6,7},{7,6},{8,9},{9,8},{10,11... | collective-permute-start | bytes 1572872 | tf_op jit(solution)/shard_map/ppermute | solution.py:262
  49.5 24.2 %copy-start.6 = (bf16[16,2,32,256]{3,2,1,0:T(8,128)(2,1)}, bf16[16,2,32,256]{3,2,1,0:T(8,128)(2,1)S(1)}, u32[]{:S(2)}) copy-start(bf16[16,2,32,256]{3,2,1,0:T(8,128)(2,1)S(1)} %collective-permute-done.7.refs_1_) | copy-start | bytes 1572868
  49.5 24.2 %collective-permute-start.11 = (bf16[16,2,32,256]{3,2,1,0:T(8,128)(2,1)S(1)}, bf16[16,2,32,256]{3,2,1,0:T(8,128)(2,1)}, u32[]{:S(2)}, u32[]{:S(2)}) collective-permute-start(bf16[16,2,32,256]{3,2,1,0:T(8,128)(2,1)S(1)} %collective-permute-done.7.refs_1_), channel_id=1, source_target_pairs={{0,1},{1,0},{2,3},{3,2},{4,5},{5,4},{6,7},{7,6},{8,9},{9,8},{10,11... | collective-permute-start | bytes 1572872 | tf_op jit(solution)/shard_map/ppermute | solution.py:262
  49.5 24.1 %all-to-all-start.1 = ((bf16[16,2,32,256]{3,2,1,0:T(8,128)(2,1)}), bf16[16,2,32,256]{3,2,1,0:T(8,128)(2,1)S(1)}, u32[]{:S(2)}, u32[]{:S(2)}) async-start(bf16[16,2,32,256]{3,2,1,0:T(8,128)(2,1)} %pack.3), calls=%async_computation.1 | async-start | bytes 1048576 | tf_op jit(solution)/shard_map/all_to_all | solution.py:273
  53.5 20.3 %copy-start.8 = (s32[8]{0:T(128)}, s32[8]{0:T(128)S(1)}, u32[]{:S(2)}) copy-start(s32[8]{0:T(128)S(1)} %stack.35.where) | copy-start | bytes 100
  53.6 1.1 collective-permute-start.3
  54.7 3.5 %collective-permute-start.2 = (f32[1,2]{1,0:T(1,128)S(1)}, f32[1,2]{1,0:T(1,128)S(1)}, u32[]{:S(2)}, u32[]{:S(2)}) collective-permute-start(f32[1,2]{1,0:T(1,128)S(1)} %bitcast.25), channel_id=1, source_target_pairs={{0,6},{2,0},{4,2},{6,4},{1,7},{3,1},{5,3},{7,5},{8,14},{10,8},{12,... | collective-permute-start | bytes 32 | tf_op jit(solution)/shard_map/ppermute | solution.py:258
  58.3 5.0 %collective-permute-start.1 = (f32[1,2]{1,0:T(1,128)S(1)}, f32[1,2]{1,0:T(1,128)S(1)}, u32[]{:S(2)}, u32[]{:S(2)}) collective-permute-start(f32[1,2]{1,0:T(1,128)S(1)} %bitcast.26), channel_id=1, source_target_pairs={{0,4},{2,6},{4,0},{6,2},{1,5},{3,7},{5,1},{7,3},{8,12},{10,14},{12... | collective-permute-start | bytes 32 | tf_op jit(solution)/shard_map/ppermute | solution.py:258
  63.3 4.8 %collective-permute-start = (f32[1,2]{1,0:T(1,128)S(1)}, f32[1,2]{1,0:T(1,128)S(1)}, u32[]{:S(2)}, u32[]{:S(2)}) collective-permute-start(f32[1,2]{1,0:T(1,128)S(1)} %bitcast.27), channel_id=1, source_target_pairs={{0,2},{2,4},{4,6},{6,0},{1,3},{3,5},{5,7},{7,1},{8,10},{10,12},{12... | collective-permute-start | bytes 32 | tf_op jit(solution)/shard_map/ppermute | solution.py:258
  68.1 1.1 collective-permute-start.6
  69.2 1.1 collective-permute-start.5
  70.3 1.1 collective-permute-start.4
  73.7 0.8 copy-start.2
  73.7 1.0 copy-start.7
  98.6 4.5 %collective-permute-start.14 = (bf16[4,16,2,32,256]{4,3,2,1,0:T(8,128)(2,1)}, bf16[4,16,2,32,256]{4,3,2,1,0:T(8,128)(2,1)S(1)}, u32[]{:S(2)}, u32[]{:S(2)}) collective-permute-start(bf16[4,16,2,32,256]{4,3,2,1,0:T(8,128)(2,1)} %get-tuple-element.16), channel_id=1, source_target_pairs={{0,1},{1,0},{2,3},{3,2},{4,5},{5,4},{6,7},{7,6},{8,9},{9,8},{10,11... | collective-permute-start | bytes 6291464 | tf_op jit(solution)/shard_map/ppermute | solution.py:262
  106.8 15.0 %collective-permute-start.15 = (bf16[16,2,32,256]{3,2,1,0:T(8,128)(2,1)}, bf16[16,2,32,256]{3,2,1,0:T(8,128)(2,1)S(1)}, u32[]{:S(2)}, u32[]{:S(2)}) collective-permute-start(bf16[16,2,32,256]{3,2,1,0:T(8,128)(2,1)} %get-tuple-element.19), channel_id=1, source_target_pairs={{0,6},{2,0},{4,2},{6,4},{1,7},{3,1},{5,3},{7,5},{8,14},{10,8},{12,... | collective-permute-start | bytes 1572872 | tf_op jit(solution)/shard_map/ppermute | solution.py:258
  107.7 26.4 %collective-permute-start.17 = (bf16[16,2,32,256]{3,2,1,0:T(8,128)(2,1)}, bf16[16,2,32,256]{3,2,1,0:T(8,128)(2,1)S(1)}, u32[]{:S(2)}, u32[]{:S(2)}) collective-permute-start(bf16[16,2,32,256]{3,2,1,0:T(8,128)(2,1)} %get-tuple-element.20), channel_id=1, source_target_pairs={{0,2},{2,4},{4,6},{6,0},{1,3},{3,5},{5,7},{7,1},{8,10},{10,12},{12... | collective-permute-start | bytes 1572872 | tf_op jit(solution)/shard_map/ppermute | solution.py:258
  108.9 25.3 %collective-permute-start.16 = (bf16[16,2,32,256]{3,2,1,0:T(8,128)(2,1)}, bf16[16,2,32,256]{3,2,1,0:T(8,128)(2,1)}, u32[]{:S(2)}, u32[]{:S(2)}) collective-permute-start(bf16[16,2,32,256]{3,2,1,0:T(8,128)(2,1)} %get-tuple-element.21), channel_id=1, source_target_pairs={{0,4},{2,6},{4,0},{6,2},{1,5},{3,7},{5,1},{7,3},{8,12},{10,14},{12... | collective-permute-start | bytes 1572872 | tf_op jit(solution)/shard_map/ppermute | solution.py:258
  109.2 27.2 %all-to-all-start.2 = ((bf16[16,32,256]{2,1,0:T(8,128)(2,1)}), bf16[16,32,256]{2,1,0:T(8,128)(2,1)S(1)}, u32[]{:S(2)}, u32[]{:S(2)}) async-start(bf16[16,32,256]{2,1,0:T(8,128)(2,1)} %get-tuple-element.14), calls=%async_computation.2 | async-start | bytes 524288 | tf_op jit(solution)/shard_map/all_to_all | solution.py:292
  136.4 7.1 %copy-start.3 = (bf16[16,32,256]{2,1,0:T(8,128)(2,1)}, bf16[16,32,256]{2,1,0:T(8,128)(2,1)S(1)}, u32[]{:S(2)}) copy-start(bf16[16,32,256]{2,1,0:T(8,128)(2,1)S(1)} %all-to-all-done.2.in_ref) | copy-start | bytes 786436
  136.4 17.9 %all-to-all-start.3 = ((bf16[16,2,32,256]{3,2,1,0:T(8,128)(2,1)}), bf16[16,2,32,256]{3,2,1,0:T(8,128)(2,1)S(1)}, u32[]{:S(2)}, u32[]{:S(2)}) async-start(bf16[16,2,32,256]{3,2,1,0:T(8,128)(2,1)} %fusion.2), calls=%async_computation.3 | async-start | bytes 1048576 | tf_op jit(solution)/shard_map/all_to_all | solution.py:293
  154.2 0.8 copy-start

commit v2 on v1

v2 whole, which is shorter than its diff:
```python
import functools

import jax
import jax.numpy as jnp
from jax import lax
from jax.experimental import pallas as pl
from jax.experimental.pallas import tpu as pltpu
from jax.sharding import Mesh
from jax.sharding import PartitionSpec as P

EPSILON = 1e-05
NEGATIVE = -1e30
LOG2E = 1.4426950408889634

STRIPE = 32
SLICES = 16
PARTS = 8
WIDTH = 256
HALF = 128
TILE = 128
GROUPS = 4
CHUNK = PARTS * TILE
ROWS = GROUPS * TILE
PAIRS = PARTS // 2
SECTION = ("x", "y")
ALL = ("x", "y", "z", "core")
SCALE = HALF ** (-0.5)


def pack_kernel(a_ref, b_ref, out_ref):
    for head in range(SLICES):
        cols = slice(head * WIDTH, (head + 1) * WIDTH)
        out_ref[head, 0] = a_ref[:, cols]
        out_ref[head, 1] = b_ref[:, cols]


def pack(a, b):
    return pl.pallas_call(
        pack_kernel,
        out_shape=jax.ShapeDtypeStruct((SLICES, 2, STRIPE, WIDTH), a.dtype),
        in_specs=[pl.BlockSpec(memory_space=pltpu.VMEM)] * 2,
        out_specs=pl.BlockSpec(memory_space=pltpu.VMEM),
        name="pack",
    )(a, b)


def unpack_pair_kernel(in_ref, a_ref, b_ref):
    for head in range(SLICES):
        cols = slice(head * WIDTH, (head + 1) * WIDTH)
        a_ref[:, cols] = in_ref[head, 0]
        b_ref[:, cols] = in_ref[head, 1]


def unpack_pair(x):
    shape = jax.ShapeDtypeStruct((STRIPE, SLICES * WIDTH), x.dtype)
    return pl.pallas_call(
        unpack_pair_kernel,
        out_shape=(shape, shape),
        in_specs=[pl.BlockSpec(memory_space=pltpu.VMEM)],
        out_specs=(pl.BlockSpec(memory_space=pltpu.VMEM),) * 2,
        name="unpack_pair",
    )(x)


def unpack_one_kernel(in_ref, a_ref):
    for head in range(SLICES):
        a_ref[:, head * WIDTH : (head + 1) * WIDTH] = in_ref[head]


def unpack_one(x):
    return pl.pallas_call(
        unpack_one_kernel,
        out_shape=jax.ShapeDtypeStruct((STRIPE, SLICES * WIDTH), x.dtype),
        in_specs=[pl.BlockSpec(memory_space=pltpu.VMEM)],
        out_specs=pl.BlockSpec(memory_space=pltpu.VMEM),
        name="unpack_one",
    )(x)


def dot_nt(a, b):
    return lax.dot_general(a, b, (((1,), (1,)), ((), ())), preferred_element_type=jnp.float32)


def dot_nn(a, b):
    return lax.dot_general(a, b, (((1,), (0,)), ((), ())), preferred_element_type=jnp.float32)


def dot_tn(a, b):
    return lax.dot_general(a, b, (((0,), (0,)), ((), ())), preferred_element_type=jnp.float32)


def fold(op, x):
    out = x[:, :128]
    for c in range(1, x.shape[1] // 128):
        out = op(out, x[:, c * 128 : (c + 1) * 128])
    return out


def core_kernel(lengths, where, lams, qg, *refs):
    kv_parts = refs[:PARTS]
    dq_out, *term_outs = refs[PARTS : PARTS + 1 + PARTS]
    ks, vs, p1s, p2s, das, mixs, t1s, t2s, outs, stat1, stat2, wide, key_pos, in_sems, out_sems = refs[
        2 * PARTS + 1 :
    ]

    copies = []
    for kind, dst in ((0, ks), (1, vs)):
        for u in range(PARTS):
            copy = pltpu.make_async_copy(
                kv_parts[u].at[:, :, kind], dst.at[:, u], in_sems.at[kind * PARTS + u]
            )
            copy.start()
            copies.append(copy)

    lane = lax.broadcasted_iota(jnp.int32, (1, TILE), 1)
    for j in range(GROUPS):
        length = jnp.full((1, TILE), lengths[4 * j], jnp.int32)
        for nl in range(1, 4):
            length = jnp.where(lane // STRIPE == nl, lengths[4 * j + nl], length)
        for u in range(PARTS):
            slot = where[u] * STRIPE + lane % STRIPE
            pos = 256 * (4 * j + lane // STRIPE) + slot
            key_pos[j, :, u * TILE : (u + 1) * TILE] = jnp.where(slot < length, pos, 1 << 30)

    weight = lams[where[PARTS] % 2]
    row = lax.broadcasted_iota(jnp.int32, (ROWS, 1), 0)
    row_slot = where[0] * STRIPE + row % STRIPE
    row_pos = 256 * (row // STRIPE) + row_slot
    q = qg[:, 0].reshape(ROWS, WIDTH)
    q1, q2 = q[:, :HALF], q[:, HALF:]
    stat1[...] = jnp.full((ROWS, 128), NEGATIVE, jnp.float32)
    stat2[...] = jnp.full((ROWS, 128), NEGATIVE, jnp.float32)

    for copy in copies[:PARTS]:
        copy.wait()
    for j in range(GROUPS):
        lo = j * TILE

        for pair in range(PAIRS):
            k = ks[j, slice(2 * pair, 2 * pair + 2)].reshape(2 * TILE, WIDTH)
            cols = slice(pair * 2 * TILE, (pair + 1) * 2 * TILE)
            vis = key_pos[j, :, cols] <= row_pos[lo:]
            s1 = jnp.where(vis, dot_nt(q1[lo:], k[:, :HALF]), NEGATIVE)
            s2 = jnp.where(vis, dot_nt(q2[lo:], k[:, HALF:]), NEGATIVE)
            p1s[j, lo:, cols] = s1
            p2s[j, lo:, cols] = s2
            stat1[lo:] = jnp.maximum(stat1[lo:], fold(jnp.maximum, s1))
            stat2[lo:] = jnp.maximum(stat2[lo:], fold(jnp.maximum, s2))

    m1 = jnp.max(stat1[...], axis=1, keepdims=True)
    m2 = jnp.max(stat2[...], axis=1, keepdims=True)
    stat1[...] = jnp.zeros((ROWS, 128), jnp.float32)
    stat2[...] = jnp.zeros((ROWS, 128), jnp.float32)
    for j in range(GROUPS):
        lo = j * TILE

        for pair in range(PAIRS):
            cols = slice(pair * 2 * TILE, (pair + 1) * 2 * TILE)
            p1 = jnp.exp2((p1s[j, lo:, cols] - m1[lo:]) * (SCALE * LOG2E))
            p2 = jnp.exp2((p2s[j, lo:, cols] - m2[lo:]) * (SCALE * LOG2E))
            p1s[j, lo:, cols] = p1
            p2s[j, lo:, cols] = p2
            stat1[lo:] += fold(jnp.add, p1)
            stat2[lo:] += fold(jnp.add, p2)

    inv1 = 1.0 / jnp.sum(stat1[...], axis=1, keepdims=True)
    inv2 = 1.0 / jnp.sum(stat2[...], axis=1, keepdims=True)
    winv2 = weight * inv2

    for copy in copies[PARTS:]:
        copy.wait()
    wide[...] = jnp.zeros((ROWS, WIDTH), jnp.float32)
    for j in range(GROUPS):
        lo = j * TILE

        for pair in range(PAIRS):
            cols = slice(pair * 2 * TILE, (pair + 1) * 2 * TILE)
            a = p1s[j, lo:, cols] * inv1[lo:] - p2s[j, lo:, cols] * winv2[lo:]
            mixs[j, lo:, cols] = a.astype(jnp.bfloat16)

        wide[lo:] += dot_nn(mixs[j, lo:], vs[j].reshape(CHUNK, WIDTH))

    o = wide[...]
    factor = lax.rsqrt(jnp.mean(o * o, axis=1, keepdims=True) + EPSILON)
    y = o * factor
    length = jnp.full((ROWS, 1), lengths[0], jnp.int32)
    for n in range(1, SLICES):
        length = jnp.where(row // STRIPE == n, lengths[n], length)
    live = (row_slot < length).astype(jnp.float32)
    g = qg[:, 1].reshape(ROWS, WIDTH).astype(jnp.float32) * live
    d_out = (factor * (g - y * jnp.mean(g * y, axis=1, keepdims=True))).astype(jnp.bfloat16)

    stat1[...] = jnp.zeros((ROWS, 128), jnp.float32)
    stat2[...] = jnp.zeros((ROWS, 128), jnp.float32)
    for j in range(GROUPS):
        lo = j * TILE

        for pair in range(PAIRS):
            cols = slice(pair * 2 * TILE, (pair + 1) * 2 * TILE)
            da = dot_nt(d_out[lo:], vs[j, slice(2 * pair, 2 * pair + 2)].reshape(2 * TILE, WIDTH))
            das[j, lo:, cols] = da
            stat1[lo:] += fold(jnp.add, da * p1s[j, lo:, cols])
            stat2[lo:] += fold(jnp.add, da * p2s[j, lo:, cols])

    e1 = jnp.sum(stat1[...], axis=1, keepdims=True) * inv1
    e2 = jnp.sum(stat2[...], axis=1, keepdims=True) * inv2

    wide[...] = jnp.zeros((ROWS, WIDTH), jnp.float32)
    out_copies = []
    for j in range(GROUPS):
        lo = j * TILE

        for pair in range(PAIRS):
            cols = slice(pair * 2 * TILE, (pair + 1) * 2 * TILE)
            da = das[j, lo:, cols]
            t1 = p1s[j, lo:, cols] * (inv1[lo:] * (da - e1[lo:]))
            t2 = p2s[j, lo:, cols] * (inv2[lo:] * (da - e2[lo:]))
            t1s[j, lo:, cols] = t1.astype(jnp.bfloat16)
            t2s[j, lo:, cols] = t2.astype(jnp.bfloat16)

        k = ks[j].reshape(CHUNK, WIDTH)
        wide[lo:, :HALF] += dot_nn(t1s[j, lo:], k[:, :HALF])
        wide[lo:, HALF:] += dot_nn(t2s[j, lo:], k[:, HALF:])

        for pair in range(PAIRS):
            cols = slice(pair * 2 * TILE, (pair + 1) * 2 * TILE)
            dk1 = dot_tn(t1s[j, lo:, cols], q1[lo:]) * SCALE
            dk2 = dot_tn(t2s[j, lo:, cols], q2[lo:]) * (-SCALE * weight)
            dv = dot_tn(mixs[j, lo:, cols], d_out[lo:]).astype(jnp.bfloat16)
            dk = jnp.concatenate([dk1, dk2], axis=1).astype(jnp.bfloat16)
            outs[j, slice(2 * pair, 2 * pair + 2), :, 0] = dk.reshape(2, 4, STRIPE, WIDTH)
            outs[j, slice(2 * pair, 2 * pair + 2), :, 1] = dv.reshape(2, 4, STRIPE, WIDTH)

        for u in range(PARTS):
            copy = pltpu.make_async_copy(
                outs.at[j, u], term_outs[u].at[pl.ds(4 * j, 4)], out_sems.at[PARTS * j + u]
            )
            copy.start()
            out_copies.append(copy)

    dq_out[:, :, :HALF] = (wide[:, :HALF] * SCALE).astype(jnp.bfloat16).reshape(SLICES, STRIPE, HALF)
    dq_out[:, :, HALF:] = (
        (wide[:, HALF:] * (-SCALE * weight)).astype(jnp.bfloat16).reshape(SLICES, STRIPE, HALF)
    )
    for copy in out_copies:
        copy.wait()


def core(lengths, where, lams, qg, kv_parts):
    vmem = pl.BlockSpec(memory_space=pltpu.VMEM)
    smem = pl.BlockSpec(memory_space=pltpu.SMEM)
    hbm = pl.BlockSpec(memory_space=pl.ANY)
    b16, f32 = jnp.bfloat16, jnp.float32
    parts = [x.reshape(GROUPS, 4, 2, STRIPE, WIDTH) for x in kv_parts]
    return pl.pallas_call(
        core_kernel,
        out_shape=(
            jax.ShapeDtypeStruct((SLICES, STRIPE, WIDTH), b16),
        )
        + (jax.ShapeDtypeStruct((SLICES, 2, STRIPE, WIDTH), b16),) * PARTS,
        in_specs=[smem, smem, smem, vmem] + [hbm] * PARTS,
        out_specs=(vmem,) + (hbm,) * PARTS,
        scratch_shapes=[
            pltpu.VMEM((GROUPS, PARTS, 4, STRIPE, WIDTH), b16),
            pltpu.VMEM((GROUPS, PARTS, 4, STRIPE, WIDTH), b16),
            pltpu.VMEM((GROUPS, ROWS, CHUNK), f32),
            pltpu.VMEM((GROUPS, ROWS, CHUNK), f32),
            pltpu.VMEM((GROUPS, ROWS, CHUNK), f32),
            pltpu.VMEM((GROUPS, ROWS, CHUNK), b16),
            pltpu.VMEM((GROUPS, ROWS, CHUNK), b16),
            pltpu.VMEM((GROUPS, ROWS, CHUNK), b16),
            pltpu.VMEM((GROUPS, PARTS, 4, 2, STRIPE, WIDTH), b16),
            pltpu.VMEM((ROWS, 128), f32),
            pltpu.VMEM((ROWS, 128), f32),
            pltpu.VMEM((ROWS, WIDTH), f32),
            pltpu.VMEM((GROUPS, 1, CHUNK), jnp.int32),
            pltpu.SemaphoreType.DMA((PARTS * 2,)),
            pltpu.SemaphoreType.DMA((GROUPS * PARTS,)),
        ],
        compiler_params=pltpu.CompilerParams(vmem_limit_bytes=60 * 1024 * 1024),
        name="attention",
    )(lengths, where, lams, qg, *parts)


def along_z(x, d):
    return lax.ppermute(x, "z", [(i, (i + d) % 4) for i in range(4)])


def swap(x):
    return lax.ppermute(x, "core", [(0, 1), (1, 0)])


def shards(queries, keys, values, out_grad, lam, lengths):
    z, c = lax.axis_index("z"), lax.axis_index("core")
    section = lax.axis_index("x") * 4 + lax.axis_index("y")
    where = jnp.stack(
        [2 * ((z - d) % 4) + c for d in range(4)]
        + [2 * ((z - d) % 4) + 1 - c for d in range(4)]
        + [section]
    ).astype(jnp.int32)

    kv = lax.all_to_all(pack(keys, values), SECTION, 0, 0, tiled=True)
    lams = lax.ppermute(
        lam, ALL, [(s * 8 + t, (2 * t + s // 8) * 8 + s % 8) for s in range(SLICES) for t in range(PARTS)]
    )
    kv, qg, lams = lax.optimization_barrier((kv, pack(queries, out_grad), lams))
    near = [along_z(kv, d) for d in (1, 2, 3)]
    qg = lax.all_to_all(qg, SECTION, 0, 0, tiled=True)
    *near, qg = lax.optimization_barrier((*near, qg))
    near = [kv] + near

    d_query, *terms = core(lengths, where, lams, qg, near + [swap(x) for x in near])

    f32, b16 = jnp.float32, jnp.bfloat16
    dq = lax.all_to_all(d_query, SECTION, 0, 0, tiled=True)
    merged = [
        (own.astype(f32) + swap(other).astype(f32)).astype(b16)
        for own, other in zip(terms[:4], terms[4:])
    ]
    total = merged[0].astype(f32)
    for d in (1, 2, 3):
        total = total + along_z(merged[d], -d).astype(f32)
    dkv = lax.all_to_all(total.astype(b16), SECTION, 0, 0, tiled=True)
    dk, dv = unpack_pair(dkv)
    return (unpack_one(dq), dk, dv)


def solution(mesh):
    fine = Mesh(mesh.devices.reshape(4, 4, 4, 2), ("x", "y", "z", "core"))
    rows = P(ALL, None)
    return jax.shard_map(
        shards,
        mesh=fine,
        in_specs=(rows, rows, rows, rows, P(("z", "core")), P()),
        out_specs=(rows, rows, rows),
        check_vma=False,
    )
```

time: 158 us -> 124 us (0.78)
  waiting for transfers between devices: 78.3 us -> 60.1 us
  Pallas kernels: 31.2 us -> 23.2 us
  starting transfers between devices: 35.8 us -> 32.1 us
  local copies, waits for them, and re-layouts: 4.49 us -> 2.7 us
    ppermute x9 -> x6, waiting for transfers between devices: 52 us -> 27.7 us  [along_z(): return lax.ppermute(x, 'z', [(i, (i + d) % 4) for i in range(4)])]
    all_to_all x1, waiting for transfers between devices: 0.01 us -> 10 us  [shards(): qg = lax.all_to_all(qg, SECTION, 0, 0, tiled=True)]
    pallas_call x1, Pallas kernels: 23.9 us -> 15.9 us  [core(): pl.pallas_call(core_kernel, out_shape=(jax.ShapeDtypeStruct((SLICES, STRI...]
    ppermute x9 -> x8, waiting for transfers between devices: 7.67 us -> 3.45 us  [swap(): return lax.ppermute(x, 'core', [(0, 1), (1, 0)])]
    all_to_all x1, starting transfers between devices: 7.13 us -> 4.65 us  [shards(): dkv = lax.all_to_all(total.astype(b16), SECTION, 0, 0, tiled=True)]
    all_to_all x1, starting transfers between devices: 7.13 us -> 4.67 us  [shards(): dq = lax.all_to_all(d_query, SECTION, 0, 0, tiled=True)]
    ppermute x9 -> x6, starting transfers between devices: 9.14 us -> 7.8 us  [along_z(): return lax.ppermute(x, 'z', [(i, (i + d) % 4) for i in range(4)])]
  transfers between devices with their start and end apart: 22 -> 19, of which waited for: 14 -> 12; matrix products, arithmetic and copies ran while one was open for 2% -> 4% of each run, Pallas kernels for 2% -> 3%
where the time goes in v2:
time: 124 us; the launch traced here: 123 us
  waiting for transfers between devices  60.1 us (48%)
  starting transfers between devices  32.1 us (26%)
  Pallas kernels  23.2 us (19%)
  other arithmetic  4.12 us (3%)
  local copies, waits for them, and re-layouts  2.7 us (2%)
    ppermute x6, waiting for transfers between devices, along_z(): return lax.ppermute(x, 'z', [(i, (i + d) % 4) for i in range(4)])  27.7 us
    pallas_call x1, Pallas kernels, core(): pl.pallas_call(core_kernel, out_shape=(jax.ShapeDtypeStruct((SLICES, STRI...  15.9 us
    all_to_all x1, waiting for transfers between devices, shards(): qg = lax.all_to_all(qg, SECTION, 0, 0, tiled=True)  10 us
    all_to_all x1, waiting for transfers between devices, shards(): dkv = lax.all_to_all(total.astype(b16), SECTION, 0, 0, tiled=True)  10 us
    all_to_all x1, waiting for transfers between devices, shards(): kv = lax.all_to_all(pack(keys, values), SECTION, 0, 0, tiled=True)  8.94 us
    ppermute x6, starting transfers between devices, along_z(): return lax.ppermute(x, 'z', [(i, (i + d) % 4) for i in range(4)])  7.8 us
    all_to_all x1, starting transfers between devices, shards(): kv = lax.all_to_all(pack(keys, values), SECTION, 0, 0, tiled=True)  7.25 us
    all_to_all x1, starting transfers between devices, shards(): qg = lax.all_to_all(qg, SECTION, 0, 0, tiled=True)  5.18 us
  transfers between devices with their start and end apart: 19, of which 12 were waited for; matrix products, arithmetic and copies ran while one was open for 4% of the time, Pallas kernels for 3%

profile of v2, /device:TPU:0, one launch (start us, length us, event | category | flops | bytes accessed | tf_op | source)
XLA Modules:
  0.0 123.0 jit_solution(13020104730409695577)
XLA Ops:
  0.6 1.9 %pack.2 = bf16[16,2,32,256]{3,2,1,0:T(8,128)(2,1)} custom-call(bf16[32,4096]{1,0:T(8,128)(2,1)} %a_ref.2, bf16[32,4096]{1,0:T(8,128)(2,1)} %b_ref.2), custom_call_target="tpu_custom_call" | custom-call | tf_op jit(solution)/shard_map/pack/pallas_call | solution.py:38
  2.5 0.0 copy-start.12
  2.5 7.2 %all-to-all-start = ((bf16[16,2,32,256]{3,2,1,0:T(8,128)(2,1)}), bf16[16,2,32,256]{3,2,1,0:T(8,128)(2,1)S(1)}, u32[]{:S(2)}, u32[]{:S(2)}) async-start(bf16[16,2,32,256]{3,2,1,0:T(8,128)(2,1)} %pack.2), calls=%async_computation | async-start | bytes 1048576 | tf_op jit(solution)/shard_map/all_to_all | solution.py:302
  9.7 0.0 copy-done.12
  9.8 0.7 collective-permute-start
  10.4 1.9 %pack.3 = bf16[16,2,32,256]{3,2,1,0:T(8,128)(2,1)} custom-call(bf16[32,4096]{1,0:T(8,128)(2,1)} %a_ref.3, bf16[32,4096]{1,0:T(8,128)(2,1)} %b_ref.3), custom_call_target="tpu_custom_call" | custom-call | tf_op jit(solution)/shard_map/pack/pallas_call | solution.py:38
  12.3 0.0 collective-permute-done.lams
  12.3 0.0 copy-start.11
  12.3 8.9 %all-to-all-done = bf16[16,2,32,256]{3,2,1,0:T(8,128)(2,1)S(1)} async-done(((bf16[16,2,32,256]{3,2,1,0:T(8,128)(2,1)}), bf16[16,2,32,256]{3,2,1,0:T(8,128)(2,1)S(1)}, u32[]{:S(2)}, u32[]{:S(2)}) %all-to-all-start) | async-done | bytes 524320 | tf_op jit(solution)/shard_map/all_to_all | solution.py:302
  21.2 4.0 %collective-permute-start.3 = (bf16[16,2,32,256]{3,2,1,0:T(8,128)(2,1)S(1)}, bf16[16,2,32,256]{3,2,1,0:T(8,128)(2,1)S(1)}, u32[]{:S(2)}, u32[]{:S(2)}) collective-permute-start(bf16[16,2,32,256]{3,2,1,0:T(8,128)(2,1)S(1)} %all-to-all-done), channel_id=1, source_target_pairs={{0,6},{2,0},{4,2},{6,4},{1,7},{3,1},{5,3},{7,5},{8,14},{10,8},{12,... | collective-permute-start | bytes 1572872 | tf_op jit(solution)/shard_map/ppermute | solution.py:286
  25.3 0.0 collective-permute-start.2
  25.3 1.3 %collective-permute-start.1 = (bf16[16,2,32,256]{3,2,1,0:T(8,128)(2,1)S(1)}, bf16[16,2,32,256]{3,2,1,0:T(8,128)(2,1)S(1)}, u32[]{:S(2)}, u32[]{:S(2)}) collective-permute-start(bf16[16,2,32,256]{3,2,1,0:T(8,128)(2,1)S(1)} %all-to-all-done), channel_id=1, source_target_pairs={{0,2},{2,4},{4,6},{6,0},{1,3},{3,5},{5,7},{7,1},{8,10},{10,12},{12... | collective-permute-start | bytes 1572872 | tf_op jit(solution)/shard_map/ppermute | solution.py:286
  26.5 0.0 copy-done.11
  26.5 5.2 %all-to-all-start.1 = ((bf16[16,2,32,256]{3,2,1,0:T(8,128)(2,1)}), bf16[16,2,32,256]{3,2,1,0:T(8,128)(2,1)S(1)}, u32[]{:S(2)}, u32[]{:S(2)}) async-start(bf16[16,2,32,256]{3,2,1,0:T(8,128)(2,1)} %pack.3), calls=%async_computation.1 | async-start | bytes 1048576 | tf_op jit(solution)/shard_map/all_to_all | solution.py:308
  31.7 0.1 collective-permute-start.4
  31.8 10.0 %all-to-all-done.1.qg = bf16[16,2,32,256]{3,2,1,0:T(8,128)(2,1)S(1)} async-done(((bf16[16,2,32,256]{3,2,1,0:T(8,128)(2,1)}), bf16[16,2,32,256]{3,2,1,0:T(8,128)(2,1)S(1)}, u32[]{:S(2)}, u32[]{:S(2)}) %all-to-all-start.1) | async-done | bytes 524320 | tf_op jit(solution)/shard_map/all_to_all | solution.py:308
  41.8 4.6 %collective-permute-done.3 = bf16[16,2,32,256]{3,2,1,0:T(8,128)(2,1)S(1)} collective-permute-done((bf16[16,2,32,256]{3,2,1,0:T(8,128)(2,1)S(1)}, bf16[16,2,32,256]{3,2,1,0:T(8,128)(2,1)S(1)}, u32[]{:S(2)}, u32[]{:S(2)}) %collective-permute-start.3) | collective-permute-done | bytes 524320 | tf_op jit(solution)/shard_map/ppermute | solution.py:286
  46.4 0.0 collective-permute-done.2
  46.5 3.4 %collective-permute-done.1 = bf16[16,2,32,256]{3,2,1,0:T(8,128)(2,1)S(1)} collective-permute-done((bf16[16,2,32,256]{3,2,1,0:T(8,128)(2,1)S(1)}, bf16[16,2,32,256]{3,2,1,0:T(8,128)(2,1)S(1)}, u32[]{:S(2)}, u32[]{:S(2)}) %collective-permute-start.1) | collective-permute-done | bytes 524320 | tf_op jit(solution)/shard_map/ppermute | solution.py:286
  49.9 0.0 collective-permute-start.5
  49.9 0.5 collective-permute-start.6
  50.4 0.0 collective-permute-start.7
  50.4 0.0 copy-done.1
  50.4 0.7 stack.39.where
  51.1 0.0 collective-permute-done.4
  51.1 0.8 collective-permute-done.5
  51.9 0.7 collective-permute-done.6
  52.7 0.7 collective-permute-done.7
  53.4 0.0 copy-done.2
  53.4 0.0 copy-done.7
  53.4 0.0 copy-done.8
  53.4 0.0 copy-done.9
  53.4 0.0 copy-done.10
  53.4 15.9 %attention.1 = (bf16[16,32,256]{2,1,0:T(8,128)(2,1)}, bf16[16,2,32,256]{3,2,1,0:T(8,128)(2,1)}, bf16[16,2,32,256]{3,2,1,0:T(8,128)(2,1)}, bf16[16,2,32,256]{3,2,...) custom-call(s32[16]{0:T(128)} %lengths.1, ...), custom_call_target="tpu_custom_call" | custom-call | tf_op jit(solution)/shard_map/attention/pallas_call | solution.py:255
  69.4 0.4 collective-permute-start.9
  69.8 0.4 collective-permute-start.11
  70.2 0.1 collective-permute-start.8
  70.3 0.4 collective-permute-start.13
  70.7 1.1 collective-permute-done.9
  71.8 1.3 %add_convert_fusion.3 = bf16[16,2,32,256]{3,2,1,0:T(8,128)(2,1)S(1)} fusion(bf16[16,2,32,256]{3,2,1,0:T(8,128)(2,1)S(1)} %collective-permute-done.9, bf16[16,2,32,256]{3,2,1,0:T(8,128)(2,1)} %get-tuple-element.31), kind=kLoop, calls=%fused_computation.3 | loop fusion | flops 1048576 | bytes 1572864 | tf_op jit(solution)/shard_map/convert_element_type | solution.py:317
  73.1 1.0 collective-permute-start.10
  74.1 0.0 collective-permute-done.11
  74.1 0.0 copy-done.5
  74.1 0.2 add_convert_fusion.2
  74.3 0.4 collective-permute-start.12
  74.6 0.0 collective-permute-done.13
  74.6 0.5 copy-done.4
  75.1 0.2 add_convert_fusion.1
  75.3 0.0 copy-start.6
  75.3 1.2 collective-permute-start.14
  76.5 4.7 %all-to-all-start.2 = ((bf16[16,32,256]{2,1,0:T(8,128)(2,1)}), bf16[16,32,256]{2,1,0:T(8,128)(2,1)S(1)}, u32[]{:S(2)}, u32[]{:S(2)}) async-start(bf16[16,32,256]{2,1,0:T(8,128)(2,1)} %get-tuple-element.28), calls=%async_computation.2 | async-start | bytes 524288 | tf_op jit(solution)/shard_map/all_to_all | solution.py:315
  81.2 0.0 collective-permute-done.8
  81.2 6.7 %collective-permute-done.10 = bf16[16,2,32,256]{3,2,1,0:T(8,128)(2,1)S(1)} collective-permute-done((bf16[16,2,32,256]{3,2,1,0:T(8,128)(2,1)S(1)}, bf16[16,2,32,256]{3,2,1,0:T(8,128)(2,1)S(1)}, u32[]{:S(2)}, u32[]{:S(2)}) %collective-permute-start.10) | collective-permute-done | bytes 524320 | tf_op jit(solution)/shard_map/ppermute | solution.py:286
  87.9 2.9 %collective-permute-done.12 = bf16[16,2,32,256]{3,2,1,0:T(8,128)(2,1)} collective-permute-done((bf16[16,2,32,256]{3,2,1,0:T(8,128)(2,1)S(1)}, bf16[16,2,32,256]{3,2,1,0:T(8,128)(2,1)}, u32[]{:S(2)}, u32[]{:S(2)}) %collective-permute-start.12) | collective-permute-done | bytes 524320 | tf_op jit(solution)/shard_map/ppermute | solution.py:286
  90.8 10.1 %collective-permute-done.14 = bf16[16,2,32,256]{3,2,1,0:T(8,128)(2,1)} collective-permute-done((bf16[16,2,32,256]{3,2,1,0:T(8,128)(2,1)S(1)}, bf16[16,2,32,256]{3,2,1,0:T(8,128)(2,1)}, u32[]{:S(2)}, u32[]{:S(2)}) %collective-permute-start.14) | collective-permute-done | bytes 524320 | tf_op jit(solution)/shard_map/ppermute | solution.py:286
  100.9 0.0 copy-done.6
  100.9 2.4 %add_convert_fusion = bf16[16,2,32,256]{3,2,1,0:T(8,128)(2,1)} fusion(bf16[16,2,32,256]{3,2,1,0:T(8,128)(2,1)} %collective-permute-done.14, bf16[16,2,32,256]{3,2,1,0:T(8,128)(2,1)} %collective-permute-done.12, bf16[16,2,32,256]{3,2,1,0:T(8,128)(2,1)S(1)} %collective-permute-done.10, bf16[16,2,32,256]{3,2,1,0:T(8,128)(2,1)S(1)} %collective-permute-done.8, ...), kind=kLoop, calls=%fused_computation | loop fusion | flops 3145728 | bytes 3145728 | tf_op jit(solution)/shard_map/convert_element_type | solution.py:323
  103.3 0.0 all-to-all-done.2.in_ref
  103.3 0.7 copy-done.3
  104.0 4.7 %all-to-all-start.3 = ((bf16[16,2,32,256]{3,2,1,0:T(8,128)(2,1)}), bf16[16,2,32,256]{3,2,1,0:T(8,128)(2,1)S(1)}, u32[]{:S(2)}, u32[]{:S(2)}) async-start(bf16[16,2,32,256]{3,2,1,0:T(8,128)(2,1)} %add_convert_fusion), calls=%async_computation.3 | async-start | bytes 1048576 | tf_op jit(solution)/shard_map/all_to_all | solution.py:323
  108.7 1.7 %unpack_one.1 = bf16[32,4096]{1,0:T(8,128)(2,1)} custom-call(bf16[16,32,256]{2,1,0:T(8,128)(2,1)} %copy-done.3), custom_call_target="tpu_custom_call" | custom-call | tf_op jit(solution)/shard_map/unpack_one/pallas_call | solution.py:71
  110.4 10.0 %all-to-all-done.3.in_ref = bf16[16,2,32,256]{3,2,1,0:T(8,128)(2,1)S(1)} async-done(((bf16[16,2,32,256]{3,2,1,0:T(8,128)(2,1)}), bf16[16,2,32,256]{3,2,1,0:T(8,128)(2,1)S(1)}, u32[]{:S(2)}, u32[]{:S(2)}) %all-to-all-start.3) | async-done | bytes 524320 | tf_op jit(solution)/shard_map/all_to_all | solution.py:323
  120.4 0.8 copy-done
  121.2 1.9 %unpack_pair.1 = (bf16[32,4096]{1,0:T(8,128)(2,1)}, bf16[32,4096]{1,0:T(8,128)(2,1)}) custom-call(bf16[16,2,32,256]{3,2,1,0:T(8,128)(2,1)} %copy-done), custom_call_target="tpu_custom_call" | custom-call | tf_op jit(solution)/shard_map/unpack_pair/pallas_call | solution.py:56
  (10 shorter events, 0.0 us)
Async XLA Ops:
  2.5 7.3 %copy-start.12 = (f32[2]{0:T(128)S(1)}, f32[2]{0:T(128)}, u32[]{:S(2)}) copy-start(f32[2]{0:T(128)} %param.10) | copy-start | bytes 28
  2.5 18.8 %all-to-all-start = ((bf16[16,2,32,256]{3,2,1,0:T(8,128)(2,1)}), bf16[16,2,32,256]{3,2,1,0:T(8,128)(2,1)S(1)}, u32[]{:S(2)}, u32[]{:S(2)}) async-start(bf16[16,2,32,256]{3,2,1,0:T(8,128)(2,1)} %pack.2), calls=%async_computation | async-start | bytes 1048576 | tf_op jit(solution)/shard_map/all_to_all | solution.py:302
  9.8 2.5 %collective-permute-start = (f32[2]{0:T(128)S(1)}, f32[2]{0:T(128)S(1)}, u32[]{:S(2)}, u32[]{:S(2)}) collective-permute-start(f32[2]{0:T(128)S(1)} %copy-done.12), channel_id=1, source_target_pairs={{0,0},{1,16},{2,32},{3,48},{4,64},{5,80},{6,96},{7,112},{8,1},{9,1... | collective-permute-start | bytes 32 | tf_op jit(solution)/shard_map/ppermute | solution.py:303
  12.3 14.2 %copy-start.11 = (f32[2]{0:T(128)}, f32[2]{0:T(128)S(1)}, u32[]{:S(2)}) copy-start(f32[2]{0:T(128)S(1)} %collective-permute-done.lams) | copy-start | bytes 28
  21.2 29.1 %copy-start.1 = (bf16[16,2,32,256]{3,2,1,0:T(8,128)(2,1)}, bf16[16,2,32,256]{3,2,1,0:T(8,128)(2,1)S(1)}, u32[]{:S(2)}) copy-start(bf16[16,2,32,256]{3,2,1,0:T(8,128)(2,1)S(1)} %all-to-all-done) | copy-start | bytes 1572868
  21.2 25.2 %collective-permute-start.3 = (bf16[16,2,32,256]{3,2,1,0:T(8,128)(2,1)S(1)}, bf16[16,2,32,256]{3,2,1,0:T(8,128)(2,1)S(1)}, u32[]{:S(2)}, u32[]{:S(2)}) collective-permute-start(bf16[16,2,32,256]{3,2,1,0:T(8,128)(2,1)S(1)} %all-to-all-done), channel_id=1, source_target_pairs={{0,6},{2,0},{4,2},{6,4},{1,7},{3,1},{5,3},{7,5},{8,14},{10,8},{12,... | collective-permute-start | bytes 1572872 | tf_op jit(solution)/shard_map/ppermute | solution.py:286
  25.3 21.2 %collective-permute-start.2 = (bf16[16,2,32,256]{3,2,1,0:T(8,128)(2,1)S(1)}, bf16[16,2,32,256]{3,2,1,0:T(8,128)(2,1)S(1)}, u32[]{:S(2)}, u32[]{:S(2)}) collective-permute-start(bf16[16,2,32,256]{3,2,1,0:T(8,128)(2,1)S(1)} %all-to-all-done), channel_id=1, source_target_pairs={{0,4},{2,6},{4,0},{6,2},{1,5},{3,7},{5,1},{7,3},{8,12},{10,14},{12... | collective-permute-start | bytes 1572872 | tf_op jit(solution)/shard_map/ppermute | solution.py:286
  25.3 24.6 %collective-permute-start.1 = (bf16[16,2,32,256]{3,2,1,0:T(8,128)(2,1)S(1)}, bf16[16,2,32,256]{3,2,1,0:T(8,128)(2,1)S(1)}, u32[]{:S(2)}, u32[]{:S(2)}) collective-permute-start(bf16[16,2,32,256]{3,2,1,0:T(8,128)(2,1)S(1)} %all-to-all-done), channel_id=1, source_target_pairs={{0,2},{2,4},{4,6},{6,0},{1,3},{3,5},{5,7},{7,1},{8,10},{10,12},{12... | collective-permute-start | bytes 1572872 | tf_op jit(solution)/shard_map/ppermute | solution.py:286
  26.5 15.3 %all-to-all-start.1 = ((bf16[16,2,32,256]{3,2,1,0:T(8,128)(2,1)}), bf16[16,2,32,256]{3,2,1,0:T(8,128)(2,1)S(1)}, u32[]{:S(2)}, u32[]{:S(2)}) async-start(bf16[16,2,32,256]{3,2,1,0:T(8,128)(2,1)} %pack.3), calls=%async_computation.1 | async-start | bytes 1048576 | tf_op jit(solution)/shard_map/all_to_all | solution.py:308
  31.7 19.3 %collective-permute-start.4 = (bf16[16,2,32,256]{3,2,1,0:T(8,128)(2,1)S(1)}, bf16[16,2,32,256]{3,2,1,0:T(8,128)(2,1)S(1)}, u32[]{:S(2)}, u32[]{:S(2)}) collective-permute-start(bf16[16,2,32,256]{3,2,1,0:T(8,128)(2,1)S(1)} %all-to-all-done), channel_id=1, source_target_pairs={{0,1},{1,0},{2,3},{3,2},{4,5},{5,4},{6,7},{7,6},{8,9},{9,8},{10,11... | collective-permute-start | bytes 1572872 | tf_op jit(solution)/shard_map/ppermute | solution.py:290
  41.8 11.6 %copy-start.2 = (bf16[16,2,32,256]{3,2,1,0:T(8,128)(2,1)}, bf16[16,2,32,256]{3,2,1,0:T(8,128)(2,1)S(1)}, u32[]{:S(2)}) copy-start(bf16[16,2,32,256]{3,2,1,0:T(8,128)(2,1)S(1)} %all-to-all-done.1.qg) | copy-start | bytes 1572868
  46.4 7.0 %copy-start.7 = (bf16[16,2,32,256]{3,2,1,0:T(8,128)(2,1)}, bf16[16,2,32,256]{3,2,1,0:T(8,128)(2,1)S(1)}, u32[]{:S(2)}) copy-start(bf16[16,2,32,256]{3,2,1,0:T(8,128)(2,1)S(1)} %collective-permute-done.3) | copy-start | bytes 1572868
  46.4 7.0 %copy-start.8 = (bf16[16,2,32,256]{3,2,1,0:T(8,128)(2,1)}, bf16[16,2,32,256]{3,2,1,0:T(8,128)(2,1)S(1)}, u32[]{:S(2)}) copy-start(bf16[16,2,32,256]{3,2,1,0:T(8,128)(2,1)S(1)} %collective-permute-done.2) | copy-start | bytes 1572868
  49.9 3.6 %copy-start.9 = (bf16[16,2,32,256]{3,2,1,0:T(8,128)(2,1)}, bf16[16,2,32,256]{3,2,1,0:T(8,128)(2,1)S(1)}, u32[]{:S(2)}) copy-start(bf16[16,2,32,256]{3,2,1,0:T(8,128)(2,1)S(1)} %collective-permute-done.1) | copy-start | bytes 1572868
  49.9 2.0 %collective-permute-start.5 = (bf16[16,2,32,256]{3,2,1,0:T(8,128)(2,1)S(1)}, bf16[16,2,32,256]{3,2,1,0:T(8,128)(2,1)}, u32[]{:S(2)}, u32[]{:S(2)}) collective-permute-start(bf16[16,2,32,256]{3,2,1,0:T(8,128)(2,1)S(1)} %collective-permute-done.1), channel_id=1, source_target_pairs={{0,1},{1,0},{2,3},{3,2},{4,5},{5,4},{6,7},{7,6},{8,9},{9,8},{10,11... | collective-permute-start | bytes 1572872 | tf_op jit(solution)/shard_map/ppermute | solution.py:290
  49.9 2.8 %collective-permute-start.6 = (bf16[16,2,32,256]{3,2,1,0:T(8,128)(2,1)S(1)}, bf16[16,2,32,256]{3,2,1,0:T(8,128)(2,1)}, u32[]{:S(2)}, u32[]{:S(2)}) collective-permute-start(bf16[16,2,32,256]{3,2,1,0:T(8,128)(2,1)S(1)} %collective-permute-done.2), channel_id=1, source_target_pairs={{0,1},{1,0},{2,3},{3,2},{4,5},{5,4},{6,7},{7,6},{8,9},{9,8},{10,11... | collective-permute-start | bytes 1572872 | tf_op jit(solution)/shard_map/ppermute | solution.py:290
  50.4 3.0 %collective-permute-start.7 = (bf16[16,2,32,256]{3,2,1,0:T(8,128)(2,1)S(1)}, bf16[16,2,32,256]{3,2,1,0:T(8,128)(2,1)}, u32[]{:S(2)}, u32[]{:S(2)}) collective-permute-start(bf16[16,2,32,256]{3,2,1,0:T(8,128)(2,1)S(1)} %collective-permute-done.3), channel_id=1, source_target_pairs={{0,1},{1,0},{2,3},{3,2},{4,5},{5,4},{6,7},{7,6},{8,9},{9,8},{10,11... | collective-permute-start | bytes 1572872 | tf_op jit(solution)/shard_map/ppermute | solution.py:290
  51.1 2.4 %copy-start.10 = (bf16[16,2,32,256]{3,2,1,0:T(8,128)(2,1)}, bf16[16,2,32,256]{3,2,1,0:T(8,128)(2,1)S(1)}, u32[]{:S(2)}) copy-start(bf16[16,2,32,256]{3,2,1,0:T(8,128)(2,1)S(1)} %collective-permute-done.4) | copy-start | bytes 1572868
  69.4 2.4 %collective-permute-start.9 = (bf16[16,2,32,256]{3,2,1,0:T(8,128)(2,1)}, bf16[16,2,32,256]{3,2,1,0:T(8,128)(2,1)S(1)}, u32[]{:S(2)}, u32[]{:S(2)}) collective-permute-start(bf16[16,2,32,256]{3,2,1,0:T(8,128)(2,1)} %get-tuple-element.32), channel_id=1, source_target_pairs={{0,1},{1,0},{2,3},{3,2},{4,5},{5,4},{6,7},{7,6},{8,9},{9,8},{10,11... | collective-permute-start | bytes 1572872 | tf_op jit(solution)/shard_map/ppermute | solution.py:290
  69.8 4.3 %collective-permute-start.11 = (bf16[16,2,32,256]{3,2,1,0:T(8,128)(2,1)}, bf16[16,2,32,256]{3,2,1,0:T(8,128)(2,1)S(1)}, u32[]{:S(2)}, u32[]{:S(2)}) collective-permute-start(bf16[16,2,32,256]{3,2,1,0:T(8,128)(2,1)} %get-tuple-element.34), channel_id=1, source_target_pairs={{0,1},{1,0},{2,3},{3,2},{4,5},{5,4},{6,7},{7,6},{8,9},{9,8},{10,11... | collective-permute-start | bytes 1572872 | tf_op jit(solution)/shard_map/ppermute | solution.py:290
  70.2 11.0 %collective-permute-start.8 = (bf16[16,2,32,256]{3,2,1,0:T(8,128)(2,1)}, bf16[16,2,32,256]{3,2,1,0:T(8,128)(2,1)S(1)}, u32[]{:S(2)}, u32[]{:S(2)}) collective-permute-start(bf16[16,2,32,256]{3,2,1,0:T(8,128)(2,1)} %get-tuple-element.30), channel_id=1, source_target_pairs={{0,1},{1,0},{2,3},{3,2},{4,5},{5,4},{6,7},{7,6},{8,9},{9,8},{10,11... | collective-permute-start | bytes 1572872 | tf_op jit(solution)/shard_map/ppermute | solution.py:290
  70.3 4.3 %collective-permute-start.13 = (bf16[16,2,32,256]{3,2,1,0:T(8,128)(2,1)}, bf16[16,2,32,256]{3,2,1,0:T(8,128)(2,1)S(1)}, u32[]{:S(2)}, u32[]{:S(2)}) collective-permute-start(bf16[16,2,32,256]{3,2,1,0:T(8,128)(2,1)} %get-tuple-element.36), channel_id=1, source_target_pairs={{0,1},{1,0},{2,3},{3,2},{4,5},{5,4},{6,7},{7,6},{8,9},{9,8},{10,11... | collective-permute-start | bytes 1572872 | tf_op jit(solution)/shard_map/ppermute | solution.py:290
  71.8 2.3 %copy-start.5 = (bf16[16,2,32,256]{3,2,1,0:T(8,128)(2,1)S(1)}, bf16[16,2,32,256]{3,2,1,0:T(8,128)(2,1)}, u32[]{:S(2)}) copy-start(bf16[16,2,32,256]{3,2,1,0:T(8,128)(2,1)} %get-tuple-element.33) | copy-start | bytes 1572868
  73.1 14.8 %collective-permute-start.10 = (bf16[16,2,32,256]{3,2,1,0:T(8,128)(2,1)S(1)}, bf16[16,2,32,256]{3,2,1,0:T(8,128)(2,1)S(1)}, u32[]{:S(2)}, u32[]{:S(2)}) collective-permute-start(bf16[16,2,32,256]{3,2,1,0:T(8,128)(2,1)S(1)} %add_convert_fusion.3), channel_id=1, source_target_pairs={{0,6},{2,0},{4,2},{6,4},{1,7},{3,1},{5,3},{7,5},{8,14},{10,8},{12,... | collective-permute-start | bytes 1572872 | tf_op jit(solution)/shard_map/ppermute | solution.py:286
  74.1 1.0 copy-start.4
  74.3 16.5 %collective-permute-start.12 = (bf16[16,2,32,256]{3,2,1,0:T(8,128)(2,1)S(1)}, bf16[16,2,32,256]{3,2,1,0:T(8,128)(2,1)}, u32[]{:S(2)}, u32[]{:S(2)}) collective-permute-start(bf16[16,2,32,256]{3,2,1,0:T(8,128)(2,1)S(1)} %add_convert_fusion.2), channel_id=1, source_target_pairs={{0,4},{2,6},{4,0},{6,2},{1,5},{3,7},{5,1},{7,3},{8,12},{10,14},{12... | collective-permute-start | bytes 1572872 | tf_op jit(solution)/shard_map/ppermute | solution.py:286
  75.3 25.6 %copy-start.6 = (bf16[16,2,32,256]{3,2,1,0:T(8,128)(2,1)S(1)}, bf16[16,2,32,256]{3,2,1,0:T(8,128)(2,1)}, u32[]{:S(2)}) copy-start(bf16[16,2,32,256]{3,2,1,0:T(8,128)(2,1)} %get-tuple-element.29) | copy-start | bytes 1572868
  75.3 25.6 %collective-permute-start.14 = (bf16[16,2,32,256]{3,2,1,0:T(8,128)(2,1)S(1)}, bf16[16,2,32,256]{3,2,1,0:T(8,128)(2,1)}, u32[]{:S(2)}, u32[]{:S(2)}) collective-permute-start(bf16[16,2,32,256]{3,2,1,0:T(8,128)(2,1)S(1)} %add_convert_fusion.1), channel_id=1, source_target_pairs={{0,2},{2,4},{4,6},{6,0},{1,3},{3,5},{5,7},{7,1},{8,10},{10,12},{12... | collective-permute-start | bytes 1572872 | tf_op jit(solution)/shard_map/ppermute | solution.py:286
  76.5 26.8 %all-to-all-start.2 = ((bf16[16,32,256]{2,1,0:T(8,128)(2,1)}), bf16[16,32,256]{2,1,0:T(8,128)(2,1)S(1)}, u32[]{:S(2)}, u32[]{:S(2)}) async-start(bf16[16,32,256]{2,1,0:T(8,128)(2,1)} %get-tuple-element.28), calls=%async_computation.2 | async-start | bytes 524288 | tf_op jit(solution)/shard_map/all_to_all | solution.py:315
  103.3 0.7 copy-start.3
  104.0 16.3 %all-to-all-start.3 = ((bf16[16,2,32,256]{3,2,1,0:T(8,128)(2,1)}), bf16[16,2,32,256]{3,2,1,0:T(8,128)(2,1)S(1)}, u32[]{:S(2)}, u32[]{:S(2)}) async-start(bf16[16,2,32,256]{3,2,1,0:T(8,128)(2,1)} %add_convert_fusion), calls=%async_computation.3 | async-start | bytes 1048576 | tf_op jit(solution)/shard_map/all_to_all | solution.py:323
  120.4 0.8 copy-start

commit v3 on v2

--- a/solution.py
+++ b/solution.py
@@ -22,6 +22,7 @@
 CHUNK = PARTS * TILE
 ROWS = GROUPS * TILE
 PAIRS = PARTS // 2
+LIVE_PAIRS = 2
 SECTION = ("x", "y")
 ALL = ("x", "y", "z", "core")
 SCALE = HALF ** (-0.5)
@@ -44,36 +45,20 @@
     )(a, b)
 
 
-def unpack_pair_kernel(in_ref, a_ref, b_ref):
+def unpack_kernel(in_ref, *outs):
     for head in range(SLICES):
-        cols = slice(head * WIDTH, (head + 1) * WIDTH)
-        a_ref[:, cols] = in_ref[head, 0]
-        b_ref[:, cols] = in_ref[head, 1]
-
-
-def unpack_pair(x):
+        for i, out in enumerate(outs):
+            out[:, head * WIDTH : (head + 1) * WIDTH] = in_ref[head, i]
+
+
+def unpack(x):
     shape = jax.ShapeDtypeStruct((STRIPE, SLICES * WIDTH), x.dtype)
     return pl.pallas_call(
-        unpack_pair_kernel,
-        out_shape=(shape, shape),
+        unpack_kernel,
+        out_shape=(shape,) * 3,
         in_specs=[pl.BlockSpec(memory_space=pltpu.VMEM)],
-        out_specs=(pl.BlockSpec(memory_space=pltpu.VMEM),) * 2,
-        name="unpack_pair",
-    )(x)
-
-
-def unpack_one_kernel(in_ref, a_ref):
-    for head in range(SLICES):
-        a_ref[:, head * WIDTH : (head + 1) * WIDTH] = in_ref[head]
-
-
-def unpack_one(x):
-    return pl.pallas_call(
-        unpack_one_kernel,
-        out_shape=jax.ShapeDtypeStruct((STRIPE, SLICES * WIDTH), x.dtype),
-        in_specs=[pl.BlockSpec(memory_space=pltpu.VMEM)],
-        out_specs=pl.BlockSpec(memory_space=pltpu.VMEM),
-        name="unpack_one",
+        out_specs=(pl.BlockSpec(memory_space=pltpu.VMEM),) * 3,
+        name="unpack",
     )(x)
 
 
@@ -97,55 +82,62 @@
 
 
 def core_kernel(lengths, where, lams, qg, *refs):
-    kv_parts = refs[:PARTS]
-    dq_out, *term_outs = refs[PARTS : PARTS + 1 + PARTS]
-    ks, vs, p1s, p2s, das, mixs, t1s, t2s, outs, stat1, stat2, wide, key_pos, in_sems, out_sems = refs[
-        2 * PARTS + 1 :
+    kv_halves = refs[: 2 * PARTS]
+    dq_out, *term_outs = refs[2 * PARTS : 4 * PARTS + 1]
+    ks, vs, p1s, p2s, das, mixs, t1s, t2s, outs, stat1, stat2, wide, in_sems, out_sems = refs[
+        4 * PARTS + 1 :
     ]
 
     copies = []
     for kind, dst in ((0, ks), (1, vs)):
-        for u in range(PARTS):
-            copy = pltpu.make_async_copy(
-                kv_parts[u].at[:, :, kind], dst.at[:, u], in_sems.at[kind * PARTS + u]
-            )
-            copy.start()
-            copies.append(copy)
-
-    lane = lax.broadcasted_iota(jnp.int32, (1, TILE), 1)
-    for j in range(GROUPS):
-        length = jnp.full((1, TILE), lengths[4 * j], jnp.int32)
-        for nl in range(1, 4):
-            length = jnp.where(lane // STRIPE == nl, lengths[4 * j + nl], length)
-        for u in range(PARTS):
-            slot = where[u] * STRIPE + lane % STRIPE
-            pos = 256 * (4 * j + lane // STRIPE) + slot
-            key_pos[j, :, u * TILE : (u + 1) * TILE] = jnp.where(slot < length, pos, 1 << 30)
+        for half in range(2):
+            for u in range(PARTS):
+                copy = pltpu.make_async_copy(
+                    kv_halves[2 * u + half].at[:, :, kind],
+                    dst.at[2 * half : 2 * half + 2, where[u]],
+                    in_sems.at[(kind * 2 + half) * PARTS + u],
+                )
+                copy.start()
+                copies.append(copy)
+
+    lane = lax.broadcasted_iota(jnp.int32, (1, 2 * TILE), 1)
+    lane_slice = lane % TILE // STRIPE
 
     weight = lams[where[PARTS] % 2]
     row = lax.broadcasted_iota(jnp.int32, (ROWS, 1), 0)
     row_slot = where[0] * STRIPE + row % STRIPE
-    row_pos = 256 * (row // STRIPE) + row_slot
+    tile_pos = 256 * (row[:TILE] // STRIPE) + row_slot[:TILE]
     q = qg[:, 0].reshape(ROWS, WIDTH)
     q1, q2 = q[:, :HALF], q[:, HALF:]
     stat1[...] = jnp.full((ROWS, 128), NEGATIVE, jnp.float32)
     stat2[...] = jnp.full((ROWS, 128), NEGATIVE, jnp.float32)
 
-    for copy in copies[:PARTS]:
-        copy.wait()
-    for j in range(GROUPS):
-        lo = j * TILE
+    for j in range(GROUPS):
+        lo = j * TILE
+        if j % 2 == 0:
+            for copy in copies[j // 2 * PARTS : (j // 2 + 1) * PARTS]:
+                copy.wait()
 
         for pair in range(PAIRS):
             k = ks[j, slice(2 * pair, 2 * pair + 2)].reshape(2 * TILE, WIDTH)
             cols = slice(pair * 2 * TILE, (pair + 1) * 2 * TILE)
-            vis = key_pos[j, :, cols] <= row_pos[lo:]
-            s1 = jnp.where(vis, dot_nt(q1[lo:], k[:, :HALF]), NEGATIVE)
-            s2 = jnp.where(vis, dot_nt(q2[lo:], k[:, HALF:]), NEGATIVE)
-            p1s[j, lo:, cols] = s1
-            p2s[j, lo:, cols] = s2
-            stat1[lo:] = jnp.maximum(stat1[lo:], fold(jnp.maximum, s1))
-            stat2[lo:] = jnp.maximum(stat2[lo:], fold(jnp.maximum, s2))
+            slot = (2 * pair + lane // TILE) * STRIPE + lane % STRIPE
+            vis = 256 * lane_slice + slot <= tile_pos
+            if pair >= LIVE_PAIRS:
+                length = jnp.full((1, 2 * TILE), lengths[4 * j], jnp.int32)
+                for nl in range(1, 4):
+                    length = jnp.where(lane_slice == nl, lengths[4 * j + nl], length)
+                vis = vis & (slot < length)
+                hide = jnp.where(slot < length, 0.0, NEGATIVE)
+            for half, p, stat in ((0, p1s, stat1), (HALF, p2s, stat2)):
+                scores = dot_nt(q[lo:, half : half + HALF], k[:, half : half + HALF])
+                top, rest = jnp.where(vis, scores[:TILE], NEGATIVE), scores[TILE:]
+                p[j, lo : lo + TILE, cols] = top
+                stat[lo : lo + TILE] = jnp.maximum(stat[lo : lo + TILE], fold(jnp.maximum, top))
+                if j < GROUPS - 1:
+                    rest = rest + hide if pair >= LIVE_PAIRS else rest
+                    p[j, lo + TILE :, cols] = rest
+                    stat[lo + TILE :] = jnp.maximum(stat[lo + TILE :], fold(jnp.maximum, rest))
 
     m1 = jnp.max(stat1[...], axis=1, keepdims=True)
     m2 = jnp.max(stat2[...], axis=1, keepdims=True)
@@ -167,7 +159,7 @@
     inv2 = 1.0 / jnp.sum(stat2[...], axis=1, keepdims=True)
     winv2 = weight * inv2
 
-    for copy in copies[PARTS:]:
+    for copy in copies[2 * PARTS :]:
         copy.wait()
     wide[...] = jnp.zeros((ROWS, WIDTH), jnp.float32)
     for j in range(GROUPS):
@@ -233,7 +225,9 @@
 
         for u in range(PARTS):
             copy = pltpu.make_async_copy(
-                outs.at[j, u], term_outs[u].at[pl.ds(4 * j, 4)], out_sems.at[PARTS * j + u]
+                outs.at[j, where[u]],
+                term_outs[2 * u + j // 2].at[4 * (j % 2) : 4 * (j % 2) + 4],
+                out_sems.at[PARTS * j + u],
             )
             copy.start()
             out_copies.append(copy)
@@ -246,20 +240,20 @@
         copy.wait()
 
 
-def core(lengths, where, lams, qg, kv_parts):
+def core(lengths, where, lams, qg, kv_halves):
     vmem = pl.BlockSpec(memory_space=pltpu.VMEM)
     smem = pl.BlockSpec(memory_space=pltpu.SMEM)
     hbm = pl.BlockSpec(memory_space=pl.ANY)
     b16, f32 = jnp.bfloat16, jnp.float32
-    parts = [x.reshape(GROUPS, 4, 2, STRIPE, WIDTH) for x in kv_parts]
+    halves = [x.reshape(2, 4, 2, STRIPE, WIDTH) for x in kv_halves]
     return pl.pallas_call(
         core_kernel,
         out_shape=(
             jax.ShapeDtypeStruct((SLICES, STRIPE, WIDTH), b16),
         )
-        + (jax.ShapeDtypeStruct((SLICES, 2, STRIPE, WIDTH), b16),) * PARTS,
-        in_specs=[smem, smem, smem, vmem] + [hbm] * PARTS,
-        out_specs=(vmem,) + (hbm,) * PARTS,
+        + (jax.ShapeDtypeStruct((SLICES // 2, 2, STRIPE, WIDTH), b16),) * (2 * PARTS),
+        in_specs=[smem, smem, smem, vmem] + [hbm] * (2 * PARTS),
+        out_specs=(vmem,) + (hbm,) * (2 * PARTS),
         scratch_shapes=[
             pltpu.VMEM((GROUPS, PARTS, 4, STRIPE, WIDTH), b16),
             pltpu.VMEM((GROUPS, PARTS, 4, STRIPE, WIDTH), b16),
@@ -273,13 +267,32 @@
             pltpu.VMEM((ROWS, 128), f32),
             pltpu.VMEM((ROWS, 128), f32),
             pltpu.VMEM((ROWS, WIDTH), f32),
-            pltpu.VMEM((GROUPS, 1, CHUNK), jnp.int32),
-            pltpu.SemaphoreType.DMA((PARTS * 2,)),
+            pltpu.SemaphoreType.DMA((PARTS * 4,)),
             pltpu.SemaphoreType.DMA((GROUPS * PARTS,)),
         ],
         compiler_params=pltpu.CompilerParams(vmem_limit_bytes=60 * 1024 * 1024),
         name="attention",
-    )(lengths, where, lams, qg, *parts)
+    )(lengths, where, lams, qg, *halves)
+
+
+def final_kernel(*refs):
+    d_query, *ins, out = refs
+    out[:, 0] = d_query[...]
+    for half in range(2):
+        total = ins[half][...].astype(jnp.float32)
+        for x in ins[2 + half :: 2]:
+            total = total + x[...].astype(jnp.float32)
+        out[8 * half : 8 * half + 8, 1:] = total.astype(out.dtype)
+
+
+def final(d_query, *halves):
+    return pl.pallas_call(
+        final_kernel,
+        out_shape=jax.ShapeDtypeStruct((SLICES, 3, STRIPE, WIDTH), jnp.bfloat16),
+        in_specs=[pl.BlockSpec(memory_space=pltpu.VMEM)] * (1 + len(halves)),
+        out_specs=pl.BlockSpec(memory_space=pltpu.VMEM),
+        name="final",
+    )(d_query, *halves)
 
 
 def along_z(x, d):
@@ -304,25 +317,28 @@
         lam, ALL, [(s * 8 + t, (2 * t + s // 8) * 8 + s % 8) for s in range(SLICES) for t in range(PARTS)]
     )
     kv, qg, lams = lax.optimization_barrier((kv, pack(queries, out_grad), lams))
-    near = [along_z(kv, d) for d in (1, 2, 3)]
+    lower, upper = lax.optimization_barrier((kv[:8], kv[8:]))
+    lower_up, upper_down = along_z(lower, 1), along_z(upper, -1)
+    upper_up, lower_down = along_z(upper, 1), along_z(lower, -1)
+    lower_far, upper_far = along_z(lower_up, 1), along_z(upper_down, -1)
     qg = lax.all_to_all(qg, SECTION, 0, 0, tiled=True)
-    *near, qg = lax.optimization_barrier((*near, qg))
-    near = [kv] + near
+    upper_up, lower_down, qg = lax.optimization_barrier((upper_up, lower_down, qg))
+    near = [lower, upper, lower_up, upper_up, lower_far, upper_far, lower_down, upper_down]
 
     d_query, *terms = core(lengths, where, lams, qg, near + [swap(x) for x in near])
 
-    f32, b16 = jnp.float32, jnp.bfloat16
-    dq = lax.all_to_all(d_query, SECTION, 0, 0, tiled=True)
-    merged = [
-        (own.astype(f32) + swap(other).astype(f32)).astype(b16)
-        for own, other in zip(terms[:4], terms[4:])
-    ]
-    total = merged[0].astype(f32)
-    for d in (1, 2, 3):
-        total = total + along_z(merged[d], -d).astype(f32)
-    dkv = lax.all_to_all(total.astype(b16), SECTION, 0, 0, tiled=True)
-    dk, dv = unpack_pair(dkv)
-    return (unpack_one(dq), dk, dv)
+    def add(*xs):
+        return sum(x.astype(jnp.float32) for x in xs).astype(jnp.bfloat16)
+
+    own, other = terms[:PARTS], [swap(x) for x in terms[PARTS:]]
+    lower_far = along_z(add(own[4], other[4]), -1)
+    upper_far = along_z(add(own[5], other[5]), 1)
+    upper_1 = along_z(add(own[3], other[3]), -1)
+    lower_3 = along_z(add(own[6], other[6]), 1)
+    lower_1 = along_z(add(own[2], other[2], lower_far), -1)
+    upper_3 = along_z(add(own[7], other[7], upper_far), 1)
+    total = final(d_query, own[0], own[1], other[0], other[1], lower_3, upper_1, lower_1, upper_3)
+    return unpack(lax.all_to_all(total, SECTION, 0, 0, tiled=True))
 
 
 def solution(mesh):

time: 124 us -> 115 us (0.927)
  waiting for transfers between devices: 60.1 us -> 33.4 us
  blocking collectives: 0 us -> 18.7 us
  other arithmetic: 4.12 us -> 1.59 us
    all_to_all x0 -> x1, blocking collectives: none -> 18.7 us  [shards(): return unpack(lax.all_to_all(total, SECTION, 0, 0, tiled=True))]
    all_to_all x2 -> x0, waiting for transfers between devices: 10 us -> none  [the longest x1 10 us: shards(): dkv = lax.all_to_all(total.astype(b16), SECTION, 0, 0, tiled=True)]
    all_to_all x2 -> x0, starting transfers between devices: 9.32 us -> none  [the longest x1 4.67 us: shards(): dq = lax.all_to_all(d_query, SECTION, 0, 0, tiled=True)]
    ppermute x6 -> x12, starting transfers between devices: 7.8 us -> 16.4 us  [along_z(): return lax.ppermute(x, 'z', [(i, (i + d) % 4) for i in range(4)])]
    ppermute x6 -> x12, waiting for transfers between devices: 27.7 us -> 19.6 us  [along_z(): return lax.ppermute(x, 'z', [(i, (i + d) % 4) for i in range(4)])]
    all_to_all x1, waiting for transfers between devices: 10 us -> 3.27 us  [shards(): qg = lax.all_to_all(qg, SECTION, 0, 0, tiled=True)]
    convert_element_type x4 -> x6, other arithmetic: 4.12 us -> 1.59 us  [add(): return sum((x.astype(jnp.float32) for x in xs)).astype(jnp.bfloat16)]
    ppermute x8 -> x16, waiting for transfers between devices: 3.45 us -> 1.59 us  [swap(): return lax.ppermute(x, 'core', [(0, 1), (1, 0)])]
  transfers between devices with their start and end apart: 19 -> 31, of which waited for: 12 -> 13; matrix products, arithmetic and copies ran while one was open for 4% -> 2% of each run, Pallas kernels for 3% -> 2%
where the time goes in v3:
time: 115 us; the launch traced here: 114 us
  waiting for transfers between devices  33.4 us (29%)
  starting transfers between devices  32.8 us (29%)
  Pallas kernels  23.9 us (21%)
  blocking collectives  18.7 us (16%)
  local copies, waits for them, and re-layouts  2.86 us (2%)
  other arithmetic  1.59 us (1%)
    ppermute x12, waiting for transfers between devices, along_z(): return lax.ppermute(x, 'z', [(i, (i + d) % 4) for i in range(4)])  19.6 us
    all_to_all x1, blocking collectives, shards(): return unpack(lax.all_to_all(total, SECTION, 0, 0, tiled=True))  18.7 us
    ppermute x12, starting transfers between devices, along_z(): return lax.ppermute(x, 'z', [(i, (i + d) % 4) for i in range(4)])  16.4 us
    pallas_call x1, Pallas kernels, core(): pl.pallas_call(core_kernel, out_shape=(jax.ShapeDtypeStruct((SLICES, STRI...  15.4 us
    all_to_all x1, waiting for transfers between devices, shards(): kv = lax.all_to_all(pack(keys, values), SECTION, 0, 0, tiled=True)  8.93 us
    all_to_all x1, starting transfers between devices, shards(): kv = lax.all_to_all(pack(keys, values), SECTION, 0, 0, tiled=True)  7.25 us
    all_to_all x1, starting transfers between devices, shards(): qg = lax.all_to_all(qg, SECTION, 0, 0, tiled=True)  5.28 us
    pallas_call x2, Pallas kernels, pack(): pl.pallas_call(pack_kernel, out_shape=jax.ShapeDtypeStruct((SLICES, 2, ST...  3.76 us
  transfers between devices with their start and end apart: 31, of which 13 were waited for; matrix products, arithmetic and copies ran while one was open for 2% of the time, Pallas kernels for 2%

profile of v3, /device:TPU:0, one launch (start us, length us, event | category | flops | bytes accessed | tf_op | source)
XLA Modules:
  0.0 114.3 jit_solution(9713593771033214938)
XLA Ops:
  0.6 1.9 %pack.2 = bf16[16,2,32,256]{3,2,1,0:T(8,128)(2,1)} custom-call(bf16[32,4096]{1,0:T(8,128)(2,1)} %a_ref.2, bf16[32,4096]{1,0:T(8,128)(2,1)} %b_ref.2), custom_call_target="tpu_custom_call" | custom-call | tf_op jit(solution)/shard_map/pack/pallas_call | solution.py:39
  2.5 7.2 %all-to-all-start = ((bf16[16,2,32,256]{3,2,1,0:T(8,128)(2,1)}), bf16[16,2,32,256]{3,2,1,0:T(8,128)(2,1)S(1)}, u32[]{:S(2)}, u32[]{:S(2)}) async-start(bf16[16,2,32,256]{3,2,1,0:T(8,128)(2,1)} %pack.2), calls=%async_computation | async-start | bytes 1048576 | tf_op jit(solution)/shard_map/all_to_all | solution.py:315
  9.8 0.7 collective-permute-start
  10.4 1.9 %pack.3 = bf16[16,2,32,256]{3,2,1,0:T(8,128)(2,1)} custom-call(bf16[32,4096]{1,0:T(8,128)(2,1)} %a_ref.3, bf16[32,4096]{1,0:T(8,128)(2,1)} %b_ref.3), custom_call_target="tpu_custom_call" | custom-call | tf_op jit(solution)/shard_map/pack/pallas_call | solution.py:39
  12.3 8.9 %all-to-all-done = bf16[16,2,32,256]{3,2,1,0:T(8,128)(2,1)S(1)} async-done(((bf16[16,2,32,256]{3,2,1,0:T(8,128)(2,1)}), bf16[16,2,32,256]{3,2,1,0:T(8,128)(2,1)S(1)}, u32[]{:S(2)}, u32[]{:S(2)}) %all-to-all-start) | async-done | bytes 524320 | tf_op jit(solution)/shard_map/all_to_all | solution.py:315
  21.3 0.0 copy-start.1
  21.3 0.0 copy-start.2
  21.3 4.1 %collective-permute-start.5 = (bf16[8,2,32,256]{3,2,1,0:T(8,128)(2,1)S(1)}, bf16[8,2,32,256]{3,2,1,0:T(8,128)(2,1)S(1)}, u32[]{:S(2)}, u32[]{:S(2)}) collective-permute-start(bf16[8,2,32,256]{3,2,1,0:T(8,128)(2,1)S(1)} %get-tuple-element.30), channel_id=1, source_target_pairs={{0,6},{2,0},{4,2},{6,4},{1,7},{3,1},{5,3},{7,5},{8,14},{10,8},{12,... | collective-permute-start | bytes 786440 | tf_op jit(solution)/shard_map/ppermute | solution.py:299
  25.4 0.0 collective-permute-start.1
  25.4 3.3 %collective-permute-start.2 = (bf16[8,2,32,256]{3,2,1,0:T(8,128)(2,1)S(1)}, bf16[8,2,32,256]{3,2,1,0:T(8,128)(2,1)S(1)}, u32[]{:S(2)}, u32[]{:S(2)}) collective-permute-start(bf16[8,2,32,256]{3,2,1,0:T(8,128)(2,1)S(1)} %get-tuple-element.31), channel_id=1, source_target_pairs={{0,6},{2,0},{4,2},{6,4},{1,7},{3,1},{5,3},{7,5},{8,14},{10,8},{12,... | collective-permute-start | bytes 786440 | tf_op jit(solution)/shard_map/ppermute | solution.py:299
  28.7 5.3 %all-to-all-start.1 = ((bf16[16,2,32,256]{3,2,1,0:T(8,128)(2,1)}), bf16[16,2,32,256]{3,2,1,0:T(8,128)(2,1)S(1)}, u32[]{:S(2)}, u32[]{:S(2)}) async-start(bf16[16,2,32,256]{3,2,1,0:T(8,128)(2,1)} %pack.3), calls=%async_computation.1 | async-start | bytes 1048576 | tf_op jit(solution)/shard_map/all_to_all | solution.py:324
  34.0 0.1 collective-permute-start.8
  34.1 0.0 collective-permute-done.5
  34.1 0.5 collective-permute-start.7
  34.7 1.2 %collective-permute-done.1 = bf16[8,2,32,256]{3,2,1,0:T(8,128)(2,1)S(1)} collective-permute-done((bf16[8,2,32,256]{3,2,1,0:T(8,128)(2,1)S(1)}, bf16[8,2,32,256]{3,2,1,0:T(8,128)(2,1)S(1)}, u32[]{:S(2)}, u32[]{:S(2)}) %collective-permute-start.1) | collective-permute-done | bytes 262176 | tf_op jit(solution)/shard_map/ppermute | solution.py:299
  35.9 0.0 collective-permute-start.14
  35.9 2.9 %collective-permute-done.3 = bf16[8,2,32,256]{3,2,1,0:T(8,128)(2,1)S(1)} collective-permute-done((bf16[8,2,32,256]{3,2,1,0:T(8,128)(2,1)S(1)}, bf16[8,2,32,256]{3,2,1,0:T(8,128)(2,1)S(1)}, u32[]{:S(2)}, u32[]{:S(2)}) %collective-permute-start.3) | collective-permute-done | bytes 262176 | tf_op jit(solution)/shard_map/ppermute | solution.py:299
  38.8 0.0 collective-permute-start.6
  38.8 0.0 collective-permute-done.2
  38.8 2.0 %collective-permute-start.4 = (bf16[8,2,32,256]{3,2,1,0:T(8,128)(2,1)S(1)}, bf16[8,2,32,256]{3,2,1,0:T(8,128)(2,1)S(1)}, u32[]{:S(2)}, u32[]{:S(2)}) collective-permute-start(bf16[8,2,32,256]{3,2,1,0:T(8,128)(2,1)S(1)} %collective-permute-done.3), channel_id=1, source_target_pairs={{0,2},{2,4},{4,6},{6,0},{1,3},{3,5},{5,7},{7,1},{8,10},{10,12},{12... | collective-permute-start | bytes 786440 | tf_op jit(solution)/shard_map/ppermute | solution.py:299
  40.8 3.3 %all-to-all-done.1.qg = bf16[16,2,32,256]{3,2,1,0:T(8,128)(2,1)S(1)} async-done(((bf16[16,2,32,256]{3,2,1,0:T(8,128)(2,1)}), bf16[16,2,32,256]{3,2,1,0:T(8,128)(2,1)S(1)}, u32[]{:S(2)}, u32[]{:S(2)}) %all-to-all-start.1) | async-done | bytes 524320 | tf_op jit(solution)/shard_map/all_to_all | solution.py:324
  44.1 0.1 collective-permute-start.9
  44.2 0.5 collective-permute-start.10
  44.7 0.1 collective-permute-start.13
  44.8 0.4 collective-permute-done.6
  45.2 0.1 collective-permute-start.12
  45.2 1.2 %collective-permute-done.4 = bf16[8,2,32,256]{3,2,1,0:T(8,128)(2,1)S(1)} collective-permute-done((bf16[8,2,32,256]{3,2,1,0:T(8,128)(2,1)S(1)}, bf16[8,2,32,256]{3,2,1,0:T(8,128)(2,1)S(1)}, u32[]{:S(2)}, u32[]{:S(2)}) %collective-permute-start.4) | collective-permute-done | bytes 262176 | tf_op jit(solution)/shard_map/ppermute | solution.py:299
  46.5 0.0 collective-permute-start.11
  46.5 0.7 stack.39.where
  47.2 0.9 collective-permute-done.11
  48.2 15.4 %attention.1 = (bf16[16,32,256]{2,1,0:T(8,128)(2,1)}, bf16[8,2,32,256]{3,2,1,0:T(8,128)(2,1)}, bf16[8,2,32,256]{3,2,1,0:T(8,128)(2,1)}, bf16[8,2,32,256]{3,2,1,0...) custom-call(s32[16]{0:T(128)} %lengths.1, ...), custom_call_target="tpu_custom_call" | custom-call | tf_op jit(solution)/shard_map/attention/pallas_call | solution.py:249
  63.6 0.2 collective-permute-start.17
  63.8 0.3 collective-permute-start.22
  64.2 0.2 collective-permute-start.15
  64.4 0.3 collective-permute-start.19
  64.7 0.2 collective-permute-start.21
  64.9 0.6 collective-permute-done.17
  65.4 0.2 collective-permute-start.26
  65.6 1.1 add_convert_fusion.5
  66.7 0.4 collective-permute-start.25
  67.1 0.1 add_convert_fusion.3
  67.2 0.1 collective-permute-done.26
  67.3 0.3 collective-permute-start.23
  67.6 0.5 copy-done.16
  68.1 0.1 add_convert_fusion.1
  68.2 1.3 %collective-permute-start.27 = (bf16[8,2,32,256]{3,2,1,0:T(8,128)(2,1)S(1)}, bf16[8,2,32,256]{3,2,1,0:T(8,128)(2,1)S(1)}, u32[]{:S(2)}, u32[]{:S(2)}) collective-permute-start(bf16[8,2,32,256]{3,2,1,0:T(8,128)(2,1)S(1)} %add_convert_fusion.1), channel_id=1, source_target_pairs={{0,2},{2,4},{4,6},{6,0},{1,3},{3,5},{5,7},{7,1},{8,10},{10,12},{12... | collective-permute-start | bytes 786440 | tf_op jit(solution)/shard_map/ppermute | solution.py:299
  69.5 0.1 add_convert_fusion.4
  69.6 0.8 copy-done.26
  70.5 5.2 %collective-permute-done.23 = bf16[8,2,32,256]{3,2,1,0:T(8,128)(2,1)S(1)} collective-permute-done((bf16[8,2,32,256]{3,2,1,0:T(8,128)(2,1)S(1)}, bf16[8,2,32,256]{3,2,1,0:T(8,128)(2,1)S(1)}, u32[]{:S(2)}, u32[]{:S(2)}) %collective-permute-start.23) | collective-permute-done | bytes 262176 | tf_op jit(solution)/shard_map/ppermute | solution.py:299
  75.7 0.7 collective-permute-start.18
  76.4 0.1 add_convert_fusion.2
  76.6 2.6 %collective-permute-start.20 = (bf16[8,2,32,256]{3,2,1,0:T(8,128)(2,1)S(1)}, bf16[8,2,32,256]{3,2,1,0:T(8,128)(2,1)S(1)}, u32[]{:S(2)}, u32[]{:S(2)}) collective-permute-start(bf16[8,2,32,256]{3,2,1,0:T(8,128)(2,1)S(1)} %add_convert_fusion.4), channel_id=1, source_target_pairs={{0,6},{2,0},{4,2},{6,4},{1,7},{3,1},{5,3},{7,5},{8,14},{10,8},{12,... | collective-permute-start | bytes 786440 | tf_op jit(solution)/shard_map/ppermute | solution.py:299
  79.1 0.3 collective-permute-start.24
  79.4 0.1 add_convert_fusion
  79.6 0.0 copy-start.14
  79.6 1.8 %collective-permute-start.28 = (bf16[8,2,32,256]{3,2,1,0:T(8,128)(2,1)S(1)}, bf16[8,2,32,256]{3,2,1,0:T(8,128)(2,1)S(1)}, u32[]{:S(2)}, u32[]{:S(2)}) collective-permute-start(bf16[8,2,32,256]{3,2,1,0:T(8,128)(2,1)S(1)} %add_convert_fusion), channel_id=1, source_target_pairs={{0,2},{2,4},{4,6},{6,0},{1,3},{3,5},{5,7},{7,1},{8,10},{10,12},{12... | collective-permute-start | bytes 786440 | tf_op jit(solution)/shard_map/ppermute | solution.py:299
  81.4 4.7 %collective-permute-done.18.refs_5_ = bf16[8,2,32,256]{3,2,1,0:T(8,128)(2,1)S(1)} collective-permute-done((bf16[8,2,32,256]{3,2,1,0:T(8,128)(2,1)S(1)}, bf16[8,2,32,256]{3,2,1,0:T(8,128)(2,1)S(1)}, u32[]{:S(2)}, u32[]{:S(2)}) %collective-permute-start.18) | collective-permute-done | bytes 262176 | tf_op jit(solution)/shard_map/ppermute | solution.py:299
  86.1 3.4 %collective-permute-done.24.refs_7_ = bf16[8,2,32,256]{3,2,1,0:T(8,128)(2,1)S(1)} collective-permute-done((bf16[8,2,32,256]{3,2,1,0:T(8,128)(2,1)S(1)}, bf16[8,2,32,256]{3,2,1,0:T(8,128)(2,1)S(1)}, u32[]{:S(2)}, u32[]{:S(2)}) %collective-permute-start.24) | collective-permute-done | bytes 262176 | tf_op jit(solution)/shard_map/ppermute | solution.py:299
  89.5 0.5 collective-permute-done.28.refs_8_
  90.1 0.2 copy-done.21
  90.3 0.5 copy-done.22
  90.8 2.8 %final.1 = bf16[16,3,32,256]{3,2,1,0:T(8,128)(2,1)} custom-call(bf16[16,32,256]{2,1,0:T(8,128)(2,1)} %get-tuple-element.36.refs_0_, bf16[8,2,32,256]{3,2,1,0:T(8,128)(2,1)} %get-tuple-element.37.refs_1_, bf16[8,2,32,256]{3,2,1,0:T(8,128)(2,1)} %get-tuple-element.38.refs_2_, bf16[8,2,32,256]{3,2,1,0:T(8,128)(2,1)} %copy-done.14, ...), custom_call_target="tpu_custom_call" | custom-call | tf_op jit(solution)/shard_map/final/pallas_call | solution.py:289
  93.5 18.7 %all_to_all.15.in_ref = bf16[16,3,32,256]{3,2,1,0:T(8,128)(2,1)} all-to-all(bf16[16,3,32,256]{3,2,1,0:T(8,128)(2,1)} %final.1), channel_id=1, replica_groups=mesh['x'=4,'y'=4,'z'=4,'core'=2] {'x','y'}, dimensions={0} | all-to-all | bytes 1572864 | tf_op jit(solution)/shard_map/all_to_all | solution.py:341
  112.3 2.0 %unpack.1 = (bf16[32,4096]{1,0:T(8,128)(2,1)}, bf16[32,4096]{1,0:T(8,128)(2,1)}, bf16[32,4096]{1,0:T(8,128)(2,1)}) custom-call(bf16[16,3,32,256]{3,2,1,0:T(8,128)(2,1)} %all_to_all.15.in_ref), custom_call_target="tpu_custom_call" | custom-call | tf_op jit(solution)/shard_map/unpack/pallas_call | solution.py:56
  (70 shorter events, 0.2 us)
Async XLA Ops:
  2.5 7.3 %copy-start.28 = (f32[2]{0:T(128)S(1)}, f32[2]{0:T(128)}, u32[]{:S(2)}) copy-start(f32[2]{0:T(128)} %param.10) | copy-start | bytes 28
  2.5 18.8 %all-to-all-start = ((bf16[16,2,32,256]{3,2,1,0:T(8,128)(2,1)}), bf16[16,2,32,256]{3,2,1,0:T(8,128)(2,1)S(1)}, u32[]{:S(2)}, u32[]{:S(2)}) async-start(bf16[16,2,32,256]{3,2,1,0:T(8,128)(2,1)} %pack.2), calls=%async_computation | async-start | bytes 1048576 | tf_op jit(solution)/shard_map/all_to_all | solution.py:315
  9.8 2.6 %collective-permute-start = (f32[2]{0:T(128)S(1)}, f32[2]{0:T(128)S(1)}, u32[]{:S(2)}, u32[]{:S(2)}) collective-permute-start(f32[2]{0:T(128)S(1)} %copy-done.28), channel_id=1, source_target_pairs={{0,0},{1,16},{2,32},{3,48},{4,64},{5,80},{6,96},{7,112},{8,1},{9,1... | collective-permute-start | bytes 32 | tf_op jit(solution)/shard_map/ppermute | solution.py:316
  12.3 9.0 %copy-start.25 = (f32[2]{0:T(128)}, f32[2]{0:T(128)S(1)}, u32[]{:S(2)}) copy-start(f32[2]{0:T(128)S(1)} %collective-permute-done.lams) | copy-start | bytes 28
  21.3 12.7 %copy-start.1 = (bf16[8,2,32,256]{3,2,1,0:T(8,128)(2,1)}, bf16[8,2,32,256]{3,2,1,0:T(8,128)(2,1)S(1)}, u32[]{:S(2)}) copy-start(bf16[8,2,32,256]{3,2,1,0:T(8,128)(2,1)S(1)} %get-tuple-element.30) | copy-start | bytes 786436
  21.3 12.8 %copy-start.2 = (bf16[8,2,32,256]{3,2,1,0:T(8,128)(2,1)}, bf16[8,2,32,256]{3,2,1,0:T(8,128)(2,1)S(1)}, u32[]{:S(2)}) copy-start(bf16[8,2,32,256]{3,2,1,0:T(8,128)(2,1)S(1)} %get-tuple-element.31) | copy-start | bytes 786436
  21.3 12.8 %collective-permute-start.5 = (bf16[8,2,32,256]{3,2,1,0:T(8,128)(2,1)S(1)}, bf16[8,2,32,256]{3,2,1,0:T(8,128)(2,1)S(1)}, u32[]{:S(2)}, u32[]{:S(2)}) collective-permute-start(bf16[8,2,32,256]{3,2,1,0:T(8,128)(2,1)S(1)} %get-tuple-element.30), channel_id=1, source_target_pairs={{0,6},{2,0},{4,2},{6,4},{1,7},{3,1},{5,3},{7,5},{8,14},{10,8},{12,... | collective-permute-start | bytes 786440 | tf_op jit(solution)/shard_map/ppermute | solution.py:299
  25.4 10.5 %collective-permute-start.1 = (bf16[8,2,32,256]{3,2,1,0:T(8,128)(2,1)S(1)}, bf16[8,2,32,256]{3,2,1,0:T(8,128)(2,1)S(1)}, u32[]{:S(2)}, u32[]{:S(2)}) collective-permute-start(bf16[8,2,32,256]{3,2,1,0:T(8,128)(2,1)S(1)} %get-tuple-element.30), channel_id=1, source_target_pairs={{0,2},{2,4},{4,6},{6,0},{1,3},{3,5},{5,7},{7,1},{8,10},{10,12},{12... | collective-permute-start | bytes 786440 | tf_op jit(solution)/shard_map/ppermute | solution.py:299
  25.4 13.3 %collective-permute-start.3 = (bf16[8,2,32,256]{3,2,1,0:T(8,128)(2,1)S(1)}, bf16[8,2,32,256]{3,2,1,0:T(8,128)(2,1)S(1)}, u32[]{:S(2)}, u32[]{:S(2)}) collective-permute-start(bf16[8,2,32,256]{3,2,1,0:T(8,128)(2,1)S(1)} %get-tuple-element.31), channel_id=1, source_target_pairs={{0,2},{2,4},{4,6},{6,0},{1,3},{3,5},{5,7},{7,1},{8,10},{10,12},{12... | collective-permute-start | bytes 786440 | tf_op jit(solution)/shard_map/ppermute | solution.py:299
  25.4 13.3 %collective-permute-start.2 = (bf16[8,2,32,256]{3,2,1,0:T(8,128)(2,1)S(1)}, bf16[8,2,32,256]{3,2,1,0:T(8,128)(2,1)S(1)}, u32[]{:S(2)}, u32[]{:S(2)}) collective-permute-start(bf16[8,2,32,256]{3,2,1,0:T(8,128)(2,1)S(1)} %get-tuple-element.31), channel_id=1, source_target_pairs={{0,6},{2,0},{4,2},{6,4},{1,7},{3,1},{5,3},{7,5},{8,14},{10,8},{12,... | collective-permute-start | bytes 786440 | tf_op jit(solution)/shard_map/ppermute | solution.py:299
  28.7 15.4 %all-to-all-start.1 = ((bf16[16,2,32,256]{3,2,1,0:T(8,128)(2,1)}), bf16[16,2,32,256]{3,2,1,0:T(8,128)(2,1)S(1)}, u32[]{:S(2)}, u32[]{:S(2)}) async-start(bf16[16,2,32,256]{3,2,1,0:T(8,128)(2,1)} %pack.3), calls=%async_computation.1 | async-start | bytes 1048576 | tf_op jit(solution)/shard_map/all_to_all | solution.py:324
  34.0 10.1 %collective-permute-start.8 = (bf16[8,2,32,256]{3,2,1,0:T(8,128)(2,1)S(1)}, bf16[8,2,32,256]{3,2,1,0:T(8,128)(2,1)S(1)}, u32[]{:S(2)}, u32[]{:S(2)}) collective-permute-start(bf16[8,2,32,256]{3,2,1,0:T(8,128)(2,1)S(1)} %get-tuple-element.30), channel_id=1, source_target_pairs={{0,1},{1,0},{2,3},{3,2},{4,5},{5,4},{6,7},{7,6},{8,9},{9,8},{10,11... | collective-permute-start | bytes 786440 | tf_op jit(solution)/shard_map/ppermute | solution.py:303
  34.1 14.0 %copy-start.3 = (bf16[8,2,32,256]{3,2,1,0:T(8,128)(2,1)}, bf16[8,2,32,256]{3,2,1,0:T(8,128)(2,1)S(1)}, u32[]{:S(2)}) copy-start(bf16[8,2,32,256]{3,2,1,0:T(8,128)(2,1)S(1)} %collective-permute-done.5) | copy-start | bytes 786436
  34.1 10.1 %collective-permute-start.7 = (bf16[8,2,32,256]{3,2,1,0:T(8,128)(2,1)S(1)}, bf16[8,2,32,256]{3,2,1,0:T(8,128)(2,1)S(1)}, u32[]{:S(2)}, u32[]{:S(2)}) collective-permute-start(bf16[8,2,32,256]{3,2,1,0:T(8,128)(2,1)S(1)} %get-tuple-element.31), channel_id=1, source_target_pairs={{0,1},{1,0},{2,3},{3,2},{4,5},{5,4},{6,7},{7,6},{8,9},{9,8},{10,11... | collective-permute-start | bytes 786440 | tf_op jit(solution)/shard_map/ppermute | solution.py:303
  35.9 12.2 %copy-start.4 = (bf16[8,2,32,256]{3,2,1,0:T(8,128)(2,1)}, bf16[8,2,32,256]{3,2,1,0:T(8,128)(2,1)S(1)}, u32[]{:S(2)}) copy-start(bf16[8,2,32,256]{3,2,1,0:T(8,128)(2,1)S(1)} %collective-permute-done.1) | copy-start | bytes 786436
  35.9 8.8 %collective-permute-start.14 = (bf16[8,2,32,256]{3,2,1,0:T(8,128)(2,1)S(1)}, bf16[8,2,32,256]{3,2,1,0:T(8,128)(2,1)S(1)}, u32[]{:S(2)}, u32[]{:S(2)}) collective-permute-start(bf16[8,2,32,256]{3,2,1,0:T(8,128)(2,1)S(1)} %collective-permute-done.5), channel_id=1, source_target_pairs={{0,1},{1,0},{2,3},{3,2},{4,5},{5,4},{6,7},{7,6},{8,9},{9,8},{10,11... | collective-permute-start | bytes 786440 | tf_op jit(solution)/shard_map/ppermute | solution.py:303
  38.8 9.4 %copy-start.5 = (bf16[8,2,32,256]{3,2,1,0:T(8,128)(2,1)}, bf16[8,2,32,256]{3,2,1,0:T(8,128)(2,1)S(1)}, u32[]{:S(2)}) copy-start(bf16[8,2,32,256]{3,2,1,0:T(8,128)(2,1)S(1)} %collective-permute-done.3) | copy-start | bytes 786436
  38.8 6.4 %collective-permute-start.6 = (bf16[8,2,32,256]{3,2,1,0:T(8,128)(2,1)S(1)}, bf16[8,2,32,256]{3,2,1,0:T(8,128)(2,1)S(1)}, u32[]{:S(2)}, u32[]{:S(2)}) collective-permute-start(bf16[8,2,32,256]{3,2,1,0:T(8,128)(2,1)S(1)} %collective-permute-done.5), channel_id=1, source_target_pairs={{0,6},{2,0},{4,2},{6,4},{1,7},{3,1},{5,3},{7,5},{8,14},{10,8},{12,... | collective-permute-start | bytes 786440 | tf_op jit(solution)/shard_map/ppermute | solution.py:299
  38.8 9.3 %copy-start.6 = (bf16[8,2,32,256]{3,2,1,0:T(8,128)(2,1)}, bf16[8,2,32,256]{3,2,1,0:T(8,128)(2,1)S(1)}, u32[]{:S(2)}) copy-start(bf16[8,2,32,256]{3,2,1,0:T(8,128)(2,1)S(1)} %collective-permute-done.2) | copy-start | bytes 786436
  38.8 7.7 %collective-permute-start.4 = (bf16[8,2,32,256]{3,2,1,0:T(8,128)(2,1)S(1)}, bf16[8,2,32,256]{3,2,1,0:T(8,128)(2,1)S(1)}, u32[]{:S(2)}, u32[]{:S(2)}) collective-permute-start(bf16[8,2,32,256]{3,2,1,0:T(8,128)(2,1)S(1)} %collective-permute-done.3), channel_id=1, source_target_pairs={{0,2},{2,4},{4,6},{6,0},{1,3},{3,5},{5,7},{7,1},{8,10},{10,12},{12... | collective-permute-start | bytes 786440 | tf_op jit(solution)/shard_map/ppermute | solution.py:299
  44.1 4.1 %copy-start = (bf16[16,2,32,256]{3,2,1,0:T(8,128)(2,1)}, bf16[16,2,32,256]{3,2,1,0:T(8,128)(2,1)S(1)}, u32[]{:S(2)}) copy-start(bf16[16,2,32,256]{3,2,1,0:T(8,128)(2,1)S(1)} %all-to-all-done.1.qg) | copy-start | bytes 1572868
  44.1 4.1 %copy-start.7 = (bf16[8,2,32,256]{3,2,1,0:T(8,128)(2,1)}, bf16[8,2,32,256]{3,2,1,0:T(8,128)(2,1)S(1)}, u32[]{:S(2)}) copy-start(bf16[8,2,32,256]{3,2,1,0:T(8,128)(2,1)S(1)} %collective-permute-done.8) | copy-start | bytes 786436
  44.1 3.1 %collective-permute-start.9 = (bf16[8,2,32,256]{3,2,1,0:T(8,128)(2,1)S(1)}, bf16[8,2,32,256]{3,2,1,0:T(8,128)(2,1)S(1)}, u32[]{:S(2)}, u32[]{:S(2)}) collective-permute-start(bf16[8,2,32,256]{3,2,1,0:T(8,128)(2,1)S(1)} %collective-permute-done.3), channel_id=1, source_target_pairs={{0,1},{1,0},{2,3},{3,2},{4,5},{5,4},{6,7},{7,6},{8,9},{9,8},{10,11... | collective-permute-start | bytes 786440 | tf_op jit(solution)/shard_map/ppermute | solution.py:303
  44.2 4.0 %copy-start.8 = (bf16[8,2,32,256]{3,2,1,0:T(8,128)(2,1)}, bf16[8,2,32,256]{3,2,1,0:T(8,128)(2,1)S(1)}, u32[]{:S(2)}) copy-start(bf16[8,2,32,256]{3,2,1,0:T(8,128)(2,1)S(1)} %collective-permute-done.7) | copy-start | bytes 786436
  44.2 3.0 %collective-permute-start.10 = (bf16[8,2,32,256]{3,2,1,0:T(8,128)(2,1)S(1)}, bf16[8,2,32,256]{3,2,1,0:T(8,128)(2,1)S(1)}, u32[]{:S(2)}, u32[]{:S(2)}) collective-permute-start(bf16[8,2,32,256]{3,2,1,0:T(8,128)(2,1)S(1)} %collective-permute-done.1), channel_id=1, source_target_pairs={{0,1},{1,0},{2,3},{3,2},{4,5},{5,4},{6,7},{7,6},{8,9},{9,8},{10,11... | collective-permute-start | bytes 786440 | tf_op jit(solution)/shard_map/ppermute | solution.py:303
  44.7 3.5 %copy-start.9 = (bf16[8,2,32,256]{3,2,1,0:T(8,128)(2,1)}, bf16[8,2,32,256]{3,2,1,0:T(8,128)(2,1)S(1)}, u32[]{:S(2)}) copy-start(bf16[8,2,32,256]{3,2,1,0:T(8,128)(2,1)S(1)} %collective-permute-done.14) | copy-start | bytes 786436
  44.7 2.5 %collective-permute-start.13 = (bf16[8,2,32,256]{3,2,1,0:T(8,128)(2,1)S(1)}, bf16[8,2,32,256]{3,2,1,0:T(8,128)(2,1)}, u32[]{:S(2)}, u32[]{:S(2)}) collective-permute-start(bf16[8,2,32,256]{3,2,1,0:T(8,128)(2,1)S(1)} %collective-permute-done.2), channel_id=1, source_target_pairs={{0,1},{1,0},{2,3},{3,2},{4,5},{5,4},{6,7},{7,6},{8,9},{9,8},{10,11... | collective-permute-start | bytes 786440 | tf_op jit(solution)/shard_map/ppermute | solution.py:303
  45.2 3.0 %copy-start.10 = (bf16[8,2,32,256]{3,2,1,0:T(8,128)(2,1)}, bf16[8,2,32,256]{3,2,1,0:T(8,128)(2,1)S(1)}, u32[]{:S(2)}) copy-start(bf16[8,2,32,256]{3,2,1,0:T(8,128)(2,1)S(1)} %collective-permute-done.6) | copy-start | bytes 786436
  45.2 2.0 %collective-permute-start.12 = (bf16[8,2,32,256]{3,2,1,0:T(8,128)(2,1)S(1)}, bf16[8,2,32,256]{3,2,1,0:T(8,128)(2,1)}, u32[]{:S(2)}, u32[]{:S(2)}) collective-permute-start(bf16[8,2,32,256]{3,2,1,0:T(8,128)(2,1)S(1)} %collective-permute-done.6), channel_id=1, source_target_pairs={{0,1},{1,0},{2,3},{3,2},{4,5},{5,4},{6,7},{7,6},{8,9},{9,8},{10,11... | collective-permute-start | bytes 786440 | tf_op jit(solution)/shard_map/ppermute | solution.py:303
  46.5 1.7 %copy-start.11 = (bf16[8,2,32,256]{3,2,1,0:T(8,128)(2,1)}, bf16[8,2,32,256]{3,2,1,0:T(8,128)(2,1)S(1)}, u32[]{:S(2)}) copy-start(bf16[8,2,32,256]{3,2,1,0:T(8,128)(2,1)S(1)} %collective-permute-done.4) | copy-start | bytes 786436
  46.5 1.7 %collective-permute-start.11 = (bf16[8,2,32,256]{3,2,1,0:T(8,128)(2,1)S(1)}, bf16[8,2,32,256]{3,2,1,0:T(8,128)(2,1)}, u32[]{:S(2)}, u32[]{:S(2)}) collective-permute-start(bf16[8,2,32,256]{3,2,1,0:T(8,128)(2,1)S(1)} %collective-permute-done.4), channel_id=1, source_target_pairs={{0,1},{1,0},{2,3},{3,2},{4,5},{5,4},{6,7},{7,6},{8,9},{9,8},{10,11... | collective-permute-start | bytes 786440 | tf_op jit(solution)/shard_map/ppermute | solution.py:303
  47.2 1.1 copy-start.12
  47.2 1.1 copy-start.13
  63.6 1.8 %collective-permute-start.17 = (bf16[8,2,32,256]{3,2,1,0:T(8,128)(2,1)}, bf16[8,2,32,256]{3,2,1,0:T(8,128)(2,1)S(1)}, u32[]{:S(2)}, u32[]{:S(2)}) collective-permute-start(bf16[8,2,32,256]{3,2,1,0:T(8,128)(2,1)} %get-tuple-element.42), channel_id=1, source_target_pairs={{0,1},{1,0},{2,3},{3,2},{4,5},{5,4},{6,7},{7,6},{8,9},{9,8},{10,11... | collective-permute-start | bytes 786440 | tf_op jit(solution)/shard_map/ppermute | solution.py:303
  63.8 2.9 %collective-permute-start.22 = (bf16[8,2,32,256]{3,2,1,0:T(8,128)(2,1)}, bf16[8,2,32,256]{3,2,1,0:T(8,128)(2,1)S(1)}, u32[]{:S(2)}, u32[]{:S(2)}) collective-permute-start(bf16[8,2,32,256]{3,2,1,0:T(8,128)(2,1)} %get-tuple-element.48), channel_id=1, source_target_pairs={{0,1},{1,0},{2,3},{3,2},{4,5},{5,4},{6,7},{7,6},{8,9},{9,8},{10,11... | collective-permute-start | bytes 786440 | tf_op jit(solution)/shard_map/ppermute | solution.py:303
  64.2 15.4 %collective-permute-start.15 = (bf16[8,2,32,256]{3,2,1,0:T(8,128)(2,1)}, bf16[8,2,32,256]{3,2,1,0:T(8,128)(2,1)S(1)}, u32[]{:S(2)}, u32[]{:S(2)}) collective-permute-start(bf16[8,2,32,256]{3,2,1,0:T(8,128)(2,1)} %get-tuple-element.39), channel_id=1, source_target_pairs={{0,1},{1,0},{2,3},{3,2},{4,5},{5,4},{6,7},{7,6},{8,9},{9,8},{10,11... | collective-permute-start | bytes 786440 | tf_op jit(solution)/shard_map/ppermute | solution.py:303
  64.4 3.8 %collective-permute-start.19 = (bf16[8,2,32,256]{3,2,1,0:T(8,128)(2,1)}, bf16[8,2,32,256]{3,2,1,0:T(8,128)(2,1)S(1)}, u32[]{:S(2)}, u32[]{:S(2)}) collective-permute-start(bf16[8,2,32,256]{3,2,1,0:T(8,128)(2,1)} %get-tuple-element.44), channel_id=1, source_target_pairs={{0,1},{1,0},{2,3},{3,2},{4,5},{5,4},{6,7},{7,6},{8,9},{9,8},{10,11... | collective-permute-start | bytes 786440 | tf_op jit(solution)/shard_map/ppermute | solution.py:303
  64.7 4.9 %collective-permute-start.21 = (bf16[8,2,32,256]{3,2,1,0:T(8,128)(2,1)}, bf16[8,2,32,256]{3,2,1,0:T(8,128)(2,1)S(1)}, u32[]{:S(2)}, u32[]{:S(2)}) collective-permute-start(bf16[8,2,32,256]{3,2,1,0:T(8,128)(2,1)} %get-tuple-element.46), channel_id=1, source_target_pairs={{0,1},{1,0},{2,3},{3,2},{4,5},{5,4},{6,7},{7,6},{8,9},{9,8},{10,11... | collective-permute-start | bytes 786440 | tf_op jit(solution)/shard_map/ppermute | solution.py:303
  65.4 1.9 %collective-permute-start.26 = (bf16[8,2,32,256]{3,2,1,0:T(8,128)(2,1)}, bf16[8,2,32,256]{3,2,1,0:T(8,128)(2,1)S(1)}, u32[]{:S(2)}, u32[]{:S(2)}) collective-permute-start(bf16[8,2,32,256]{3,2,1,0:T(8,128)(2,1)} %get-tuple-element.52), channel_id=1, source_target_pairs={{0,1},{1,0},{2,3},{3,2},{4,5},{5,4},{6,7},{7,6},{8,9},{9,8},{10,11... | collective-permute-start | bytes 786440 | tf_op jit(solution)/shard_map/ppermute | solution.py:303
  65.6 1.1 copy-start.27
  65.6 1.5 %copy-start.17 = (bf16[8,2,32,256]{3,2,1,0:T(8,128)(2,1)S(1)}, bf16[8,2,32,256]{3,2,1,0:T(8,128)(2,1)}, u32[]{:S(2)}) copy-start(bf16[8,2,32,256]{3,2,1,0:T(8,128)(2,1)} %get-tuple-element.47) | copy-start | bytes 786436
  66.7 9.8 %collective-permute-start.25 = (bf16[8,2,32,256]{3,2,1,0:T(8,128)(2,1)S(1)}, bf16[8,2,32,256]{3,2,1,0:T(8,128)(2,1)S(1)}, u32[]{:S(2)}, u32[]{:S(2)}) collective-permute-start(bf16[8,2,32,256]{3,2,1,0:T(8,128)(2,1)S(1)} %copy-done.27), channel_id=1, source_target_pairs={{0,1},{1,0},{2,3},{3,2},{4,5},{5,4},{6,7},{7,6},{8,9},{9,8},{10,11... | collective-permute-start | bytes 786440 | tf_op jit(solution)/shard_map/ppermute | solution.py:303
  67.1 1.0 copy-start.16
  67.3 8.4 %collective-permute-start.23 = (bf16[8,2,32,256]{3,2,1,0:T(8,128)(2,1)S(1)}, bf16[8,2,32,256]{3,2,1,0:T(8,128)(2,1)S(1)}, u32[]{:S(2)}, u32[]{:S(2)}) collective-permute-start(bf16[8,2,32,256]{3,2,1,0:T(8,128)(2,1)S(1)} %add_convert_fusion.3), channel_id=1, source_target_pairs={{0,6},{2,0},{4,2},{6,4},{1,7},{3,1},{5,3},{7,5},{8,14},{10,8},{12,... | collective-permute-start | bytes 786440 | tf_op jit(solution)/shard_map/ppermute | solution.py:299
  68.1 1.4 %copy-start.15 = (bf16[8,2,32,256]{3,2,1,0:T(8,128)(2,1)S(1)}, bf16[8,2,32,256]{3,2,1,0:T(8,128)(2,1)}, u32[]{:S(2)}) copy-start(bf16[8,2,32,256]{3,2,1,0:T(8,128)(2,1)} %get-tuple-element.43) | copy-start | bytes 786436
  68.2 10.9 %collective-permute-start.27 = (bf16[8,2,32,256]{3,2,1,0:T(8,128)(2,1)S(1)}, bf16[8,2,32,256]{3,2,1,0:T(8,128)(2,1)S(1)}, u32[]{:S(2)}, u32[]{:S(2)}) collective-permute-start(bf16[8,2,32,256]{3,2,1,0:T(8,128)(2,1)S(1)} %add_convert_fusion.1), channel_id=1, source_target_pairs={{0,2},{2,4},{4,6},{6,0},{1,3},{3,5},{5,7},{7,1},{8,10},{10,12},{12... | collective-permute-start | bytes 786440 | tf_op jit(solution)/shard_map/ppermute | solution.py:299
  69.5 1.0 copy-start.26
  69.5 6.9 %copy-start.24 = (bf16[8,2,32,256]{3,2,1,0:T(8,128)(2,1)S(1)}, bf16[8,2,32,256]{3,2,1,0:T(8,128)(2,1)}, u32[]{:S(2)}) copy-start(bf16[8,2,32,256]{3,2,1,0:T(8,128)(2,1)} %get-tuple-element.45) | copy-start | bytes 786436
  70.5 10.9 %collective-permute-start.16 = (bf16[8,2,32,256]{3,2,1,0:T(8,128)(2,1)S(1)}, bf16[8,2,32,256]{3,2,1,0:T(8,128)(2,1)S(1)}, u32[]{:S(2)}, u32[]{:S(2)}) collective-permute-start(bf16[8,2,32,256]{3,2,1,0:T(8,128)(2,1)S(1)} %copy-done.26), channel_id=1, source_target_pairs={{0,1},{1,0},{2,3},{3,2},{4,5},{5,4},{6,7},{7,6},{8,9},{9,8},{10,11... | collective-permute-start | bytes 786440 | tf_op jit(solution)/shard_map/ppermute | solution.py:303
  75.7 10.5 %collective-permute-start.18 = (bf16[8,2,32,256]{3,2,1,0:T(8,128)(2,1)S(1)}, bf16[8,2,32,256]{3,2,1,0:T(8,128)(2,1)S(1)}, u32[]{:S(2)}, u32[]{:S(2)}) collective-permute-start(bf16[8,2,32,256]{3,2,1,0:T(8,128)(2,1)S(1)} %add_convert_fusion.5), channel_id=1, source_target_pairs={{0,2},{2,4},{4,6},{6,0},{1,3},{3,5},{5,7},{7,1},{8,10},{10,12},{12... | collective-permute-start | bytes 786440 | tf_op jit(solution)/shard_map/ppermute | solution.py:299
  76.4 3.0 %copy-start.23 = (bf16[8,2,32,256]{3,2,1,0:T(8,128)(2,1)S(1)}, bf16[8,2,32,256]{3,2,1,0:T(8,128)(2,1)}, u32[]{:S(2)}) copy-start(bf16[8,2,32,256]{3,2,1,0:T(8,128)(2,1)} %get-tuple-element.49) | copy-start | bytes 786436
  76.6 9.6 %collective-permute-start.20 = (bf16[8,2,32,256]{3,2,1,0:T(8,128)(2,1)S(1)}, bf16[8,2,32,256]{3,2,1,0:T(8,128)(2,1)S(1)}, u32[]{:S(2)}, u32[]{:S(2)}) collective-permute-start(bf16[8,2,32,256]{3,2,1,0:T(8,128)(2,1)S(1)} %add_convert_fusion.4), channel_id=1, source_target_pairs={{0,6},{2,0},{4,2},{6,4},{1,7},{3,1},{5,3},{7,5},{8,14},{10,8},{12,... | collective-permute-start | bytes 786440 | tf_op jit(solution)/shard_map/ppermute | solution.py:299
  79.1 10.4 %collective-permute-start.24 = (bf16[8,2,32,256]{3,2,1,0:T(8,128)(2,1)S(1)}, bf16[8,2,32,256]{3,2,1,0:T(8,128)(2,1)S(1)}, u32[]{:S(2)}, u32[]{:S(2)}) collective-permute-start(bf16[8,2,32,256]{3,2,1,0:T(8,128)(2,1)S(1)} %add_convert_fusion.2), channel_id=1, source_target_pairs={{0,6},{2,0},{4,2},{6,4},{1,7},{3,1},{5,3},{7,5},{8,14},{10,8},{12,... | collective-permute-start | bytes 786440 | tf_op jit(solution)/shard_map/ppermute | solution.py:299
  79.6 10.5 %copy-start.14 = (bf16[8,2,32,256]{3,2,1,0:T(8,128)(2,1)}, bf16[8,2,32,256]{3,2,1,0:T(8,128)(2,1)S(1)}, u32[]{:S(2)}) copy-start(bf16[8,2,32,256]{3,2,1,0:T(8,128)(2,1)S(1)} %collective-permute-done.15.refs_3_) | copy-start | bytes 786436
  79.6 10.5 %collective-permute-start.28 = (bf16[8,2,32,256]{3,2,1,0:T(8,128)(2,1)S(1)}, bf16[8,2,32,256]{3,2,1,0:T(8,128)(2,1)S(1)}, u32[]{:S(2)}, u32[]{:S(2)}) collective-permute-start(bf16[8,2,32,256]{3,2,1,0:T(8,128)(2,1)S(1)} %add_convert_fusion), channel_id=1, source_target_pairs={{0,2},{2,4},{4,6},{6,0},{1,3},{3,5},{5,7},{7,1},{8,10},{10,12},{12... | collective-permute-start | bytes 786440 | tf_op jit(solution)/shard_map/ppermute | solution.py:299
  81.4 8.7 %copy-start.18 = (bf16[8,2,32,256]{3,2,1,0:T(8,128)(2,1)}, bf16[8,2,32,256]{3,2,1,0:T(8,128)(2,1)S(1)}, u32[]{:S(2)}) copy-start(bf16[8,2,32,256]{3,2,1,0:T(8,128)(2,1)S(1)} %collective-permute-done.16.refs_4_) | copy-start | bytes 786436
  86.1 3.9 %copy-start.19 = (bf16[8,2,32,256]{3,2,1,0:T(8,128)(2,1)}, bf16[8,2,32,256]{3,2,1,0:T(8,128)(2,1)S(1)}, u32[]{:S(2)}) copy-start(bf16[8,2,32,256]{3,2,1,0:T(8,128)(2,1)S(1)} %collective-permute-done.18.refs_5_) | copy-start | bytes 786436
  86.1 3.9 %copy-start.20 = (bf16[8,2,32,256]{3,2,1,0:T(8,128)(2,1)}, bf16[8,2,32,256]{3,2,1,0:T(8,128)(2,1)S(1)}, u32[]{:S(2)}) copy-start(bf16[8,2,32,256]{3,2,1,0:T(8,128)(2,1)S(1)} %collective-permute-done.20.refs_6_) | copy-start | bytes 786436
  89.5 0.7 copy-start.21
  90.1 0.7 copy-start.22

commit v4 on v3

v4 whole, which is shorter than its diff:
```python
import functools

import jax
import jax.numpy as jnp
from jax import lax
from jax.experimental import pallas as pl
from jax.experimental.pallas import tpu as pltpu
from jax.sharding import Mesh
from jax.sharding import PartitionSpec as P

EPSILON = 1e-05
NEGATIVE = -1e30
LOG2E = 1.4426950408889634

STRIPE = 32
SLICES = 16
PARTS = 8
WIDTH = 256
HALF = 128
ROWS = SLICES * STRIPE
TILE = 64
NEXT = TILE // STRIPE
GROUPS = ROWS // TILE
CHUNK = PARTS * TILE
STORED = sum(ROWS - j * TILE for j in range(GROUPS))
STEP = 256
SPAN = STEP // TILE
STEPS = PARTS // SPAN
HALVES = GROUPS // 2
LIVE_STEPS = STEPS // 2
SECTION = ("x", "y")
ALL = ("x", "y", "z", "core")
SCALE = HALF ** (-0.5)


def pack_kernel(a_ref, b_ref, out_ref):
    for head in range(SLICES):
        cols = slice(head * WIDTH, (head + 1) * WIDTH)
        out_ref[head, 0] = a_ref[:, cols]
        out_ref[head, 1] = b_ref[:, cols]


def pack(a, b):
    return pl.pallas_call(
        pack_kernel,
        out_shape=jax.ShapeDtypeStruct((SLICES, 2, STRIPE, WIDTH), a.dtype),
        in_specs=[pl.BlockSpec(memory_space=pltpu.VMEM)] * 2,
        out_specs=pl.BlockSpec(memory_space=pltpu.VMEM),
        name="pack",
    )(a, b)


def unpack_kernel(in_ref, *outs):
    for head in range(SLICES):
        for i, out in enumerate(outs):
            out[:, head * WIDTH : (head + 1) * WIDTH] = in_ref[head, i]


def unpack(x):
    shape = jax.ShapeDtypeStruct((STRIPE, SLICES * WIDTH), x.dtype)
    return pl.pallas_call(
        unpack_kernel,
        out_shape=(shape,) * 3,
        in_specs=[pl.BlockSpec(memory_space=pltpu.VMEM)],
        out_specs=(pl.BlockSpec(memory_space=pltpu.VMEM),) * 3,
        name="unpack",
    )(x)


def dot_nt(a, b):
    return lax.dot_general(a, b, (((1,), (1,)), ((), ())), preferred_element_type=jnp.float32)


def dot_nn(a, b):
    return lax.dot_general(a, b, (((1,), (0,)), ((), ())), preferred_element_type=jnp.float32)


def dot_tn(a, b):
    return lax.dot_general(a, b, (((0,), (0,)), ((), ())), preferred_element_type=jnp.float32)


def fold(op, x):
    out = x[:, :128]
    for c in range(1, x.shape[1] // 128):
        out = op(out, x[:, c * 128 : (c + 1) * 128])
    return out


def core_kernel(lengths, where, lams, qg_in, *refs):
    kv_halves = refs[: 2 * PARTS]
    dq_out, *term_outs = refs[2 * PARTS : 4 * PARTS + 1]
    qg, dq, kvs, p1s, p2s, das, mixs, t1s, t2s, outs, stat1, stat2, wide, dos, in_sems, out_sems = refs[
        4 * PARTS + 1 :
    ]

    copies = {}

    def fetch(name, src, dst):
        copy = pltpu.make_async_copy(src, dst, in_sems.at[sum(map(len, copies.values()))])
        copy.start()
        copies.setdefault(name, []).append(copy)

    def arrived(*name):
        for copy in copies[name]:
            copy.wait()

    fetch(("queries",), qg_in, qg)
    for kind in range(2):
        for half in range(2):
            for u in range(PARTS):
                chunks = slice(half * HALVES, (half + 1) * HALVES)
                fetch((kind, half), kv_halves[2 * u + half].at[:, :, kind], kvs.at[chunks, where[u], :, kind])

    def keys(j, parts=slice(0, PARTS)):
        return kvs[j, parts, :, 0].reshape(-1, WIDTH)

    def values(j, parts=slice(0, PARTS)):
        return kvs[j, parts, :, 1].reshape(-1, WIDTH)

    def of(j, skip=0, count=None):
        first = sum(ROWS - i * TILE for i in range(j)) + skip
        return slice(first, first + (ROWS - j * TILE - skip if count is None else count))

    lane = lax.broadcasted_iota(jnp.int32, (1, STEP), 1)
    lane_slice = lane % TILE // STRIPE

    weight = lams[where[PARTS] % 2]
    row = lax.broadcasted_iota(jnp.int32, (ROWS, 1), 0)
    row_slot = where[0] * STRIPE + row % STRIPE
    tile_pos = 256 * (row[:TILE] // STRIPE) + row_slot[:TILE]
    arrived("queries")
    q = qg[:, 0].reshape(ROWS, WIDTH)
    q1, q2 = q[:, :HALF], q[:, HALF:]
    stat1[...] = jnp.full((ROWS, 128), NEGATIVE, jnp.float32)
    stat2[...] = jnp.full((ROWS, 128), NEGATIVE, jnp.float32)

    for j in range(GROUPS):
        lo = j * TILE
        if j % HALVES == 0:
            arrived(0, j // HALVES)

        for step in range(STEPS):
            k = keys(j, slice(SPAN * step, SPAN * step + SPAN))
            cols = slice(step * STEP, (step + 1) * STEP)
            slot = (SPAN * step + lane // TILE) * STRIPE + lane % STRIPE
            vis = 256 * lane_slice + slot <= tile_pos
            if step >= LIVE_STEPS:
                length = jnp.full((1, STEP), lengths[NEXT * j], jnp.int32)
                for nl in range(1, NEXT):
                    length = jnp.where(lane_slice == nl, lengths[NEXT * j + nl], length)
                vis = vis & (slot < length)
                hide = jnp.where(slot < length, 0.0, NEGATIVE)
            for half, p, stat in ((0, p1s, stat1), (HALF, p2s, stat2)):
                scores = dot_nt(q[lo:, half : half + HALF], k[:, half : half + HALF])
                top, rest = jnp.where(vis, scores[:TILE], NEGATIVE), scores[TILE:]
                p[of(j, 0, TILE), cols] = top
                stat[lo : lo + TILE] = jnp.maximum(stat[lo : lo + TILE], fold(jnp.maximum, top))
                if j < GROUPS - 1:
                    rest = rest + hide if step >= LIVE_STEPS else rest
                    p[of(j, TILE), cols] = rest
                    stat[lo + TILE :] = jnp.maximum(stat[lo + TILE :], fold(jnp.maximum, rest))

    m1 = jnp.max(stat1[...], axis=1, keepdims=True)
    m2 = jnp.max(stat2[...], axis=1, keepdims=True)
    stat1[...] = jnp.zeros((ROWS, 128), jnp.float32)
    stat2[...] = jnp.zeros((ROWS, 128), jnp.float32)
    for j in range(GROUPS):
        lo = j * TILE

        for step in range(STEPS):
            cols = slice(step * STEP, (step + 1) * STEP)
            p1 = jnp.exp2((p1s[of(j), cols] - m1[lo:]) * (SCALE * LOG2E))
            p2 = jnp.exp2((p2s[of(j), cols] - m2[lo:]) * (SCALE * LOG2E))
            p1s[of(j), cols] = p1
            p2s[of(j), cols] = p2
            stat1[lo:] += fold(jnp.add, p1)
            stat2[lo:] += fold(jnp.add, p2)

    inv1 = 1.0 / jnp.sum(stat1[...], axis=1, keepdims=True)
    inv2 = 1.0 / jnp.sum(stat2[...], axis=1, keepdims=True)
    winv2 = weight * inv2

    wide[...] = jnp.zeros((ROWS, WIDTH), jnp.float32)
    for j in range(GROUPS):
        lo = j * TILE
        if j % HALVES == 0:
            arrived(1, j // HALVES)

        for step in range(STEPS):
            cols = slice(step * STEP, (step + 1) * STEP)
            a = p1s[of(j), cols] * inv1[lo:] - p2s[of(j), cols] * winv2[lo:]
            mixs[of(j), cols] = a.astype(jnp.bfloat16)

        wide[lo:] += dot_nn(mixs[of(j)], values(j))

    for n in range(SLICES):
        part = slice(n * STRIPE, (n + 1) * STRIPE)
        o = wide[part]
        factor = lax.rsqrt(jnp.mean(o * o, axis=1, keepdims=True) + EPSILON)
        y = o * factor
        live = (row_slot[:STRIPE] < lengths[n]).astype(jnp.float32)
        g = qg[n, 1].astype(jnp.float32) * live
        d_out = factor * (g - y * jnp.mean(g * y, axis=1, keepdims=True))
        dos[part] = d_out.astype(jnp.bfloat16)
    d_out = dos[...]

    stat1[...] = jnp.zeros((ROWS, 128), jnp.float32)
    stat2[...] = jnp.zeros((ROWS, 128), jnp.float32)
    for j in range(GROUPS):
        lo = j * TILE

        for step in range(STEPS):
            cols = slice(step * STEP, (step + 1) * STEP)
            da = dot_nt(d_out[lo:], values(j, slice(SPAN * step, SPAN * step + SPAN)))
            das[of(j), cols] = da
            stat1[lo:] += fold(jnp.add, da * p1s[of(j), cols])
            stat2[lo:] += fold(jnp.add, da * p2s[of(j), cols])

    e1 = jnp.sum(stat1[...], axis=1, keepdims=True) * inv1
    e2 = jnp.sum(stat2[...], axis=1, keepdims=True) * inv2

    wide[...] = jnp.zeros((ROWS, WIDTH), jnp.float32)
    out_copies = []

    def send(src, dst):
        copy = pltpu.make_async_copy(src, dst, out_sems.at[len(out_copies)])
        copy.start()
        out_copies.append(copy)

    for j in range(GROUPS):
        lo = j * TILE

        for step in range(STEPS):
            cols = slice(step * STEP, (step + 1) * STEP)
            da = das[of(j), cols]
            t1 = p1s[of(j), cols] * (inv1[lo:] * (da - e1[lo:]))
            t2 = p2s[of(j), cols] * (inv2[lo:] * (da - e2[lo:]))
            t1s[of(j), cols] = t1.astype(jnp.bfloat16)
            t2s[of(j), cols] = t2.astype(jnp.bfloat16)

        k = keys(j)
        wide[lo:, :HALF] += dot_nn(t1s[of(j)], k[:, :HALF])
        wide[lo:, HALF:] += dot_nn(t2s[of(j)], k[:, HALF:])

        for step in range(STEPS):
            cols = slice(step * STEP, (step + 1) * STEP)
            dk1 = dot_tn(q1[lo:], t1s[of(j), cols]) * SCALE
            dk2 = dot_tn(q2[lo:], t2s[of(j), cols]) * (-SCALE * weight)
            dk = jnp.concatenate([dk1, dk2], axis=0)
            dv = dot_tn(d_out[lo:], mixs[of(j), cols])
            parts = slice(SPAN * step, SPAN * step + SPAN)
            for kind, x in ((0, dk), (1, dv)):
                outs[j // HALVES, parts, j % HALVES, :, kind] = (
                    x.T.astype(jnp.bfloat16).reshape(SPAN, NEXT, STRIPE, WIDTH)
                )

        for u in range(PARTS):
            half, at = j // HALVES, j % HALVES
            send(outs.at[half, where[u], at], term_outs[2 * u + half].at[at])

    dq[:, :, :HALF] = (wide[:, :HALF] * SCALE).astype(jnp.bfloat16).reshape(SLICES, STRIPE, HALF)
    dq[:, :, HALF:] = (
        (wide[:, HALF:] * (-SCALE * weight)).astype(jnp.bfloat16).reshape(SLICES, STRIPE, HALF)
    )
    send(dq, dq_out)
    for copy in out_copies:
        copy.wait()


def core(lengths, where, lams, qg, kv_halves):
    smem = pl.BlockSpec(memory_space=pltpu.SMEM)
    hbm = pl.BlockSpec(memory_space=pl.ANY)
    b16, f32 = jnp.bfloat16, jnp.float32
    halves = [x.reshape(HALVES, NEXT, 2, STRIPE, WIDTH) for x in kv_halves]
    d_query, *terms = pl.pallas_call(
        core_kernel,
        out_shape=(
            jax.ShapeDtypeStruct((SLICES, STRIPE, WIDTH), b16),
        )
        + (jax.ShapeDtypeStruct((HALVES, NEXT, 2, STRIPE, WIDTH), b16),) * (2 * PARTS),
        in_specs=[smem, smem, smem, hbm] + [hbm] * (2 * PARTS),
        out_specs=(hbm,) + (hbm,) * (2 * PARTS),
        scratch_shapes=[
            pltpu.VMEM((SLICES, 2, STRIPE, WIDTH), b16),
            pltpu.VMEM((SLICES, STRIPE, WIDTH), b16),
            pltpu.VMEM((GROUPS, PARTS, NEXT, 2, STRIPE, WIDTH), b16),
            pltpu.VMEM((STORED, CHUNK), f32),
            pltpu.VMEM((STORED, CHUNK), f32),
            pltpu.VMEM((STORED, CHUNK), f32),
            pltpu.VMEM((STORED, CHUNK), b16),
            pltpu.VMEM((STORED, CHUNK), b16),
            pltpu.VMEM((STORED, CHUNK), b16),
            pltpu.VMEM((2, PARTS, HALVES, NEXT, 2, STRIPE, WIDTH), b16),
            pltpu.VMEM((ROWS, 128), f32),
            pltpu.VMEM((ROWS, 128), f32),
            pltpu.VMEM((ROWS, WIDTH), f32),
            pltpu.VMEM((ROWS, WIDTH), b16),
            pltpu.SemaphoreType.DMA((1 + PARTS * 4,)),
            pltpu.SemaphoreType.DMA((1 + PARTS * GROUPS,)),
        ],
        compiler_params=pltpu.CompilerParams(vmem_limit_bytes=60 * 1024 * 1024),
        name="attention",
    )(lengths, where, lams, qg, *halves)
    return d_query, *[x.reshape(SLICES // 2, 2, STRIPE, WIDTH) for x in terms]


def final_kernel(*refs):
    d_query, *ins, out = refs
    out[:, 0] = d_query[...]
    for half in range(2):
        total = ins[half][...].astype(jnp.float32)
        for x in ins[2 + half :: 2]:
            total = total + x[...].astype(jnp.float32)
        out[8 * half : 8 * half + 8, 1:] = total.astype(out.dtype)


def final(d_query, *halves):
    return pl.pallas_call(
        final_kernel,
        out_shape=jax.ShapeDtypeStruct((SLICES, 3, STRIPE, WIDTH), jnp.bfloat16),
        in_specs=[pl.BlockSpec(memory_space=pltpu.VMEM)] * (1 + len(halves)),
        out_specs=pl.BlockSpec(memory_space=pltpu.VMEM),
        name="final",
    )(d_query, *halves)


def along_z(x, d):
    return lax.ppermute(x, "z", [(i, (i + d) % 4) for i in range(4)])


def swap(x):
    return lax.ppermute(x, "core", [(0, 1), (1, 0)])


def shards(queries, keys, values, out_grad, lam, lengths):
    z, c = lax.axis_index("z"), lax.axis_index("core")
    section = lax.axis_index("x") * 4 + lax.axis_index("y")
    where = jnp.stack(
        [2 * ((z - d) % 4) + c for d in range(4)]
        + [2 * ((z - d) % 4) + 1 - c for d in range(4)]
        + [section]
    ).astype(jnp.int32)

    kv = lax.all_to_all(pack(keys, values), SECTION, 0, 0, tiled=True)
    lams = lax.ppermute(
        lam, ALL, [(s * 8 + t, (2 * t + s // 8) * 8 + s % 8) for s in range(SLICES) for t in range(PARTS)]
    )
    kv, qg, lams, where = lax.optimization_barrier((kv, pack(queries, out_grad), lams, where))
    lower, upper = lax.optimization_barrier((kv[:8], kv[8:]))
    lower_up, upper_down = along_z(lower, 1), along_z(upper, -1)
    upper_up, lower_down = along_z(upper, 1), along_z(lower, -1)
    lower_far, upper_far = along_z(lower_up, 1), along_z(upper_down, -1)
    qg = lax.all_to_all(qg, SECTION, 0, 0, tiled=True)
    upper_up, lower_down, qg = lax.optimization_barrier((upper_up, lower_down, qg))
    near = [lower, upper, lower_up, upper_up, lower_far, upper_far, lower_down, upper_down]

    d_query, *terms = core(lengths, where, lams, qg, near + [swap(x) for x in near])

    def add(*xs):
        return sum(x.astype(jnp.float32) for x in xs).astype(jnp.bfloat16)

    own, other = terms[:PARTS], [swap(x) for x in terms[PARTS:]]
    lower_far = along_z(add(own[4], other[4]), -1)
    upper_far = along_z(add(own[5], other[5]), 1)
    upper_1 = along_z(add(own[3], other[3]), -1)
    lower_3 = along_z(add(own[6], other[6]), 1)
    lower_1 = along_z(add(own[2], other[2], lower_far), -1)
    upper_3 = along_z(add(own[7], other[7], upper_far), 1)
    total = final(d_query, own[0], own[1], other[0], other[1], lower_3, upper_1, lower_1, upper_3)
    return unpack(lax.all_to_all(total, SECTION, 0, 0, tiled=True))


def solution(mesh):
    fine = Mesh(mesh.devices.reshape(4, 4, 4, 2), ("x", "y", "z", "core"))
    rows = P(ALL, None)
    return jax.shard_map(
        shards,
        mesh=fine,
        in_specs=(rows, rows, rows, rows, P(("z", "core")), P()),
        out_specs=(rows, rows, rows),
        check_vma=False,
    )
```

time: 115 us -> 114 us (level)
  Pallas kernels: 23.9 us -> 21.9 us
    pallas_call x1, Pallas kernels: 15.4 us -> 13.4 us  [core(): pl.pallas_call(core_kernel, out_shape=(jax.ShapeDtypeStruct((SLICES, STRI...]
    unnamed x58 -> x64, local copies, waits for them, and re-layouts: 2.13 us -> 2.79 us
where the time goes in v4:
time: 114 us; the launch traced here: 113 us
  starting transfers between devices  33.1 us (29%)
  waiting for transfers between devices  33 us (29%)
  Pallas kernels  21.9 us (19%)
  blocking collectives  18.7 us (16%)
  local copies, waits for them, and re-layouts  3.51 us (3%)
  other arithmetic  1.68 us (1%)
    ppermute x12, waiting for transfers between devices, along_z(): return lax.ppermute(x, 'z', [(i, (i + d) % 4) for i in range(4)])  19.5 us
    all_to_all x1, blocking collectives, shards(): return unpack(lax.all_to_all(total, SECTION, 0, 0, tiled=True))  18.7 us
    ppermute x12, starting transfers between devices, along_z(): return lax.ppermute(x, 'z', [(i, (i + d) % 4) for i in range(4)])  16.5 us
    pallas_call x1, Pallas kernels, core(): pl.pallas_call(core_kernel, out_shape=(jax.ShapeDtypeStruct((SLICES, STRI...  13.4 us
    all_to_all x1, waiting for transfers between devices, shards(): kv = lax.all_to_all(pack(keys, values), SECTION, 0, 0, tiled=True)  8.2 us
    all_to_all x1, starting transfers between devices, shards(): kv = lax.all_to_all(pack(keys, values), SECTION, 0, 0, tiled=True)  7.25 us
    all_to_all x1, starting transfers between devices, shards(): qg = lax.all_to_all(qg, SECTION, 0, 0, tiled=True)  5.28 us
    pallas_call x2, Pallas kernels, pack(): pl.pallas_call(pack_kernel, out_shape=jax.ShapeDtypeStruct((SLICES, 2, ST...  3.73 us
  transfers between devices with their start and end apart: 31, of which 13 were waited for; matrix products, arithmetic and copies ran while one was open for 2% of the time, Pallas kernels for 2%

profile of v4, /device:TPU:0, one launch (start us, length us, event | category | flops | bytes accessed | tf_op | source)
XLA Modules:
  0.0 113.1 jit_solution(11651636098553970280)
XLA Ops:
  0.6 1.9 %pack.2 = bf16[16,2,32,256]{3,2,1,0:T(8,128)(2,1)} custom-call(bf16[32,4096]{1,0:T(8,128)(2,1)} %a_ref.2, bf16[32,4096]{1,0:T(8,128)(2,1)} %b_ref.2), custom_call_target="tpu_custom_call" | custom-call | tf_op jit(solution)/shard_map/pack/pallas_call | solution.py:44
  2.5 7.2 %all-to-all-start = ((bf16[16,2,32,256]{3,2,1,0:T(8,128)(2,1)}), bf16[16,2,32,256]{3,2,1,0:T(8,128)(2,1)S(1)}, u32[]{:S(2)}, u32[]{:S(2)}) async-start(bf16[16,2,32,256]{3,2,1,0:T(8,128)(2,1)} %pack.2), calls=%async_computation | async-start | bytes 1048576 | tf_op jit(solution)/shard_map/all_to_all | solution.py:344
  9.8 0.7 collective-permute-start
  10.5 1.9 %pack.3 = bf16[16,2,32,256]{3,2,1,0:T(8,128)(2,1)} custom-call(bf16[32,4096]{1,0:T(8,128)(2,1)} %a_ref.3, bf16[32,4096]{1,0:T(8,128)(2,1)} %b_ref.3), custom_call_target="tpu_custom_call" | custom-call | tf_op jit(solution)/shard_map/pack/pallas_call | solution.py:44
  12.4 0.7 stack.39.where
  13.1 0.0 collective-permute-done.lams
  13.1 8.2 %all-to-all-done = bf16[16,2,32,256]{3,2,1,0:T(8,128)(2,1)S(1)} async-done(((bf16[16,2,32,256]{3,2,1,0:T(8,128)(2,1)}), bf16[16,2,32,256]{3,2,1,0:T(8,128)(2,1)S(1)}, u32[]{:S(2)}, u32[]{:S(2)}) %all-to-all-start) | async-done | bytes 524320 | tf_op jit(solution)/shard_map/all_to_all | solution.py:344
  21.3 0.0 copy-start.1
  21.3 0.0 copy-start.2
  21.3 4.1 %collective-permute-start.5 = (bf16[8,2,32,256]{3,2,1,0:T(8,128)(2,1)S(1)}, bf16[8,2,32,256]{3,2,1,0:T(8,128)(2,1)S(1)}, u32[]{:S(2)}, u32[]{:S(2)}) collective-permute-start(bf16[8,2,32,256]{3,2,1,0:T(8,128)(2,1)S(1)} %get-tuple-element.32), channel_id=1, source_target_pairs={{0,6},{2,0},{4,2},{6,4},{1,7},{3,1},{5,3},{7,5},{8,14},{10,8},{12,... | collective-permute-start | bytes 786440 | tf_op jit(solution)/shard_map/ppermute | solution.py:328
  25.4 0.0 collective-permute-start.1
  25.4 0.0 collective-permute-start.3
  25.4 3.3 %collective-permute-start.2 = (bf16[8,2,32,256]{3,2,1,0:T(8,128)(2,1)S(1)}, bf16[8,2,32,256]{3,2,1,0:T(8,128)(2,1)S(1)}, u32[]{:S(2)}, u32[]{:S(2)}) collective-permute-start(bf16[8,2,32,256]{3,2,1,0:T(8,128)(2,1)S(1)} %get-tuple-element.33), channel_id=1, source_target_pairs={{0,6},{2,0},{4,2},{6,4},{1,7},{3,1},{5,3},{7,5},{8,14},{10,8},{12,... | collective-permute-start | bytes 786440 | tf_op jit(solution)/shard_map/ppermute | solution.py:328
  28.7 5.3 %all-to-all-start.1 = ((bf16[16,2,32,256]{3,2,1,0:T(8,128)(2,1)}), bf16[16,2,32,256]{3,2,1,0:T(8,128)(2,1)S(1)}, u32[]{:S(2)}, u32[]{:S(2)}) async-start(bf16[16,2,32,256]{3,2,1,0:T(8,128)(2,1)} %pack.3), calls=%async_computation.1 | async-start | bytes 1048576 | tf_op jit(solution)/shard_map/all_to_all | solution.py:353
  34.0 0.1 collective-permute-start.8
  34.1 0.5 collective-permute-start.7
  34.7 1.2 %collective-permute-done.1 = bf16[8,2,32,256]{3,2,1,0:T(8,128)(2,1)S(1)} collective-permute-done((bf16[8,2,32,256]{3,2,1,0:T(8,128)(2,1)S(1)}, bf16[8,2,32,256]{3,2,1,0:T(8,128)(2,1)S(1)}, u32[]{:S(2)}, u32[]{:S(2)}) %collective-permute-start.1) | collective-permute-done | bytes 262176 | tf_op jit(solution)/shard_map/ppermute | solution.py:328
  35.9 0.0 collective-permute-start.14
  35.9 2.9 %collective-permute-done.3 = bf16[8,2,32,256]{3,2,1,0:T(8,128)(2,1)S(1)} collective-permute-done((bf16[8,2,32,256]{3,2,1,0:T(8,128)(2,1)S(1)}, bf16[8,2,32,256]{3,2,1,0:T(8,128)(2,1)S(1)}, u32[]{:S(2)}, u32[]{:S(2)}) %collective-permute-start.3) | collective-permute-done | bytes 262176 | tf_op jit(solution)/shard_map/ppermute | solution.py:328
  38.8 2.0 %collective-permute-start.4 = (bf16[8,2,32,256]{3,2,1,0:T(8,128)(2,1)S(1)}, bf16[8,2,32,256]{3,2,1,0:T(8,128)(2,1)S(1)}, u32[]{:S(2)}, u32[]{:S(2)}) collective-permute-start(bf16[8,2,32,256]{3,2,1,0:T(8,128)(2,1)S(1)} %collective-permute-done.3), channel_id=1, source_target_pairs={{0,2},{2,4},{4,6},{6,0},{1,3},{3,5},{5,7},{7,1},{8,10},{10,12},{12... | collective-permute-start | bytes 786440 | tf_op jit(solution)/shard_map/ppermute | solution.py:328
  40.8 3.3 %all-to-all-done.1.qg_in = bf16[16,2,32,256]{3,2,1,0:T(8,128)(2,1)S(1)} async-done(((bf16[16,2,32,256]{3,2,1,0:T(8,128)(2,1)}), bf16[16,2,32,256]{3,2,1,0:T(8,128)(2,1)S(1)}, u32[]{:S(2)}, u32[]{:S(2)}) %all-to-all-start.1) | async-done | bytes 524320 | tf_op jit(solution)/shard_map/all_to_all | solution.py:353
  44.1 0.1 collective-permute-start.9
  44.2 0.5 collective-permute-start.10
  44.7 0.1 collective-permute-start.13
  44.8 0.4 collective-permute-done.6
  45.2 0.1 collective-permute-start.12
  45.2 1.2 %collective-permute-done.4 = bf16[8,2,32,256]{3,2,1,0:T(8,128)(2,1)S(1)} collective-permute-done((bf16[8,2,32,256]{3,2,1,0:T(8,128)(2,1)S(1)}, bf16[8,2,32,256]{3,2,1,0:T(8,128)(2,1)S(1)}, u32[]{:S(2)}, u32[]{:S(2)}) %collective-permute-start.4) | collective-permute-done | bytes 262176 | tf_op jit(solution)/shard_map/ppermute | solution.py:328
  46.4 0.0 collective-permute-start.11
  46.5 0.3 collective-permute-done.12
  46.8 1.2 %collective-permute-done.11 = bf16[8,2,32,256]{3,2,1,0:T(8,128)(2,1)S(1)} collective-permute-done((bf16[8,2,32,256]{3,2,1,0:T(8,128)(2,1)S(1)}, bf16[8,2,32,256]{3,2,1,0:T(8,128)(2,1)S(1)}, u32[]{:S(2)}, u32[]{:S(2)}) %collective-permute-start.11) | collective-permute-done | bytes 262176 | tf_op jit(solution)/shard_map/ppermute | solution.py:332
  48.0 0.7 copy-done.22
  48.8 13.4 %attention.1 = (bf16[16,32,256]{2,1,0:T(8,128)(2,1)}, bf16[4,2,2,32,256]{4,3,2,1,0:T(8,128)(2,1)}, bf16[4,2,2,32,256]{4,3,2,1,0:T(8,128)(2,1)}, bf16[4,2,2,32,25...) custom-call(s32[16]{0:T(128)} %lengths.1, ...), custom_call_target="tpu_custom_call" | custom-call | tf_op jit(solution)/shard_map/attention/pallas_call | solution.py:275
  62.2 0.2 collective-permute-start.17
  62.4 0.4 collective-permute-start.22
  62.8 0.1 collective-permute-start.15
  63.0 0.4 collective-permute-start.19
  63.3 0.1 collective-permute-start.21
  63.5 0.6 collective-permute-done.17
  64.0 0.1 collective-permute-start.26
  64.2 1.1 fusion.7
  65.3 0.7 collective-permute-start.25
  66.0 0.1 fusion.3
  66.1 0.3 collective-permute-start.23
  66.5 0.5 copy-done.14
  66.9 0.1 fusion
  67.1 1.3 %collective-permute-start.27 = (bf16[8,2,32,256]{3,2,1,0:T(8,128)(2,1)S(1)}, bf16[8,2,32,256]{3,2,1,0:T(8,128)(2,1)S(1)}, u32[]{:S(2)}, u32[]{:S(2)}) collective-permute-start(bf16[8,2,32,256]{3,2,1,0:T(8,128)(2,1)S(1)} %fusion), channel_id=1, source_target_pairs={{0,2},{2,4},{4,6},{6,0},{1,3},{3,5},{5,7},{7,1},{8,10},{10,12},{12... | collective-permute-start | bytes 786440 | tf_op jit(solution)/shard_map/ppermute | solution.py:328
  68.4 0.1 fusion.6
  68.5 0.8 copy-done.29
  69.3 5.2 %collective-permute-done.23 = bf16[8,2,32,256]{3,2,1,0:T(8,128)(2,1)S(1)} collective-permute-done((bf16[8,2,32,256]{3,2,1,0:T(8,128)(2,1)S(1)}, bf16[8,2,32,256]{3,2,1,0:T(8,128)(2,1)S(1)}, u32[]{:S(2)}, u32[]{:S(2)}) %collective-permute-start.23) | collective-permute-done | bytes 262176 | tf_op jit(solution)/shard_map/ppermute | solution.py:328
  74.5 0.7 collective-permute-start.18
  75.3 0.1 fusion.5
  75.4 2.6 %collective-permute-start.20 = (bf16[8,2,32,256]{3,2,1,0:T(8,128)(2,1)S(1)}, bf16[8,2,32,256]{3,2,1,0:T(8,128)(2,1)S(1)}, u32[]{:S(2)}, u32[]{:S(2)}) collective-permute-start(bf16[8,2,32,256]{3,2,1,0:T(8,128)(2,1)S(1)} %fusion.6), channel_id=1, source_target_pairs={{0,6},{2,0},{4,2},{6,4},{1,7},{3,1},{5,3},{7,5},{8,14},{10,8},{12,... | collective-permute-start | bytes 786440 | tf_op jit(solution)/shard_map/ppermute | solution.py:328
  78.0 0.3 collective-permute-start.24
  78.3 0.1 fusion.2
  78.4 0.0 copy-start.4
  78.5 1.8 %collective-permute-start.28 = (bf16[8,2,32,256]{3,2,1,0:T(8,128)(2,1)S(1)}, bf16[8,2,32,256]{3,2,1,0:T(8,128)(2,1)S(1)}, u32[]{:S(2)}, u32[]{:S(2)}) collective-permute-start(bf16[8,2,32,256]{3,2,1,0:T(8,128)(2,1)S(1)} %fusion.2), channel_id=1, source_target_pairs={{0,2},{2,4},{4,6},{6,0},{1,3},{3,5},{5,7},{7,1},{8,10},{10,12},{12... | collective-permute-start | bytes 786440 | tf_op jit(solution)/shard_map/ppermute | solution.py:328
  80.3 4.7 %collective-permute-done.18.refs_5_ = bf16[8,2,32,256]{3,2,1,0:T(8,128)(2,1)S(1)} collective-permute-done((bf16[8,2,32,256]{3,2,1,0:T(8,128)(2,1)S(1)}, bf16[8,2,32,256]{3,2,1,0:T(8,128)(2,1)S(1)}, u32[]{:S(2)}, u32[]{:S(2)}) %collective-permute-start.18) | collective-permute-done | bytes 262176 | tf_op jit(solution)/shard_map/ppermute | solution.py:328
  85.0 3.4 %collective-permute-done.24.refs_7_ = bf16[8,2,32,256]{3,2,1,0:T(8,128)(2,1)S(1)} collective-permute-done((bf16[8,2,32,256]{3,2,1,0:T(8,128)(2,1)S(1)}, bf16[8,2,32,256]{3,2,1,0:T(8,128)(2,1)S(1)}, u32[]{:S(2)}, u32[]{:S(2)}) %collective-permute-start.24) | collective-permute-done | bytes 262176 | tf_op jit(solution)/shard_map/ppermute | solution.py:328
  88.4 0.5 collective-permute-done.28.refs_8_
  88.9 0.2 copy-done.24
  89.1 0.5 copy-done.25
  89.6 2.8 %final.1 = bf16[16,3,32,256]{3,2,1,0:T(8,128)(2,1)} custom-call(bf16[16,32,256]{2,1,0:T(8,128)(2,1)} %get-tuple-element.38.refs_0_, bf16[8,2,32,256]{3,2,1,0:T(8,128)(2,1)} %bitcast.55, bf16[8,2,32,256]{3,2,1,0:T(8,128)(2,1)} %bitcast.56, bf16[8,2,32,256]{3,2,1,0:T(8,128)(2,1)} %copy-done.4, bf16[8,2,32,256]{3,2,1,0:T(8,128)(2,1)} %copy-done.18, ...), custom_call_target="tpu_custom_call" | custom-call | tf_op jit(solution)/shard_map/final/pallas_call | solution.py:318
  92.3 18.7 %all_to_all.15.in_ref = bf16[16,3,32,256]{3,2,1,0:T(8,128)(2,1)} all-to-all(bf16[16,3,32,256]{3,2,1,0:T(8,128)(2,1)} %final.1), channel_id=1, replica_groups=mesh['x'=4,'y'=4,'z'=4,'core'=2] {'x','y'}, dimensions={0} | all-to-all | bytes 1572864 | tf_op jit(solution)/shard_map/all_to_all | solution.py:370
  111.0 2.0 %unpack.1 = (bf16[32,4096]{1,0:T(8,128)(2,1)}, bf16[32,4096]{1,0:T(8,128)(2,1)}, bf16[32,4096]{1,0:T(8,128)(2,1)}) custom-call(bf16[16,3,32,256]{3,2,1,0:T(8,128)(2,1)} %all_to_all.15.in_ref), custom_call_target="tpu_custom_call" | custom-call | tf_op jit(solution)/shard_map/unpack/pallas_call | solution.py:61
  (76 shorter events, 0.2 us)
Async XLA Ops:
  2.5 7.3 %copy-start.31 = (f32[2]{0:T(128)S(1)}, f32[2]{0:T(128)}, u32[]{:S(2)}) copy-start(f32[2]{0:T(128)} %param.10) | copy-start | bytes 28
  2.5 18.8 %all-to-all-start = ((bf16[16,2,32,256]{3,2,1,0:T(8,128)(2,1)}), bf16[16,2,32,256]{3,2,1,0:T(8,128)(2,1)S(1)}, u32[]{:S(2)}, u32[]{:S(2)}) async-start(bf16[16,2,32,256]{3,2,1,0:T(8,128)(2,1)} %pack.2), calls=%async_computation | async-start | bytes 1048576 | tf_op jit(solution)/shard_map/all_to_all | solution.py:344
  9.8 3.3 %collective-permute-start = (f32[2]{0:T(128)S(1)}, f32[2]{0:T(128)S(1)}, u32[]{:S(2)}, u32[]{:S(2)}) collective-permute-start(f32[2]{0:T(128)S(1)} %copy-done.31), channel_id=1, source_target_pairs={{0,0},{1,16},{2,32},{3,48},{4,64},{5,80},{6,96},{7,112},{8,1},{9,1... | collective-permute-start | bytes 32 | tf_op jit(solution)/shard_map/ppermute | solution.py:345
  13.1 8.2 %copy-start.28 = (f32[2]{0:T(128)}, f32[2]{0:T(128)S(1)}, u32[]{:S(2)}) copy-start(f32[2]{0:T(128)S(1)} %collective-permute-done.lams) | copy-start | bytes 28
  21.3 12.7 %copy-start.1 = (bf16[8,2,32,256]{3,2,1,0:T(8,128)(2,1)}, bf16[8,2,32,256]{3,2,1,0:T(8,128)(2,1)S(1)}, u32[]{:S(2)}) copy-start(bf16[8,2,32,256]{3,2,1,0:T(8,128)(2,1)S(1)} %get-tuple-element.32) | copy-start | bytes 786436
  21.3 12.8 %copy-start.2 = (bf16[8,2,32,256]{3,2,1,0:T(8,128)(2,1)}, bf16[8,2,32,256]{3,2,1,0:T(8,128)(2,1)S(1)}, u32[]{:S(2)}) copy-start(bf16[8,2,32,256]{3,2,1,0:T(8,128)(2,1)S(1)} %get-tuple-element.33) | copy-start | bytes 786436
  21.3 12.8 %collective-permute-start.5 = (bf16[8,2,32,256]{3,2,1,0:T(8,128)(2,1)S(1)}, bf16[8,2,32,256]{3,2,1,0:T(8,128)(2,1)S(1)}, u32[]{:S(2)}, u32[]{:S(2)}) collective-permute-start(bf16[8,2,32,256]{3,2,1,0:T(8,128)(2,1)S(1)} %get-tuple-element.32), channel_id=1, source_target_pairs={{0,6},{2,0},{4,2},{6,4},{1,7},{3,1},{5,3},{7,5},{8,14},{10,8},{12,... | collective-permute-start | bytes 786440 | tf_op jit(solution)/shard_map/ppermute | solution.py:328
  25.4 10.5 %collective-permute-start.1 = (bf16[8,2,32,256]{3,2,1,0:T(8,128)(2,1)S(1)}, bf16[8,2,32,256]{3,2,1,0:T(8,128)(2,1)S(1)}, u32[]{:S(2)}, u32[]{:S(2)}) collective-permute-start(bf16[8,2,32,256]{3,2,1,0:T(8,128)(2,1)S(1)} %get-tuple-element.32), channel_id=1, source_target_pairs={{0,2},{2,4},{4,6},{6,0},{1,3},{3,5},{5,7},{7,1},{8,10},{10,12},{12... | collective-permute-start | bytes 786440 | tf_op jit(solution)/shard_map/ppermute | solution.py:328
  25.4 13.3 %collective-permute-start.3 = (bf16[8,2,32,256]{3,2,1,0:T(8,128)(2,1)S(1)}, bf16[8,2,32,256]{3,2,1,0:T(8,128)(2,1)S(1)}, u32[]{:S(2)}, u32[]{:S(2)}) collective-permute-start(bf16[8,2,32,256]{3,2,1,0:T(8,128)(2,1)S(1)} %get-tuple-element.33), channel_id=1, source_target_pairs={{0,2},{2,4},{4,6},{6,0},{1,3},{3,5},{5,7},{7,1},{8,10},{10,12},{12... | collective-permute-start | bytes 786440 | tf_op jit(solution)/shard_map/ppermute | solution.py:328
  25.4 13.3 %collective-permute-start.2 = (bf16[8,2,32,256]{3,2,1,0:T(8,128)(2,1)S(1)}, bf16[8,2,32,256]{3,2,1,0:T(8,128)(2,1)S(1)}, u32[]{:S(2)}, u32[]{:S(2)}) collective-permute-start(bf16[8,2,32,256]{3,2,1,0:T(8,128)(2,1)S(1)} %get-tuple-element.33), channel_id=1, source_target_pairs={{0,6},{2,0},{4,2},{6,4},{1,7},{3,1},{5,3},{7,5},{8,14},{10,8},{12,... | collective-permute-start | bytes 786440 | tf_op jit(solution)/shard_map/ppermute | solution.py:328
  28.7 15.4 %all-to-all-start.1 = ((bf16[16,2,32,256]{3,2,1,0:T(8,128)(2,1)}), bf16[16,2,32,256]{3,2,1,0:T(8,128)(2,1)S(1)}, u32[]{:S(2)}, u32[]{:S(2)}) async-start(bf16[16,2,32,256]{3,2,1,0:T(8,128)(2,1)} %pack.3), calls=%async_computation.1 | async-start | bytes 1048576 | tf_op jit(solution)/shard_map/all_to_all | solution.py:353
  34.0 10.1 %collective-permute-start.8 = (bf16[8,2,32,256]{3,2,1,0:T(8,128)(2,1)S(1)}, bf16[8,2,32,256]{3,2,1,0:T(8,128)(2,1)S(1)}, u32[]{:S(2)}, u32[]{:S(2)}) collective-permute-start(bf16[8,2,32,256]{3,2,1,0:T(8,128)(2,1)S(1)} %get-tuple-element.32), channel_id=1, source_target_pairs={{0,1},{1,0},{2,3},{3,2},{4,5},{5,4},{6,7},{7,6},{8,9},{9,8},{10,11... | collective-permute-start | bytes 786440 | tf_op jit(solution)/shard_map/ppermute | solution.py:332
  34.1 14.6 %copy-start.3 = (bf16[8,2,32,256]{3,2,1,0:T(8,128)(2,1)}, bf16[8,2,32,256]{3,2,1,0:T(8,128)(2,1)S(1)}, u32[]{:S(2)}) copy-start(bf16[8,2,32,256]{3,2,1,0:T(8,128)(2,1)S(1)} %collective-permute-done.5) | copy-start | bytes 786436
  34.1 10.1 %collective-permute-start.7 = (bf16[8,2,32,256]{3,2,1,0:T(8,128)(2,1)S(1)}, bf16[8,2,32,256]{3,2,1,0:T(8,128)(2,1)S(1)}, u32[]{:S(2)}, u32[]{:S(2)}) collective-permute-start(bf16[8,2,32,256]{3,2,1,0:T(8,128)(2,1)S(1)} %get-tuple-element.33), channel_id=1, source_target_pairs={{0,1},{1,0},{2,3},{3,2},{4,5},{5,4},{6,7},{7,6},{8,9},{9,8},{10,11... | collective-permute-start | bytes 786440 | tf_op jit(solution)/shard_map/ppermute | solution.py:332
  35.9 12.8 %copy-start.5 = (bf16[8,2,32,256]{3,2,1,0:T(8,128)(2,1)}, bf16[8,2,32,256]{3,2,1,0:T(8,128)(2,1)S(1)}, u32[]{:S(2)}) copy-start(bf16[8,2,32,256]{3,2,1,0:T(8,128)(2,1)S(1)} %collective-permute-done.1) | copy-start | bytes 786436
  35.9 8.8 %collective-permute-start.14 = (bf16[8,2,32,256]{3,2,1,0:T(8,128)(2,1)S(1)}, bf16[8,2,32,256]{3,2,1,0:T(8,128)(2,1)S(1)}, u32[]{:S(2)}, u32[]{:S(2)}) collective-permute-start(bf16[8,2,32,256]{3,2,1,0:T(8,128)(2,1)S(1)} %collective-permute-done.5), channel_id=1, source_target_pairs={{0,1},{1,0},{2,3},{3,2},{4,5},{5,4},{6,7},{7,6},{8,9},{9,8},{10,11... | collective-permute-start | bytes 786440 | tf_op jit(solution)/shard_map/ppermute | solution.py:332
  38.8 9.9 %copy-start.6 = (bf16[8,2,32,256]{3,2,1,0:T(8,128)(2,1)}, bf16[8,2,32,256]{3,2,1,0:T(8,128)(2,1)S(1)}, u32[]{:S(2)}) copy-start(bf16[8,2,32,256]{3,2,1,0:T(8,128)(2,1)S(1)} %collective-permute-done.3) | copy-start | bytes 786436
  38.8 6.4 %collective-permute-start.6 = (bf16[8,2,32,256]{3,2,1,0:T(8,128)(2,1)S(1)}, bf16[8,2,32,256]{3,2,1,0:T(8,128)(2,1)S(1)}, u32[]{:S(2)}, u32[]{:S(2)}) collective-permute-start(bf16[8,2,32,256]{3,2,1,0:T(8,128)(2,1)S(1)} %collective-permute-done.5), channel_id=1, source_target_pairs={{0,6},{2,0},{4,2},{6,4},{1,7},{3,1},{5,3},{7,5},{8,14},{10,8},{12,... | collective-permute-start | bytes 786440 | tf_op jit(solution)/shard_map/ppermute | solution.py:328
  38.8 9.9 %copy-start.7 = (bf16[8,2,32,256]{3,2,1,0:T(8,128)(2,1)}, bf16[8,2,32,256]{3,2,1,0:T(8,128)(2,1)S(1)}, u32[]{:S(2)}) copy-start(bf16[8,2,32,256]{3,2,1,0:T(8,128)(2,1)S(1)} %collective-permute-done.2) | copy-start | bytes 786436
  38.8 7.7 %collective-permute-start.4 = (bf16[8,2,32,256]{3,2,1,0:T(8,128)(2,1)S(1)}, bf16[8,2,32,256]{3,2,1,0:T(8,128)(2,1)S(1)}, u32[]{:S(2)}, u32[]{:S(2)}) collective-permute-start(bf16[8,2,32,256]{3,2,1,0:T(8,128)(2,1)S(1)} %collective-permute-done.3), channel_id=1, source_target_pairs={{0,2},{2,4},{4,6},{6,0},{1,3},{3,5},{5,7},{7,1},{8,10},{10,12},{12... | collective-permute-start | bytes 786440 | tf_op jit(solution)/shard_map/ppermute | solution.py:328
  44.1 4.6 %copy-start = (bf16[16,2,32,256]{3,2,1,0:T(8,128)(2,1)}, bf16[16,2,32,256]{3,2,1,0:T(8,128)(2,1)S(1)}, u32[]{:S(2)}) copy-start(bf16[16,2,32,256]{3,2,1,0:T(8,128)(2,1)S(1)} %all-to-all-done.1.qg_in) | copy-start | bytes 1572868
  44.1 4.6 %copy-start.8 = (bf16[8,2,32,256]{3,2,1,0:T(8,128)(2,1)}, bf16[8,2,32,256]{3,2,1,0:T(8,128)(2,1)S(1)}, u32[]{:S(2)}) copy-start(bf16[8,2,32,256]{3,2,1,0:T(8,128)(2,1)S(1)} %collective-permute-done.8) | copy-start | bytes 786436
  44.1 2.4 %collective-permute-start.9 = (bf16[8,2,32,256]{3,2,1,0:T(8,128)(2,1)S(1)}, bf16[8,2,32,256]{3,2,1,0:T(8,128)(2,1)S(1)}, u32[]{:S(2)}, u32[]{:S(2)}) collective-permute-start(bf16[8,2,32,256]{3,2,1,0:T(8,128)(2,1)S(1)} %collective-permute-done.3), channel_id=1, source_target_pairs={{0,1},{1,0},{2,3},{3,2},{4,5},{5,4},{6,7},{7,6},{8,9},{9,8},{10,11... | collective-permute-start | bytes 786440 | tf_op jit(solution)/shard_map/ppermute | solution.py:332
  44.2 4.5 %copy-start.9 = (bf16[8,2,32,256]{3,2,1,0:T(8,128)(2,1)}, bf16[8,2,32,256]{3,2,1,0:T(8,128)(2,1)S(1)}, u32[]{:S(2)}) copy-start(bf16[8,2,32,256]{3,2,1,0:T(8,128)(2,1)S(1)} %collective-permute-done.7) | copy-start | bytes 786436
  44.2 2.3 %collective-permute-start.10 = (bf16[8,2,32,256]{3,2,1,0:T(8,128)(2,1)S(1)}, bf16[8,2,32,256]{3,2,1,0:T(8,128)(2,1)S(1)}, u32[]{:S(2)}, u32[]{:S(2)}) collective-permute-start(bf16[8,2,32,256]{3,2,1,0:T(8,128)(2,1)S(1)} %collective-permute-done.1), channel_id=1, source_target_pairs={{0,1},{1,0},{2,3},{3,2},{4,5},{5,4},{6,7},{7,6},{8,9},{9,8},{10,11... | collective-permute-start | bytes 786440 | tf_op jit(solution)/shard_map/ppermute | solution.py:332
  44.7 4.0 %copy-start.10 = (bf16[8,2,32,256]{3,2,1,0:T(8,128)(2,1)}, bf16[8,2,32,256]{3,2,1,0:T(8,128)(2,1)S(1)}, u32[]{:S(2)}) copy-start(bf16[8,2,32,256]{3,2,1,0:T(8,128)(2,1)S(1)} %collective-permute-done.14) | copy-start | bytes 786436
  44.7 1.8 %collective-permute-start.13 = (bf16[8,2,32,256]{3,2,1,0:T(8,128)(2,1)S(1)}, bf16[8,2,32,256]{3,2,1,0:T(8,128)(2,1)S(1)}, u32[]{:S(2)}, u32[]{:S(2)}) collective-permute-start(bf16[8,2,32,256]{3,2,1,0:T(8,128)(2,1)S(1)} %collective-permute-done.2), channel_id=1, source_target_pairs={{0,1},{1,0},{2,3},{3,2},{4,5},{5,4},{6,7},{7,6},{8,9},{9,8},{10,11... | collective-permute-start | bytes 786440 | tf_op jit(solution)/shard_map/ppermute | solution.py:332
  45.1 3.6 %copy-start.11 = (bf16[8,2,32,256]{3,2,1,0:T(8,128)(2,1)}, bf16[8,2,32,256]{3,2,1,0:T(8,128)(2,1)S(1)}, u32[]{:S(2)}) copy-start(bf16[8,2,32,256]{3,2,1,0:T(8,128)(2,1)S(1)} %collective-permute-done.6) | copy-start | bytes 786436
  45.2 1.7 %collective-permute-start.12 = (bf16[8,2,32,256]{3,2,1,0:T(8,128)(2,1)S(1)}, bf16[8,2,32,256]{3,2,1,0:T(8,128)(2,1)S(1)}, u32[]{:S(2)}, u32[]{:S(2)}) collective-permute-start(bf16[8,2,32,256]{3,2,1,0:T(8,128)(2,1)S(1)} %collective-permute-done.6), channel_id=1, source_target_pairs={{0,1},{1,0},{2,3},{3,2},{4,5},{5,4},{6,7},{7,6},{8,9},{9,8},{10,11... | collective-permute-start | bytes 786440 | tf_op jit(solution)/shard_map/ppermute | solution.py:332
  46.4 2.3 %copy-start.13 = (bf16[8,2,32,256]{3,2,1,0:T(8,128)(2,1)}, bf16[8,2,32,256]{3,2,1,0:T(8,128)(2,1)S(1)}, u32[]{:S(2)}) copy-start(bf16[8,2,32,256]{3,2,1,0:T(8,128)(2,1)S(1)} %collective-permute-done.4) | copy-start | bytes 786436
  46.4 1.5 %collective-permute-start.11 = (bf16[8,2,32,256]{3,2,1,0:T(8,128)(2,1)S(1)}, bf16[8,2,32,256]{3,2,1,0:T(8,128)(2,1)S(1)}, u32[]{:S(2)}, u32[]{:S(2)}) collective-permute-start(bf16[8,2,32,256]{3,2,1,0:T(8,128)(2,1)S(1)} %collective-permute-done.4), channel_id=1, source_target_pairs={{0,1},{1,0},{2,3},{3,2},{4,5},{5,4},{6,7},{7,6},{8,9},{9,8},{10,11... | collective-permute-start | bytes 786440 | tf_op jit(solution)/shard_map/ppermute | solution.py:332
  46.5 2.3 %copy-start.15 = (bf16[8,2,32,256]{3,2,1,0:T(8,128)(2,1)}, bf16[8,2,32,256]{3,2,1,0:T(8,128)(2,1)S(1)}, u32[]{:S(2)}) copy-start(bf16[8,2,32,256]{3,2,1,0:T(8,128)(2,1)S(1)} %collective-permute-done.9) | copy-start | bytes 786436
  46.5 2.3 %copy-start.17 = (bf16[8,2,32,256]{3,2,1,0:T(8,128)(2,1)}, bf16[8,2,32,256]{3,2,1,0:T(8,128)(2,1)S(1)}, u32[]{:S(2)}) copy-start(bf16[8,2,32,256]{3,2,1,0:T(8,128)(2,1)S(1)} %collective-permute-done.10) | copy-start | bytes 786436
  46.5 2.3 %copy-start.19 = (bf16[8,2,32,256]{3,2,1,0:T(8,128)(2,1)}, bf16[8,2,32,256]{3,2,1,0:T(8,128)(2,1)S(1)}, u32[]{:S(2)}) copy-start(bf16[8,2,32,256]{3,2,1,0:T(8,128)(2,1)S(1)} %collective-permute-done.13) | copy-start | bytes 786436
  46.8 2.0 %copy-start.21 = (bf16[8,2,32,256]{3,2,1,0:T(8,128)(2,1)}, bf16[8,2,32,256]{3,2,1,0:T(8,128)(2,1)S(1)}, u32[]{:S(2)}) copy-start(bf16[8,2,32,256]{3,2,1,0:T(8,128)(2,1)S(1)} %collective-permute-done.12) | copy-start | bytes 786436
  48.0 0.7 copy-start.22
  62.2 1.8 %collective-permute-start.17 = (bf16[8,2,32,256]{3,2,1,0:T(8,128)(2,1)}, bf16[8,2,32,256]{3,2,1,0:T(8,128)(2,1)S(1)}, u32[]{:S(2)}, u32[]{:S(2)}) collective-permute-start(bf16[8,2,32,256]{3,2,1,0:T(8,128)(2,1)} %bitcast.78), channel_id=1, source_target_pairs={{0,1},{1,0},{2,3},{3,2},{4,5},{5,4},{6,7},{7,6},{8,9},{9,8},{10,11... | collective-permute-start | bytes 786440 | tf_op jit(solution)/shard_map/ppermute | solution.py:332
  62.4 2.9 %collective-permute-start.22 = (bf16[8,2,32,256]{3,2,1,0:T(8,128)(2,1)}, bf16[8,2,32,256]{3,2,1,0:T(8,128)(2,1)S(1)}, u32[]{:S(2)}, u32[]{:S(2)}) collective-permute-start(bf16[8,2,32,256]{3,2,1,0:T(8,128)(2,1)} %bitcast.77), channel_id=1, source_target_pairs={{0,1},{1,0},{2,3},{3,2},{4,5},{5,4},{6,7},{7,6},{8,9},{9,8},{10,11... | collective-permute-start | bytes 786440 | tf_op jit(solution)/shard_map/ppermute | solution.py:332
  62.8 15.6 %collective-permute-start.15 = (bf16[8,2,32,256]{3,2,1,0:T(8,128)(2,1)}, bf16[8,2,32,256]{3,2,1,0:T(8,128)(2,1)S(1)}, u32[]{:S(2)}, u32[]{:S(2)}) collective-permute-start(bf16[8,2,32,256]{3,2,1,0:T(8,128)(2,1)} %bitcast.72), channel_id=1, source_target_pairs={{0,1},{1,0},{2,3},{3,2},{4,5},{5,4},{6,7},{7,6},{8,9},{9,8},{10,11... | collective-permute-start | bytes 786440 | tf_op jit(solution)/shard_map/ppermute | solution.py:332
  63.0 4.1 %collective-permute-start.19 = (bf16[8,2,32,256]{3,2,1,0:T(8,128)(2,1)}, bf16[8,2,32,256]{3,2,1,0:T(8,128)(2,1)S(1)}, u32[]{:S(2)}, u32[]{:S(2)}) collective-permute-start(bf16[8,2,32,256]{3,2,1,0:T(8,128)(2,1)} %bitcast.75), channel_id=1, source_target_pairs={{0,1},{1,0},{2,3},{3,2},{4,5},{5,4},{6,7},{7,6},{8,9},{9,8},{10,11... | collective-permute-start | bytes 786440 | tf_op jit(solution)/shard_map/ppermute | solution.py:332
  63.3 5.2 %collective-permute-start.21 = (bf16[8,2,32,256]{3,2,1,0:T(8,128)(2,1)}, bf16[8,2,32,256]{3,2,1,0:T(8,128)(2,1)S(1)}, u32[]{:S(2)}, u32[]{:S(2)}) collective-permute-start(bf16[8,2,32,256]{3,2,1,0:T(8,128)(2,1)} %bitcast.74), channel_id=1, source_target_pairs={{0,1},{1,0},{2,3},{3,2},{4,5},{5,4},{6,7},{7,6},{8,9},{9,8},{10,11... | collective-permute-start | bytes 786440 | tf_op jit(solution)/shard_map/ppermute | solution.py:332
  64.0 2.0 %collective-permute-start.26 = (bf16[8,2,32,256]{3,2,1,0:T(8,128)(2,1)}, bf16[8,2,32,256]{3,2,1,0:T(8,128)(2,1)S(1)}, u32[]{:S(2)}, u32[]{:S(2)}) collective-permute-start(bf16[8,2,32,256]{3,2,1,0:T(8,128)(2,1)} %bitcast.76), channel_id=1, source_target_pairs={{0,1},{1,0},{2,3},{3,2},{4,5},{5,4},{6,7},{7,6},{8,9},{9,8},{10,11... | collective-permute-start | bytes 786440 | tf_op jit(solution)/shard_map/ppermute | solution.py:332
  64.2 1.1 copy-start.30
  64.2 1.8 %copy-start.16 = (bf16[4,2,2,32,256]{4,3,2,1,0:T(8,128)(2,1)S(1)}, bf16[4,2,2,32,256]{4,3,2,1,0:T(8,128)(2,1)}, u32[]{:S(2)}) copy-start(bf16[4,2,2,32,256]{4,3,2,1,0:T(8,128)(2,1)} %get-tuple-element.49) | copy-start | bytes 786436
  65.3 10.1 %collective-permute-start.25 = (bf16[8,2,32,256]{3,2,1,0:T(8,128)(2,1)S(1)}, bf16[8,2,32,256]{3,2,1,0:T(8,128)(2,1)S(1)}, u32[]{:S(2)}, u32[]{:S(2)}) collective-permute-start(bf16[8,2,32,256]{3,2,1,0:T(8,128)(2,1)S(1)} %bitcast.73), channel_id=1, source_target_pairs={{0,1},{1,0},{2,3},{3,2},{4,5},{5,4},{6,7},{7,6},{8,9},{9,8},{10,11... | collective-permute-start | bytes 786440 | tf_op jit(solution)/shard_map/ppermute | solution.py:332
  66.0 1.0 copy-start.14
  66.1 8.4 %collective-permute-start.23 = (bf16[8,2,32,256]{3,2,1,0:T(8,128)(2,1)S(1)}, bf16[8,2,32,256]{3,2,1,0:T(8,128)(2,1)S(1)}, u32[]{:S(2)}, u32[]{:S(2)}) collective-permute-start(bf16[8,2,32,256]{3,2,1,0:T(8,128)(2,1)S(1)} %fusion.3), channel_id=1, source_target_pairs={{0,6},{2,0},{4,2},{6,4},{1,7},{3,1},{5,3},{7,5},{8,14},{10,8},{12,... | collective-permute-start | bytes 786440 | tf_op jit(solution)/shard_map/ppermute | solution.py:328
  66.9 1.5 %copy-start.12 = (bf16[4,2,2,32,256]{4,3,2,1,0:T(8,128)(2,1)S(1)}, bf16[4,2,2,32,256]{4,3,2,1,0:T(8,128)(2,1)}, u32[]{:S(2)}) copy-start(bf16[4,2,2,32,256]{4,3,2,1,0:T(8,128)(2,1)} %get-tuple-element.45) | copy-start | bytes 786436
  67.1 10.9 %collective-permute-start.27 = (bf16[8,2,32,256]{3,2,1,0:T(8,128)(2,1)S(1)}, bf16[8,2,32,256]{3,2,1,0:T(8,128)(2,1)S(1)}, u32[]{:S(2)}, u32[]{:S(2)}) collective-permute-start(bf16[8,2,32,256]{3,2,1,0:T(8,128)(2,1)S(1)} %fusion), channel_id=1, source_target_pairs={{0,2},{2,4},{4,6},{6,0},{1,3},{3,5},{5,7},{7,1},{8,10},{10,12},{12... | collective-permute-start | bytes 786440 | tf_op jit(solution)/shard_map/ppermute | solution.py:328
  68.4 1.0 copy-start.29
  68.4 6.9 %copy-start.27 = (bf16[4,2,2,32,256]{4,3,2,1,0:T(8,128)(2,1)S(1)}, bf16[4,2,2,32,256]{4,3,2,1,0:T(8,128)(2,1)}, u32[]{:S(2)}) copy-start(bf16[4,2,2,32,256]{4,3,2,1,0:T(8,128)(2,1)} %get-tuple-element.47) | copy-start | bytes 786436
  69.3 10.9 %collective-permute-start.16 = (bf16[8,2,32,256]{3,2,1,0:T(8,128)(2,1)S(1)}, bf16[8,2,32,256]{3,2,1,0:T(8,128)(2,1)S(1)}, u32[]{:S(2)}, u32[]{:S(2)}) collective-permute-start(bf16[8,2,32,256]{3,2,1,0:T(8,128)(2,1)S(1)} %bitcast.71), channel_id=1, source_target_pairs={{0,1},{1,0},{2,3},{3,2},{4,5},{5,4},{6,7},{7,6},{8,9},{9,8},{10,11... | collective-permute-start | bytes 786440 | tf_op jit(solution)/shard_map/ppermute | solution.py:332
  74.5 10.5 %collective-permute-start.18 = (bf16[8,2,32,256]{3,2,1,0:T(8,128)(2,1)S(1)}, bf16[8,2,32,256]{3,2,1,0:T(8,128)(2,1)S(1)}, u32[]{:S(2)}, u32[]{:S(2)}) collective-permute-start(bf16[8,2,32,256]{3,2,1,0:T(8,128)(2,1)S(1)} %fusion.7), channel_id=1, source_target_pairs={{0,2},{2,4},{4,6},{6,0},{1,3},{3,5},{5,7},{7,1},{8,10},{10,12},{12... | collective-permute-start | bytes 786440 | tf_op jit(solution)/shard_map/ppermute | solution.py:328
  75.3 3.0 %copy-start.26 = (bf16[4,2,2,32,256]{4,3,2,1,0:T(8,128)(2,1)S(1)}, bf16[4,2,2,32,256]{4,3,2,1,0:T(8,128)(2,1)}, u32[]{:S(2)}) copy-start(bf16[4,2,2,32,256]{4,3,2,1,0:T(8,128)(2,1)} %get-tuple-element.51) | copy-start | bytes 786436
  75.4 9.6 %collective-permute-start.20 = (bf16[8,2,32,256]{3,2,1,0:T(8,128)(2,1)S(1)}, bf16[8,2,32,256]{3,2,1,0:T(8,128)(2,1)S(1)}, u32[]{:S(2)}, u32[]{:S(2)}) collective-permute-start(bf16[8,2,32,256]{3,2,1,0:T(8,128)(2,1)S(1)} %fusion.6), channel_id=1, source_target_pairs={{0,6},{2,0},{4,2},{6,4},{1,7},{3,1},{5,3},{7,5},{8,14},{10,8},{12,... | collective-permute-start | bytes 786440 | tf_op jit(solution)/shard_map/ppermute | solution.py:328
  78.0 10.4 %collective-permute-start.24 = (bf16[8,2,32,256]{3,2,1,0:T(8,128)(2,1)S(1)}, bf16[8,2,32,256]{3,2,1,0:T(8,128)(2,1)S(1)}, u32[]{:S(2)}, u32[]{:S(2)}) collective-permute-start(bf16[8,2,32,256]{3,2,1,0:T(8,128)(2,1)S(1)} %fusion.5), channel_id=1, source_target_pairs={{0,6},{2,0},{4,2},{6,4},{1,7},{3,1},{5,3},{7,5},{8,14},{10,8},{12,... | collective-permute-start | bytes 786440 | tf_op jit(solution)/shard_map/ppermute | solution.py:328
  78.4 10.4 %copy-start.4 = (bf16[8,2,32,256]{3,2,1,0:T(8,128)(2,1)}, bf16[8,2,32,256]{3,2,1,0:T(8,128)(2,1)S(1)}, u32[]{:S(2)}) copy-start(bf16[8,2,32,256]{3,2,1,0:T(8,128)(2,1)S(1)} %collective-permute-done.15.refs_3_) | copy-start | bytes 786436
  78.5 10.4 %collective-permute-start.28 = (bf16[8,2,32,256]{3,2,1,0:T(8,128)(2,1)S(1)}, bf16[8,2,32,256]{3,2,1,0:T(8,128)(2,1)S(1)}, u32[]{:S(2)}, u32[]{:S(2)}) collective-permute-start(bf16[8,2,32,256]{3,2,1,0:T(8,128)(2,1)S(1)} %fusion.2), channel_id=1, source_target_pairs={{0,2},{2,4},{4,6},{6,0},{1,3},{3,5},{5,7},{7,1},{8,10},{10,12},{12... | collective-permute-start | bytes 786440 | tf_op jit(solution)/shard_map/ppermute | solution.py:328
  80.3 8.6 %copy-start.18 = (bf16[8,2,32,256]{3,2,1,0:T(8,128)(2,1)}, bf16[8,2,32,256]{3,2,1,0:T(8,128)(2,1)S(1)}, u32[]{:S(2)}) copy-start(bf16[8,2,32,256]{3,2,1,0:T(8,128)(2,1)S(1)} %collective-permute-done.16.refs_4_) | copy-start | bytes 786436
  85.0 3.9 %copy-start.20 = (bf16[8,2,32,256]{3,2,1,0:T(8,128)(2,1)}, bf16[8,2,32,256]{3,2,1,0:T(8,128)(2,1)S(1)}, u32[]{:S(2)}) copy-start(bf16[8,2,32,256]{3,2,1,0:T(8,128)(2,1)S(1)} %collective-permute-done.18.refs_5_) | copy-start | bytes 786436
  85.0 3.9 %copy-start.23 = (bf16[8,2,32,256]{3,2,1,0:T(8,128)(2,1)}, bf16[8,2,32,256]{3,2,1,0:T(8,128)(2,1)S(1)}, u32[]{:S(2)}) copy-start(bf16[8,2,32,256]{3,2,1,0:T(8,128)(2,1)S(1)} %collective-permute-done.20.refs_6_) | copy-start | bytes 786436
  88.4 0.7 copy-start.24
  88.9 0.7 copy-start.25

commit v5 on v4

--- a/solution.py
+++ b/solution.py
@@ -304,8 +304,8 @@
     return d_query, *[x.reshape(SLICES // 2, 2, STRIPE, WIDTH) for x in terms]
 
 
-def final_kernel(*refs):
-    d_query, *ins, out = refs
+def gather_kernel(d_query, *refs):
+    *ins, out = refs
     out[:, 0] = d_query[...]
     for half in range(2):
         total = ins[half][...].astype(jnp.float32)
@@ -314,14 +314,15 @@
         out[8 * half : 8 * half + 8, 1:] = total.astype(out.dtype)
 
 
-def final(d_query, *halves):
+def gradients(kernel, name, *args):
     return pl.pallas_call(
-        final_kernel,
+        kernel,
         out_shape=jax.ShapeDtypeStruct((SLICES, 3, STRIPE, WIDTH), jnp.bfloat16),
-        in_specs=[pl.BlockSpec(memory_space=pltpu.VMEM)] * (1 + len(halves)),
+        in_specs=[pl.BlockSpec(memory_space=pltpu.VMEM)] * len(args),
         out_specs=pl.BlockSpec(memory_space=pltpu.VMEM),
-        name="final",
-    )(d_query, *halves)
+        cost_estimate=pl.CostEstimate(flops=10**6, bytes_accessed=3 * 10**6, transcendentals=0),
+        name=name,
+    )(*args)
 
 
 def along_z(x, d):
@@ -366,7 +367,11 @@
     lower_3 = along_z(add(own[6], other[6]), 1)
     lower_1 = along_z(add(own[2], other[2], lower_far), -1)
     upper_3 = along_z(add(own[7], other[7], upper_far), 1)
-    total = final(d_query, own[0], own[1], other[0], other[1], lower_3, upper_1, lower_1, upper_3)
+    gathered = gradients(
+        gather_kernel, "gather", d_query, own[0], own[1], other[0], other[1], lower_3, upper_1
+    )
+    last = jnp.pad(jnp.concatenate([lower_1, upper_3], axis=0), ((0, 0), (1, 0), (0, 0), (0, 0)))
+    total = add(gathered, last)
     return unpack(lax.all_to_all(total, SECTION, 0, 0, tiled=True))
 
 

time: 114 us -> 111 us (0.974)
  waiting for transfers between devices: 33 us -> 31 us
  other arithmetic: 1.68 us -> 2.98 us
  local copies, waits for them, and re-layouts: 3.51 us -> 2.31 us
    ppermute x12, waiting for transfers between devices: 19.5 us -> 17.8 us  [along_z(): return lax.ppermute(x, 'z', [(i, (i + d) % 4) for i in range(4)])]
    convert_element_type x6 -> x7, other arithmetic: 1.68 us -> 2.98 us  [add(): return sum((x.astype(jnp.float32) for x in xs)).astype(jnp.bfloat16)]
    unnamed x64 -> x60, local copies, waits for them, and re-layouts: 2.79 us -> 1.59 us
  transfers between devices with their start and end apart: 31 -> 31, of which waited for: 13 -> 12; matrix products, arithmetic and copies ran while one was open for 2% -> 2% of each run, Pallas kernels for 2% -> 4%
where the time goes in v5:
time: 111 us; the launch traced here: 110 us
  starting transfers between devices  33 us (30%)
  waiting for transfers between devices  31 us (28%)
  Pallas kernels  21.8 us (20%)
  blocking collectives  18.1 us (16%)
  other arithmetic  2.98 us (3%)
  local copies, waits for them, and re-layouts  2.31 us (2%)
  between operations  1.15 us (1%)
    all_to_all x1, blocking collectives, shards(): return unpack(lax.all_to_all(total, SECTION, 0, 0, tiled=True))  18.1 us
    ppermute x12, waiting for transfers between devices, along_z(): return lax.ppermute(x, 'z', [(i, (i + d) % 4) for i in range(4)])  17.8 us
    ppermute x12, starting transfers between devices, along_z(): return lax.ppermute(x, 'z', [(i, (i + d) % 4) for i in range(4)])  16.9 us
    pallas_call x1, Pallas kernels, core(): pl.pallas_call(core_kernel, out_shape=(jax.ShapeDtypeStruct((SLICES, STRI...  13.4 us
    all_to_all x1, waiting for transfers between devices, shards(): kv = lax.all_to_all(pack(keys, values), SECTION, 0, 0, tiled=True)  8.19 us
    all_to_all x1, starting transfers between devices, shards(): kv = lax.all_to_all(pack(keys, values), SECTION, 0, 0, tiled=True)  7.12 us
    all_to_all x1, starting transfers between devices, shards(): qg = lax.all_to_all(qg, SECTION, 0, 0, tiled=True)  4.87 us
    pallas_call x2, Pallas kernels, pack(): pl.pallas_call(pack_kernel, out_shape=jax.ShapeDtypeStruct((SLICES, 2, ST...  3.76 us
  transfers between devices with their start and end apart: 31, of which 12 were waited for; matrix products, arithmetic and copies ran while one was open for 2% of the time, Pallas kernels for 4%

profile of v5, /device:TPU:0, one launch (start us, length us, event | category | flops | bytes accessed | tf_op | source)
XLA Modules:
  0.0 110.2 jit_solution(3495830818717770307)
XLA Ops:
  0.6 1.9 %pack.2 = bf16[16,2,32,256]{3,2,1,0:T(8,128)(2,1)} custom-call(bf16[32,4096]{1,0:T(8,128)(2,1)} %a_ref.2, bf16[32,4096]{1,0:T(8,128)(2,1)} %b_ref.2), custom_call_target="tpu_custom_call" | custom-call | tf_op jit(solution)/shard_map/pack/pallas_call | solution.py:44
  2.5 7.1 %all-to-all-start = ((bf16[16,2,32,256]{3,2,1,0:T(8,128)(2,1)}), bf16[16,2,32,256]{3,2,1,0:T(8,128)(2,1)S(1)}, u32[]{:S(2)}, u32[]{:S(2)}) async-start(bf16[16,2,32,256]{3,2,1,0:T(8,128)(2,1)} %pack.2), calls=%async_computation | async-start | bytes 1048576 | tf_op jit(solution)/shard_map/all_to_all | solution.py:345
  9.7 0.7 collective-permute-start
  10.4 1.9 %pack.3 = bf16[16,2,32,256]{3,2,1,0:T(8,128)(2,1)} custom-call(bf16[32,4096]{1,0:T(8,128)(2,1)} %a_ref.3, bf16[32,4096]{1,0:T(8,128)(2,1)} %b_ref.3), custom_call_target="tpu_custom_call" | custom-call | tf_op jit(solution)/shard_map/pack/pallas_call | solution.py:44
  12.3 0.7 stack.39.where
  13.0 8.2 %all-to-all-done = bf16[16,2,32,256]{3,2,1,0:T(8,128)(2,1)S(1)} async-done(((bf16[16,2,32,256]{3,2,1,0:T(8,128)(2,1)}), bf16[16,2,32,256]{3,2,1,0:T(8,128)(2,1)S(1)}, u32[]{:S(2)}, u32[]{:S(2)}) %all-to-all-start) | async-done | bytes 524320 | tf_op jit(solution)/shard_map/all_to_all | solution.py:345
  21.2 0.0 copy-start.1
  21.2 0.0 copy-start.2
  21.2 4.1 %collective-permute-start.5 = (bf16[8,2,32,256]{3,2,1,0:T(8,128)(2,1)S(1)}, bf16[8,2,32,256]{3,2,1,0:T(8,128)(2,1)S(1)}, u32[]{:S(2)}, u32[]{:S(2)}) collective-permute-start(bf16[8,2,32,256]{3,2,1,0:T(8,128)(2,1)S(1)} %get-tuple-element.32), channel_id=1, source_target_pairs={{0,6},{2,0},{4,2},{6,4},{1,7},{3,1},{5,3},{7,5},{8,14},{10,8},{12,... | collective-permute-start | bytes 786440 | tf_op jit(solution)/shard_map/ppermute | solution.py:329
  25.3 0.0 collective-permute-start.3
  25.3 3.3 %collective-permute-start.2 = (bf16[8,2,32,256]{3,2,1,0:T(8,128)(2,1)S(1)}, bf16[8,2,32,256]{3,2,1,0:T(8,128)(2,1)S(1)}, u32[]{:S(2)}, u32[]{:S(2)}) collective-permute-start(bf16[8,2,32,256]{3,2,1,0:T(8,128)(2,1)S(1)} %get-tuple-element.33), channel_id=1, source_target_pairs={{0,6},{2,0},{4,2},{6,4},{1,7},{3,1},{5,3},{7,5},{8,14},{10,8},{12,... | collective-permute-start | bytes 786440 | tf_op jit(solution)/shard_map/ppermute | solution.py:329
  28.6 4.9 %all-to-all-start.1 = ((bf16[16,2,32,256]{3,2,1,0:T(8,128)(2,1)}), bf16[16,2,32,256]{3,2,1,0:T(8,128)(2,1)S(1)}, u32[]{:S(2)}, u32[]{:S(2)}) async-start(bf16[16,2,32,256]{3,2,1,0:T(8,128)(2,1)} %pack.3), calls=%async_computation.1 | async-start | bytes 1048576 | tf_op jit(solution)/shard_map/all_to_all | solution.py:354
  33.5 0.1 collective-permute-start.8
  33.6 0.5 collective-permute-start.7
  34.1 1.7 %collective-permute-done.1 = bf16[8,2,32,256]{3,2,1,0:T(8,128)(2,1)S(1)} collective-permute-done((bf16[8,2,32,256]{3,2,1,0:T(8,128)(2,1)S(1)}, bf16[8,2,32,256]{3,2,1,0:T(8,128)(2,1)S(1)}, u32[]{:S(2)}, u32[]{:S(2)}) %collective-permute-start.1) | collective-permute-done | bytes 262176 | tf_op jit(solution)/shard_map/ppermute | solution.py:329
  35.8 2.9 %collective-permute-done.3 = bf16[8,2,32,256]{3,2,1,0:T(8,128)(2,1)S(1)} collective-permute-done((bf16[8,2,32,256]{3,2,1,0:T(8,128)(2,1)S(1)}, bf16[8,2,32,256]{3,2,1,0:T(8,128)(2,1)S(1)}, u32[]{:S(2)}, u32[]{:S(2)}) %collective-permute-start.3) | collective-permute-done | bytes 262176 | tf_op jit(solution)/shard_map/ppermute | solution.py:329
  38.7 0.0 collective-permute-start.6
  38.7 2.0 %collective-permute-start.4 = (bf16[8,2,32,256]{3,2,1,0:T(8,128)(2,1)S(1)}, bf16[8,2,32,256]{3,2,1,0:T(8,128)(2,1)S(1)}, u32[]{:S(2)}, u32[]{:S(2)}) collective-permute-start(bf16[8,2,32,256]{3,2,1,0:T(8,128)(2,1)S(1)} %collective-permute-done.3), channel_id=1, source_target_pairs={{0,2},{2,4},{4,6},{6,0},{1,3},{3,5},{5,7},{7,1},{8,10},{10,12},{12... | collective-permute-start | bytes 786440 | tf_op jit(solution)/shard_map/ppermute | solution.py:329
  40.7 2.9 %all-to-all-done.1.qg_in = bf16[16,2,32,256]{3,2,1,0:T(8,128)(2,1)S(1)} async-done(((bf16[16,2,32,256]{3,2,1,0:T(8,128)(2,1)}), bf16[16,2,32,256]{3,2,1,0:T(8,128)(2,1)S(1)}, u32[]{:S(2)}, u32[]{:S(2)}) %all-to-all-start.1) | async-done | bytes 524320 | tf_op jit(solution)/shard_map/all_to_all | solution.py:354
  43.6 0.1 collective-permute-start.9
  43.7 0.5 collective-permute-start.10
  44.2 0.1 collective-permute-start.13
  44.3 0.8 collective-permute-done.6
  45.0 1.3 %collective-permute-done.4 = bf16[8,2,32,256]{3,2,1,0:T(8,128)(2,1)S(1)} collective-permute-done((bf16[8,2,32,256]{3,2,1,0:T(8,128)(2,1)S(1)}, bf16[8,2,32,256]{3,2,1,0:T(8,128)(2,1)S(1)}, u32[]{:S(2)}, u32[]{:S(2)}) %collective-permute-start.4) | collective-permute-done | bytes 262176 | tf_op jit(solution)/shard_map/ppermute | solution.py:329
  46.3 0.0 collective-permute-start.11
  46.3 0.0 collective-permute-done.9
  46.4 0.0 collective-permute-done.10
  46.4 0.2 collective-permute-done.12
  46.6 1.3 %collective-permute-done.11 = bf16[8,2,32,256]{3,2,1,0:T(8,128)(2,1)S(1)} collective-permute-done((bf16[8,2,32,256]{3,2,1,0:T(8,128)(2,1)S(1)}, bf16[8,2,32,256]{3,2,1,0:T(8,128)(2,1)S(1)}, u32[]{:S(2)}, u32[]{:S(2)}) %collective-permute-start.11) | collective-permute-done | bytes 262176 | tf_op jit(solution)/shard_map/ppermute | solution.py:333
  47.9 0.7 copy-done.21
  48.7 13.4 %attention.1 = (bf16[16,32,256]{2,1,0:T(8,128)(2,1)}, bf16[4,2,2,32,256]{4,3,2,1,0:T(8,128)(2,1)}, bf16[4,2,2,32,256]{4,3,2,1,0:T(8,128)(2,1)}, bf16[4,2,2,32,25...) custom-call(s32[16]{0:T(128)} %lengths.1, ...), custom_call_target="tpu_custom_call" | custom-call | tf_op jit(solution)/shard_map/attention/pallas_call | solution.py:275
  62.2 0.2 collective-permute-start.17
  62.4 0.4 collective-permute-start.22
  62.8 0.1 collective-permute-start.15
  62.9 0.4 collective-permute-start.19
  63.3 0.1 collective-permute-start.21
  63.4 0.6 collective-permute-done.17
  64.0 0.1 collective-permute-start.26
  64.1 1.1 fusion.10
  65.2 0.7 collective-permute-start.25
  65.9 0.1 fusion.6
  66.0 0.0 collective-permute-done.26
  66.0 0.4 collective-permute-start.23
  66.4 0.1 fusion.3
  66.5 1.8 %collective-permute-start.27 = (bf16[8,2,32,256]{3,2,1,0:T(8,128)(2,1)S(1)}, bf16[8,2,32,256]{3,2,1,0:T(8,128)(2,1)S(1)}, u32[]{:S(2)}, u32[]{:S(2)}) collective-permute-start(bf16[8,2,32,256]{3,2,1,0:T(8,128)(2,1)S(1)} %fusion.3), channel_id=1, source_target_pairs={{0,2},{2,4},{4,6},{6,0},{1,3},{3,5},{5,7},{7,1},{8,10},{10,12},{12... | collective-permute-start | bytes 786440 | tf_op jit(solution)/shard_map/ppermute | solution.py:329
  68.3 0.1 fusion.9
  68.5 0.1 collective-permute-start.16
  68.6 5.9 %collective-permute-done.23 = bf16[8,2,32,256]{3,2,1,0:T(8,128)(2,1)S(1)} collective-permute-done((bf16[8,2,32,256]{3,2,1,0:T(8,128)(2,1)S(1)}, bf16[8,2,32,256]{3,2,1,0:T(8,128)(2,1)S(1)}, u32[]{:S(2)}, u32[]{:S(2)}) %collective-permute-start.23) | collective-permute-done | bytes 262176 | tf_op jit(solution)/shard_map/ppermute | solution.py:329
  74.5 0.7 collective-permute-start.18
  75.2 0.1 fusion.8
  75.3 2.6 %collective-permute-start.20 = (bf16[8,2,32,256]{3,2,1,0:T(8,128)(2,1)S(1)}, bf16[8,2,32,256]{3,2,1,0:T(8,128)(2,1)S(1)}, u32[]{:S(2)}, u32[]{:S(2)}) collective-permute-start(bf16[8,2,32,256]{3,2,1,0:T(8,128)(2,1)S(1)} %fusion.9), channel_id=1, source_target_pairs={{0,6},{2,0},{4,2},{6,4},{1,7},{3,1},{5,3},{7,5},{8,14},{10,8},{12,... | collective-permute-start | bytes 786440 | tf_op jit(solution)/shard_map/ppermute | solution.py:329
  77.9 0.3 collective-permute-start.24
  78.2 0.1 fusion.5
  78.4 0.0 copy-start.7
  78.4 1.8 %collective-permute-start.28 = (bf16[8,2,32,256]{3,2,1,0:T(8,128)(2,1)S(1)}, bf16[8,2,32,256]{3,2,1,0:T(8,128)(2,1)S(1)}, u32[]{:S(2)}, u32[]{:S(2)}) collective-permute-start(bf16[8,2,32,256]{3,2,1,0:T(8,128)(2,1)S(1)} %fusion.5), channel_id=1, source_target_pairs={{0,2},{2,4},{4,6},{6,0},{1,3},{3,5},{5,7},{7,1},{8,10},{10,12},{12... | collective-permute-start | bytes 786440 | tf_op jit(solution)/shard_map/ppermute | solution.py:329
  80.2 4.7 %collective-permute-done.18.refs_4_ = bf16[8,2,32,256]{3,2,1,0:T(8,128)(2,1)S(1)} collective-permute-done((bf16[8,2,32,256]{3,2,1,0:T(8,128)(2,1)S(1)}, bf16[8,2,32,256]{3,2,1,0:T(8,128)(2,1)S(1)}, u32[]{:S(2)}, u32[]{:S(2)}) %collective-permute-start.18) | collective-permute-done | bytes 262176 | tf_op jit(solution)/shard_map/ppermute | solution.py:329
  84.9 0.7 copy-done.22
  85.6 0.1 copy-done.23
  85.7 2.5 %gather.1 = bf16[16,3,32,256]{3,2,1,0:T(8,128)(2,1)} custom-call(bf16[16,32,256]{2,1,0:T(8,128)(2,1)} %get-tuple-element.38.d_query, bf16[8,2,32,256]{3,2,1,0:T(8,128)(2,1)} %bitcast.55, bf16[8,2,32,256]{3,2,1,0:T(8,128)(2,1)} %bitcast.56, bf16[8,2,32,256]{3,2,1,0:T(8,128)(2,1)} %copy-done.7, bf16[8,2,32,256]{3,2,1,0:T(8,128)(2,1)} %copy-done.19, ...), custom_call_target="tpu_custom_call" | custom-call | flops 1000000 | bytes 3000000 | tf_op jit(solution)/shard_map/gather/pallas_call | solution.py:318
  88.3 0.0 collective-permute-done.24
  88.3 0.5 collective-permute-done.28
  88.8 1.3 %add_convert_fusion = bf16[16,3,32,256]{3,2,1,0:T(8,128)(2,1)S(1)} fusion(bf16[16,3,32,256]{3,2,1,0:T(8,128)(2,1)} %gather.1, bf16[8,2,32,256]{3,2,1,0:T(8,128)(2,1)S(1)} %collective-permute-done.28, bf16[8,2,32,256]{3,2,1,0:T(8,128)(2,1)S(1)} %collective-permute-done.24), kind=kLoop, calls=%fused_computation.3 | loop fusion | flops 3932160 | bytes 2097152 | tf_op jit(solution)/shard_map/convert_element_type | solution.py:361
  90.1 18.1 %all_to_all.15.in_ref = bf16[16,3,32,256]{3,2,1,0:T(8,128)(2,1)} all-to-all(bf16[16,3,32,256]{3,2,1,0:T(8,128)(2,1)S(1)} %add_convert_fusion), channel_id=1, replica_groups=mesh['x'=4,'y'=4,'z'=4,'core'=2] {'x','y'}, dimensions={0} | all-to-all | bytes 1572864 | tf_op jit(solution)/shard_map/all_to_all | solution.py:375
  108.2 2.0 %unpack.1 = (bf16[32,4096]{1,0:T(8,128)(2,1)}, bf16[32,4096]{1,0:T(8,128)(2,1)}, bf16[32,4096]{1,0:T(8,128)(2,1)}) custom-call(bf16[16,3,32,256]{3,2,1,0:T(8,128)(2,1)} %all_to_all.15.in_ref), custom_call_target="tpu_custom_call" | custom-call | tf_op jit(solution)/shard_map/unpack/pallas_call | solution.py:61
  (73 shorter events, 0.2 us)
Async XLA Ops:
  0.6 9.0 %copy-start.29 = (f32[2]{0:T(128)S(1)}, f32[2]{0:T(128)}, u32[]{:S(2)}) copy-start(f32[2]{0:T(128)} %param.10) | copy-start | bytes 28
  2.5 18.6 %all-to-all-start = ((bf16[16,2,32,256]{3,2,1,0:T(8,128)(2,1)}), bf16[16,2,32,256]{3,2,1,0:T(8,128)(2,1)S(1)}, u32[]{:S(2)}, u32[]{:S(2)}) async-start(bf16[16,2,32,256]{3,2,1,0:T(8,128)(2,1)} %pack.2), calls=%async_computation | async-start | bytes 1048576 | tf_op jit(solution)/shard_map/all_to_all | solution.py:345
  9.7 3.3 %collective-permute-start = (f32[2]{0:T(128)S(1)}, f32[2]{0:T(128)S(1)}, u32[]{:S(2)}, u32[]{:S(2)}) collective-permute-start(f32[2]{0:T(128)S(1)} %copy-done.29), channel_id=1, source_target_pairs={{0,0},{1,16},{2,32},{3,48},{4,64},{5,80},{6,96},{7,112},{8,1},{9,1... | collective-permute-start | bytes 32 | tf_op jit(solution)/shard_map/ppermute | solution.py:346
  13.0 15.6 %copy-start.26 = (f32[2]{0:T(128)}, f32[2]{0:T(128)S(1)}, u32[]{:S(2)}) copy-start(f32[2]{0:T(128)S(1)} %collective-permute-done.lams) | copy-start | bytes 28
  21.2 27.4 %copy-start.1 = (bf16[8,2,32,256]{3,2,1,0:T(8,128)(2,1)}, bf16[8,2,32,256]{3,2,1,0:T(8,128)(2,1)S(1)}, u32[]{:S(2)}) copy-start(bf16[8,2,32,256]{3,2,1,0:T(8,128)(2,1)S(1)} %get-tuple-element.32) | copy-start | bytes 786436
  21.2 27.4 %copy-start.2 = (bf16[8,2,32,256]{3,2,1,0:T(8,128)(2,1)}, bf16[8,2,32,256]{3,2,1,0:T(8,128)(2,1)S(1)}, u32[]{:S(2)}) copy-start(bf16[8,2,32,256]{3,2,1,0:T(8,128)(2,1)S(1)} %get-tuple-element.33) | copy-start | bytes 786436
  21.2 12.3 %collective-permute-start.5 = (bf16[8,2,32,256]{3,2,1,0:T(8,128)(2,1)S(1)}, bf16[8,2,32,256]{3,2,1,0:T(8,128)(2,1)S(1)}, u32[]{:S(2)}, u32[]{:S(2)}) collective-permute-start(bf16[8,2,32,256]{3,2,1,0:T(8,128)(2,1)S(1)} %get-tuple-element.32), channel_id=1, source_target_pairs={{0,6},{2,0},{4,2},{6,4},{1,7},{3,1},{5,3},{7,5},{8,14},{10,8},{12,... | collective-permute-start | bytes 786440 | tf_op jit(solution)/shard_map/ppermute | solution.py:329
  25.3 10.5 %collective-permute-start.1 = (bf16[8,2,32,256]{3,2,1,0:T(8,128)(2,1)S(1)}, bf16[8,2,32,256]{3,2,1,0:T(8,128)(2,1)S(1)}, u32[]{:S(2)}, u32[]{:S(2)}) collective-permute-start(bf16[8,2,32,256]{3,2,1,0:T(8,128)(2,1)S(1)} %get-tuple-element.32), channel_id=1, source_target_pairs={{0,2},{2,4},{4,6},{6,0},{1,3},{3,5},{5,7},{7,1},{8,10},{10,12},{12... | collective-permute-start | bytes 786440 | tf_op jit(solution)/shard_map/ppermute | solution.py:329
  25.3 13.3 %collective-permute-start.3 = (bf16[8,2,32,256]{3,2,1,0:T(8,128)(2,1)S(1)}, bf16[8,2,32,256]{3,2,1,0:T(8,128)(2,1)S(1)}, u32[]{:S(2)}, u32[]{:S(2)}) collective-permute-start(bf16[8,2,32,256]{3,2,1,0:T(8,128)(2,1)S(1)} %get-tuple-element.33), channel_id=1, source_target_pairs={{0,2},{2,4},{4,6},{6,0},{1,3},{3,5},{5,7},{7,1},{8,10},{10,12},{12... | collective-permute-start | bytes 786440 | tf_op jit(solution)/shard_map/ppermute | solution.py:329
  25.3 13.3 %collective-permute-start.2 = (bf16[8,2,32,256]{3,2,1,0:T(8,128)(2,1)S(1)}, bf16[8,2,32,256]{3,2,1,0:T(8,128)(2,1)S(1)}, u32[]{:S(2)}, u32[]{:S(2)}) collective-permute-start(bf16[8,2,32,256]{3,2,1,0:T(8,128)(2,1)S(1)} %get-tuple-element.33), channel_id=1, source_target_pairs={{0,6},{2,0},{4,2},{6,4},{1,7},{3,1},{5,3},{7,5},{8,14},{10,8},{12,... | collective-permute-start | bytes 786440 | tf_op jit(solution)/shard_map/ppermute | solution.py:329
  28.6 15.0 %all-to-all-start.1 = ((bf16[16,2,32,256]{3,2,1,0:T(8,128)(2,1)}), bf16[16,2,32,256]{3,2,1,0:T(8,128)(2,1)S(1)}, u32[]{:S(2)}, u32[]{:S(2)}) async-start(bf16[16,2,32,256]{3,2,1,0:T(8,128)(2,1)} %pack.3), calls=%async_computation.1 | async-start | bytes 1048576 | tf_op jit(solution)/shard_map/all_to_all | solution.py:354
  33.5 10.1 %collective-permute-start.8 = (bf16[8,2,32,256]{3,2,1,0:T(8,128)(2,1)S(1)}, bf16[8,2,32,256]{3,2,1,0:T(8,128)(2,1)S(1)}, u32[]{:S(2)}, u32[]{:S(2)}) collective-permute-start(bf16[8,2,32,256]{3,2,1,0:T(8,128)(2,1)S(1)} %get-tuple-element.32), channel_id=1, source_target_pairs={{0,1},{1,0},{2,3},{3,2},{4,5},{5,4},{6,7},{7,6},{8,9},{9,8},{10,11... | collective-permute-start | bytes 786440 | tf_op jit(solution)/shard_map/ppermute | solution.py:333
  33.6 15.0 %copy-start.3 = (bf16[8,2,32,256]{3,2,1,0:T(8,128)(2,1)}, bf16[8,2,32,256]{3,2,1,0:T(8,128)(2,1)S(1)}, u32[]{:S(2)}) copy-start(bf16[8,2,32,256]{3,2,1,0:T(8,128)(2,1)S(1)} %collective-permute-done.5) | copy-start | bytes 786436
  33.6 10.1 %collective-permute-start.7 = (bf16[8,2,32,256]{3,2,1,0:T(8,128)(2,1)S(1)}, bf16[8,2,32,256]{3,2,1,0:T(8,128)(2,1)S(1)}, u32[]{:S(2)}, u32[]{:S(2)}) collective-permute-start(bf16[8,2,32,256]{3,2,1,0:T(8,128)(2,1)S(1)} %get-tuple-element.33), channel_id=1, source_target_pairs={{0,1},{1,0},{2,3},{3,2},{4,5},{5,4},{6,7},{7,6},{8,9},{9,8},{10,11... | collective-permute-start | bytes 786440 | tf_op jit(solution)/shard_map/ppermute | solution.py:333
  35.8 12.8 %copy-start.4 = (bf16[8,2,32,256]{3,2,1,0:T(8,128)(2,1)}, bf16[8,2,32,256]{3,2,1,0:T(8,128)(2,1)S(1)}, u32[]{:S(2)}) copy-start(bf16[8,2,32,256]{3,2,1,0:T(8,128)(2,1)S(1)} %collective-permute-done.1) | copy-start | bytes 786436
  35.8 8.4 %collective-permute-start.14 = (bf16[8,2,32,256]{3,2,1,0:T(8,128)(2,1)S(1)}, bf16[8,2,32,256]{3,2,1,0:T(8,128)(2,1)S(1)}, u32[]{:S(2)}, u32[]{:S(2)}) collective-permute-start(bf16[8,2,32,256]{3,2,1,0:T(8,128)(2,1)S(1)} %collective-permute-done.5), channel_id=1, source_target_pairs={{0,1},{1,0},{2,3},{3,2},{4,5},{5,4},{6,7},{7,6},{8,9},{9,8},{10,11... | collective-permute-start | bytes 786440 | tf_op jit(solution)/shard_map/ppermute | solution.py:333
  38.7 9.9 %copy-start.5 = (bf16[8,2,32,256]{3,2,1,0:T(8,128)(2,1)}, bf16[8,2,32,256]{3,2,1,0:T(8,128)(2,1)S(1)}, u32[]{:S(2)}) copy-start(bf16[8,2,32,256]{3,2,1,0:T(8,128)(2,1)S(1)} %collective-permute-done.3) | copy-start | bytes 786436
  38.7 6.4 %collective-permute-start.6 = (bf16[8,2,32,256]{3,2,1,0:T(8,128)(2,1)S(1)}, bf16[8,2,32,256]{3,2,1,0:T(8,128)(2,1)S(1)}, u32[]{:S(2)}, u32[]{:S(2)}) collective-permute-start(bf16[8,2,32,256]{3,2,1,0:T(8,128)(2,1)S(1)} %collective-permute-done.5), channel_id=1, source_target_pairs={{0,6},{2,0},{4,2},{6,4},{1,7},{3,1},{5,3},{7,5},{8,14},{10,8},{12,... | collective-permute-start | bytes 786440 | tf_op jit(solution)/shard_map/ppermute | solution.py:329
  38.7 9.9 %copy-start.6 = (bf16[8,2,32,256]{3,2,1,0:T(8,128)(2,1)}, bf16[8,2,32,256]{3,2,1,0:T(8,128)(2,1)S(1)}, u32[]{:S(2)}) copy-start(bf16[8,2,32,256]{3,2,1,0:T(8,128)(2,1)S(1)} %collective-permute-done.2) | copy-start | bytes 786436
  38.7 7.7 %collective-permute-start.4 = (bf16[8,2,32,256]{3,2,1,0:T(8,128)(2,1)S(1)}, bf16[8,2,32,256]{3,2,1,0:T(8,128)(2,1)S(1)}, u32[]{:S(2)}, u32[]{:S(2)}) collective-permute-start(bf16[8,2,32,256]{3,2,1,0:T(8,128)(2,1)S(1)} %collective-permute-done.3), channel_id=1, source_target_pairs={{0,2},{2,4},{4,6},{6,0},{1,3},{3,5},{5,7},{7,1},{8,10},{10,12},{12... | collective-permute-start | bytes 786440 | tf_op jit(solution)/shard_map/ppermute | solution.py:329
  43.6 5.1 %copy-start = (bf16[16,2,32,256]{3,2,1,0:T(8,128)(2,1)}, bf16[16,2,32,256]{3,2,1,0:T(8,128)(2,1)S(1)}, u32[]{:S(2)}) copy-start(bf16[16,2,32,256]{3,2,1,0:T(8,128)(2,1)S(1)} %all-to-all-done.1.qg_in) | copy-start | bytes 1572868
  43.6 5.1 %copy-start.8 = (bf16[8,2,32,256]{3,2,1,0:T(8,128)(2,1)}, bf16[8,2,32,256]{3,2,1,0:T(8,128)(2,1)S(1)}, u32[]{:S(2)}) copy-start(bf16[8,2,32,256]{3,2,1,0:T(8,128)(2,1)S(1)} %collective-permute-done.8) | copy-start | bytes 786436
  43.6 2.8 %collective-permute-start.9 = (bf16[8,2,32,256]{3,2,1,0:T(8,128)(2,1)S(1)}, bf16[8,2,32,256]{3,2,1,0:T(8,128)(2,1)S(1)}, u32[]{:S(2)}, u32[]{:S(2)}) collective-permute-start(bf16[8,2,32,256]{3,2,1,0:T(8,128)(2,1)S(1)} %collective-permute-done.3), channel_id=1, source_target_pairs={{0,1},{1,0},{2,3},{3,2},{4,5},{5,4},{6,7},{7,6},{8,9},{9,8},{10,11... | collective-permute-start | bytes 786440 | tf_op jit(solution)/shard_map/ppermute | solution.py:333
  43.7 5.0 %copy-start.9 = (bf16[8,2,32,256]{3,2,1,0:T(8,128)(2,1)}, bf16[8,2,32,256]{3,2,1,0:T(8,128)(2,1)S(1)}, u32[]{:S(2)}) copy-start(bf16[8,2,32,256]{3,2,1,0:T(8,128)(2,1)S(1)} %collective-permute-done.7) | copy-start | bytes 786436
  43.7 2.7 %collective-permute-start.10 = (bf16[8,2,32,256]{3,2,1,0:T(8,128)(2,1)S(1)}, bf16[8,2,32,256]{3,2,1,0:T(8,128)(2,1)S(1)}, u32[]{:S(2)}, u32[]{:S(2)}) collective-permute-start(bf16[8,2,32,256]{3,2,1,0:T(8,128)(2,1)S(1)} %collective-permute-done.1), channel_id=1, source_target_pairs={{0,1},{1,0},{2,3},{3,2},{4,5},{5,4},{6,7},{7,6},{8,9},{9,8},{10,11... | collective-permute-start | bytes 786440 | tf_op jit(solution)/shard_map/ppermute | solution.py:333
  44.2 4.5 %copy-start.10 = (bf16[8,2,32,256]{3,2,1,0:T(8,128)(2,1)}, bf16[8,2,32,256]{3,2,1,0:T(8,128)(2,1)S(1)}, u32[]{:S(2)}) copy-start(bf16[8,2,32,256]{3,2,1,0:T(8,128)(2,1)S(1)} %collective-permute-done.14) | copy-start | bytes 786436
  44.2 2.2 %collective-permute-start.13 = (bf16[8,2,32,256]{3,2,1,0:T(8,128)(2,1)S(1)}, bf16[8,2,32,256]{3,2,1,0:T(8,128)(2,1)S(1)}, u32[]{:S(2)}, u32[]{:S(2)}) collective-permute-start(bf16[8,2,32,256]{3,2,1,0:T(8,128)(2,1)S(1)} %collective-permute-done.2), channel_id=1, source_target_pairs={{0,1},{1,0},{2,3},{3,2},{4,5},{5,4},{6,7},{7,6},{8,9},{9,8},{10,11... | collective-permute-start | bytes 786440 | tf_op jit(solution)/shard_map/ppermute | solution.py:333
  45.0 3.6 %copy-start.11 = (bf16[8,2,32,256]{3,2,1,0:T(8,128)(2,1)}, bf16[8,2,32,256]{3,2,1,0:T(8,128)(2,1)S(1)}, u32[]{:S(2)}) copy-start(bf16[8,2,32,256]{3,2,1,0:T(8,128)(2,1)S(1)} %collective-permute-done.6) | copy-start | bytes 786436
  45.0 1.5 %collective-permute-start.12 = (bf16[8,2,32,256]{3,2,1,0:T(8,128)(2,1)S(1)}, bf16[8,2,32,256]{3,2,1,0:T(8,128)(2,1)S(1)}, u32[]{:S(2)}, u32[]{:S(2)}) collective-permute-start(bf16[8,2,32,256]{3,2,1,0:T(8,128)(2,1)S(1)} %collective-permute-done.6), channel_id=1, source_target_pairs={{0,1},{1,0},{2,3},{3,2},{4,5},{5,4},{6,7},{7,6},{8,9},{9,8},{10,11... | collective-permute-start | bytes 786440 | tf_op jit(solution)/shard_map/ppermute | solution.py:333
  46.3 2.3 %copy-start.13 = (bf16[8,2,32,256]{3,2,1,0:T(8,128)(2,1)}, bf16[8,2,32,256]{3,2,1,0:T(8,128)(2,1)S(1)}, u32[]{:S(2)}) copy-start(bf16[8,2,32,256]{3,2,1,0:T(8,128)(2,1)S(1)} %collective-permute-done.4) | copy-start | bytes 786436
  46.3 1.5 %collective-permute-start.11 = (bf16[8,2,32,256]{3,2,1,0:T(8,128)(2,1)S(1)}, bf16[8,2,32,256]{3,2,1,0:T(8,128)(2,1)S(1)}, u32[]{:S(2)}, u32[]{:S(2)}) collective-permute-start(bf16[8,2,32,256]{3,2,1,0:T(8,128)(2,1)S(1)} %collective-permute-done.4), channel_id=1, source_target_pairs={{0,1},{1,0},{2,3},{3,2},{4,5},{5,4},{6,7},{7,6},{8,9},{9,8},{10,11... | collective-permute-start | bytes 786440 | tf_op jit(solution)/shard_map/ppermute | solution.py:333
  46.3 2.3 %copy-start.15 = (bf16[8,2,32,256]{3,2,1,0:T(8,128)(2,1)}, bf16[8,2,32,256]{3,2,1,0:T(8,128)(2,1)S(1)}, u32[]{:S(2)}) copy-start(bf16[8,2,32,256]{3,2,1,0:T(8,128)(2,1)S(1)} %collective-permute-done.9) | copy-start | bytes 786436
  46.4 2.3 %copy-start.17 = (bf16[8,2,32,256]{3,2,1,0:T(8,128)(2,1)}, bf16[8,2,32,256]{3,2,1,0:T(8,128)(2,1)S(1)}, u32[]{:S(2)}) copy-start(bf16[8,2,32,256]{3,2,1,0:T(8,128)(2,1)S(1)} %collective-permute-done.10) | copy-start | bytes 786436
  46.4 1.5 %copy-start.18 = (bf16[8,2,32,256]{3,2,1,0:T(8,128)(2,1)}, bf16[8,2,32,256]{3,2,1,0:T(8,128)(2,1)S(1)}, u32[]{:S(2)}) copy-start(bf16[8,2,32,256]{3,2,1,0:T(8,128)(2,1)S(1)} %collective-permute-done.13) | copy-start | bytes 786436
  46.6 1.3 %copy-start.20 = (bf16[8,2,32,256]{3,2,1,0:T(8,128)(2,1)}, bf16[8,2,32,256]{3,2,1,0:T(8,128)(2,1)S(1)}, u32[]{:S(2)}) copy-start(bf16[8,2,32,256]{3,2,1,0:T(8,128)(2,1)S(1)} %collective-permute-done.12) | copy-start | bytes 786436
  47.9 0.7 copy-start.21
  62.2 3.1 %copy-start.28 = (bf16[4,2,2,32,256]{4,3,2,1,0:T(8,128)(2,1)S(1)}, bf16[4,2,2,32,256]{4,3,2,1,0:T(8,128)(2,1)}, u32[]{:S(2)}) copy-start(bf16[4,2,2,32,256]{4,3,2,1,0:T(8,128)(2,1)} %get-tuple-element.52) | copy-start | bytes 786436
  62.2 3.8 %copy-start.16 = (bf16[4,2,2,32,256]{4,3,2,1,0:T(8,128)(2,1)S(1)}, bf16[4,2,2,32,256]{4,3,2,1,0:T(8,128)(2,1)}, u32[]{:S(2)}) copy-start(bf16[4,2,2,32,256]{4,3,2,1,0:T(8,128)(2,1)} %get-tuple-element.49) | copy-start | bytes 786436
  62.2 1.8 %collective-permute-start.17 = (bf16[8,2,32,256]{3,2,1,0:T(8,128)(2,1)}, bf16[8,2,32,256]{3,2,1,0:T(8,128)(2,1)S(1)}, u32[]{:S(2)}, u32[]{:S(2)}) collective-permute-start(bf16[8,2,32,256]{3,2,1,0:T(8,128)(2,1)} %bitcast.78), channel_id=1, source_target_pairs={{0,1},{1,0},{2,3},{3,2},{4,5},{5,4},{6,7},{7,6},{8,9},{9,8},{10,11... | collective-permute-start | bytes 786440 | tf_op jit(solution)/shard_map/ppermute | solution.py:333
  62.4 2.8 %collective-permute-start.22 = (bf16[8,2,32,256]{3,2,1,0:T(8,128)(2,1)}, bf16[8,2,32,256]{3,2,1,0:T(8,128)(2,1)S(1)}, u32[]{:S(2)}, u32[]{:S(2)}) collective-permute-start(bf16[8,2,32,256]{3,2,1,0:T(8,128)(2,1)} %bitcast.77), channel_id=1, source_target_pairs={{0,1},{1,0},{2,3},{3,2},{4,5},{5,4},{6,7},{7,6},{8,9},{9,8},{10,11... | collective-permute-start | bytes 786440 | tf_op jit(solution)/shard_map/ppermute | solution.py:333
  62.8 15.6 %collective-permute-start.15 = (bf16[8,2,32,256]{3,2,1,0:T(8,128)(2,1)}, bf16[8,2,32,256]{3,2,1,0:T(8,128)(2,1)S(1)}, u32[]{:S(2)}, u32[]{:S(2)}) collective-permute-start(bf16[8,2,32,256]{3,2,1,0:T(8,128)(2,1)} %bitcast.72), channel_id=1, source_target_pairs={{0,1},{1,0},{2,3},{3,2},{4,5},{5,4},{6,7},{7,6},{8,9},{9,8},{10,11... | collective-permute-start | bytes 786440 | tf_op jit(solution)/shard_map/ppermute | solution.py:333
  62.9 3.6 %collective-permute-start.19 = (bf16[8,2,32,256]{3,2,1,0:T(8,128)(2,1)}, bf16[8,2,32,256]{3,2,1,0:T(8,128)(2,1)S(1)}, u32[]{:S(2)}, u32[]{:S(2)}) collective-permute-start(bf16[8,2,32,256]{3,2,1,0:T(8,128)(2,1)} %bitcast.75), channel_id=1, source_target_pairs={{0,1},{1,0},{2,3},{3,2},{4,5},{5,4},{6,7},{7,6},{8,9},{9,8},{10,11... | collective-permute-start | bytes 786440 | tf_op jit(solution)/shard_map/ppermute | solution.py:333
  63.3 5.2 %collective-permute-start.21 = (bf16[8,2,32,256]{3,2,1,0:T(8,128)(2,1)}, bf16[8,2,32,256]{3,2,1,0:T(8,128)(2,1)S(1)}, u32[]{:S(2)}, u32[]{:S(2)}) collective-permute-start(bf16[8,2,32,256]{3,2,1,0:T(8,128)(2,1)} %bitcast.74), channel_id=1, source_target_pairs={{0,1},{1,0},{2,3},{3,2},{4,5},{5,4},{6,7},{7,6},{8,9},{9,8},{10,11... | collective-permute-start | bytes 786440 | tf_op jit(solution)/shard_map/ppermute | solution.py:333
  64.0 2.0 %collective-permute-start.26 = (bf16[8,2,32,256]{3,2,1,0:T(8,128)(2,1)}, bf16[8,2,32,256]{3,2,1,0:T(8,128)(2,1)S(1)}, u32[]{:S(2)}, u32[]{:S(2)}) collective-permute-start(bf16[8,2,32,256]{3,2,1,0:T(8,128)(2,1)} %bitcast.76), channel_id=1, source_target_pairs={{0,1},{1,0},{2,3},{3,2},{4,5},{5,4},{6,7},{7,6},{8,9},{9,8},{10,11... | collective-permute-start | bytes 786440 | tf_op jit(solution)/shard_map/ppermute | solution.py:333
  64.1 2.3 %copy-start.14 = (bf16[4,2,2,32,256]{4,3,2,1,0:T(8,128)(2,1)S(1)}, bf16[4,2,2,32,256]{4,3,2,1,0:T(8,128)(2,1)}, u32[]{:S(2)}) copy-start(bf16[4,2,2,32,256]{4,3,2,1,0:T(8,128)(2,1)} %get-tuple-element.53) | copy-start | bytes 786436
  65.2 10.1 %collective-permute-start.25 = (bf16[8,2,32,256]{3,2,1,0:T(8,128)(2,1)S(1)}, bf16[8,2,32,256]{3,2,1,0:T(8,128)(2,1)S(1)}, u32[]{:S(2)}, u32[]{:S(2)}) collective-permute-start(bf16[8,2,32,256]{3,2,1,0:T(8,128)(2,1)S(1)} %bitcast.73), channel_id=1, source_target_pairs={{0,1},{1,0},{2,3},{3,2},{4,5},{5,4},{6,7},{7,6},{8,9},{9,8},{10,11... | collective-permute-start | bytes 786440 | tf_op jit(solution)/shard_map/ppermute | solution.py:333
  65.9 2.4 %copy-start.12 = (bf16[4,2,2,32,256]{4,3,2,1,0:T(8,128)(2,1)S(1)}, bf16[4,2,2,32,256]{4,3,2,1,0:T(8,128)(2,1)}, u32[]{:S(2)}) copy-start(bf16[4,2,2,32,256]{4,3,2,1,0:T(8,128)(2,1)} %get-tuple-element.45) | copy-start | bytes 786436
  66.0 8.4 %collective-permute-start.23 = (bf16[8,2,32,256]{3,2,1,0:T(8,128)(2,1)S(1)}, bf16[8,2,32,256]{3,2,1,0:T(8,128)(2,1)S(1)}, u32[]{:S(2)}, u32[]{:S(2)}) collective-permute-start(bf16[8,2,32,256]{3,2,1,0:T(8,128)(2,1)S(1)} %fusion.6), channel_id=1, source_target_pairs={{0,6},{2,0},{4,2},{6,4},{1,7},{3,1},{5,3},{7,5},{8,14},{10,8},{12,... | collective-permute-start | bytes 786440 | tf_op jit(solution)/shard_map/ppermute | solution.py:329
  66.4 2.1 %copy-start.27 = (bf16[4,2,2,32,256]{4,3,2,1,0:T(8,128)(2,1)S(1)}, bf16[4,2,2,32,256]{4,3,2,1,0:T(8,128)(2,1)}, u32[]{:S(2)}) copy-start(bf16[4,2,2,32,256]{4,3,2,1,0:T(8,128)(2,1)} %get-tuple-element.42) | copy-start | bytes 786436
  66.4 8.8 %copy-start.25 = (bf16[4,2,2,32,256]{4,3,2,1,0:T(8,128)(2,1)S(1)}, bf16[4,2,2,32,256]{4,3,2,1,0:T(8,128)(2,1)}, u32[]{:S(2)}) copy-start(bf16[4,2,2,32,256]{4,3,2,1,0:T(8,128)(2,1)} %get-tuple-element.47) | copy-start | bytes 786436
  66.5 11.4 %collective-permute-start.27 = (bf16[8,2,32,256]{3,2,1,0:T(8,128)(2,1)S(1)}, bf16[8,2,32,256]{3,2,1,0:T(8,128)(2,1)S(1)}, u32[]{:S(2)}, u32[]{:S(2)}) collective-permute-start(bf16[8,2,32,256]{3,2,1,0:T(8,128)(2,1)S(1)} %fusion.3), channel_id=1, source_target_pairs={{0,2},{2,4},{4,6},{6,0},{1,3},{3,5},{5,7},{7,1},{8,10},{10,12},{12... | collective-permute-start | bytes 786440 | tf_op jit(solution)/shard_map/ppermute | solution.py:329
  68.3 9.9 %copy-start.24 = (bf16[4,2,2,32,256]{4,3,2,1,0:T(8,128)(2,1)S(1)}, bf16[4,2,2,32,256]{4,3,2,1,0:T(8,128)(2,1)}, u32[]{:S(2)}) copy-start(bf16[4,2,2,32,256]{4,3,2,1,0:T(8,128)(2,1)} %get-tuple-element.51) | copy-start | bytes 786436
  68.5 11.7 %collective-permute-start.16 = (bf16[8,2,32,256]{3,2,1,0:T(8,128)(2,1)S(1)}, bf16[8,2,32,256]{3,2,1,0:T(8,128)(2,1)S(1)}, u32[]{:S(2)}, u32[]{:S(2)}) collective-permute-start(bf16[8,2,32,256]{3,2,1,0:T(8,128)(2,1)S(1)} %bitcast.71), channel_id=1, source_target_pairs={{0,1},{1,0},{2,3},{3,2},{4,5},{5,4},{6,7},{7,6},{8,9},{9,8},{10,11... | collective-permute-start | bytes 786440 | tf_op jit(solution)/shard_map/ppermute | solution.py:333
  74.5 10.5 %collective-permute-start.18 = (bf16[8,2,32,256]{3,2,1,0:T(8,128)(2,1)S(1)}, bf16[8,2,32,256]{3,2,1,0:T(8,128)(2,1)S(1)}, u32[]{:S(2)}, u32[]{:S(2)}) collective-permute-start(bf16[8,2,32,256]{3,2,1,0:T(8,128)(2,1)S(1)} %fusion.10), channel_id=1, source_target_pairs={{0,2},{2,4},{4,6},{6,0},{1,3},{3,5},{5,7},{7,1},{8,10},{10,12},{12... | collective-permute-start | bytes 786440 | tf_op jit(solution)/shard_map/ppermute | solution.py:329
  75.3 9.6 %collective-permute-start.20 = (bf16[8,2,32,256]{3,2,1,0:T(8,128)(2,1)S(1)}, bf16[8,2,32,256]{3,2,1,0:T(8,128)(2,1)S(1)}, u32[]{:S(2)}, u32[]{:S(2)}) collective-permute-start(bf16[8,2,32,256]{3,2,1,0:T(8,128)(2,1)S(1)} %fusion.9), channel_id=1, source_target_pairs={{0,6},{2,0},{4,2},{6,4},{1,7},{3,1},{5,3},{7,5},{8,14},{10,8},{12,... | collective-permute-start | bytes 786440 | tf_op jit(solution)/shard_map/ppermute | solution.py:329
  77.9 10.4 %collective-permute-start.24 = (bf16[8,2,32,256]{3,2,1,0:T(8,128)(2,1)S(1)}, bf16[8,2,32,256]{3,2,1,0:T(8,128)(2,1)S(1)}, u32[]{:S(2)}, u32[]{:S(2)}) collective-permute-start(bf16[8,2,32,256]{3,2,1,0:T(8,128)(2,1)S(1)} %fusion.8), channel_id=1, source_target_pairs={{0,6},{2,0},{4,2},{6,4},{1,7},{3,1},{5,3},{7,5},{8,14},{10,8},{12,... | collective-permute-start | bytes 786440 | tf_op jit(solution)/shard_map/ppermute | solution.py:329
  78.4 6.6 %copy-start.7 = (bf16[8,2,32,256]{3,2,1,0:T(8,128)(2,1)}, bf16[8,2,32,256]{3,2,1,0:T(8,128)(2,1)S(1)}, u32[]{:S(2)}) copy-start(bf16[8,2,32,256]{3,2,1,0:T(8,128)(2,1)S(1)} %collective-permute-done.15.refs_2_) | copy-start | bytes 786436
  78.4 10.4 %collective-permute-start.28 = (bf16[8,2,32,256]{3,2,1,0:T(8,128)(2,1)S(1)}, bf16[8,2,32,256]{3,2,1,0:T(8,128)(2,1)S(1)}, u32[]{:S(2)}, u32[]{:S(2)}) collective-permute-start(bf16[8,2,32,256]{3,2,1,0:T(8,128)(2,1)S(1)} %fusion.5), channel_id=1, source_target_pairs={{0,2},{2,4},{4,6},{6,0},{1,3},{3,5},{5,7},{7,1},{8,10},{10,12},{12... | collective-permute-start | bytes 786440 | tf_op jit(solution)/shard_map/ppermute | solution.py:329
  80.2 4.7 %copy-start.19 = (bf16[8,2,32,256]{3,2,1,0:T(8,128)(2,1)}, bf16[8,2,32,256]{3,2,1,0:T(8,128)(2,1)S(1)}, u32[]{:S(2)}) copy-start(bf16[8,2,32,256]{3,2,1,0:T(8,128)(2,1)S(1)} %collective-permute-done.16.refs_3_) | copy-start | bytes 786436
  84.9 0.7 copy-start.22
  84.9 0.8 copy-start.23

commit v6 on v5

--- a/solution.py
+++ b/solution.py
@@ -221,6 +221,8 @@
 
     wide[...] = jnp.zeros((ROWS, WIDTH), jnp.float32)
     out_copies = []
+    r1 = (q1.astype(jnp.float32) * inv1).astype(jnp.bfloat16)
+    r2 = (q2.astype(jnp.float32) * inv2).astype(jnp.bfloat16)
 
     def send(src, dst):
         copy = pltpu.make_async_copy(src, dst, out_sems.at[len(out_copies)])
@@ -233,8 +235,8 @@
         for step in range(STEPS):
             cols = slice(step * STEP, (step + 1) * STEP)
             da = das[of(j), cols]
-            t1 = p1s[of(j), cols] * (inv1[lo:] * (da - e1[lo:]))
-            t2 = p2s[of(j), cols] * (inv2[lo:] * (da - e2[lo:]))
+            t1 = p1s[of(j), cols] * (da - e1[lo:])
+            t2 = p2s[of(j), cols] * (da - e2[lo:])
             t1s[of(j), cols] = t1.astype(jnp.bfloat16)
             t2s[of(j), cols] = t2.astype(jnp.bfloat16)
 
@@ -244,8 +246,8 @@
 
         for step in range(STEPS):
             cols = slice(step * STEP, (step + 1) * STEP)
-            dk1 = dot_tn(q1[lo:], t1s[of(j), cols]) * SCALE
-            dk2 = dot_tn(q2[lo:], t2s[of(j), cols]) * (-SCALE * weight)
+            dk1 = dot_tn(r1[lo:], t1s[of(j), cols]) * SCALE
+            dk2 = dot_tn(r2[lo:], t2s[of(j), cols]) * (-SCALE * weight)
             dk = jnp.concatenate([dk1, dk2], axis=0)
             dv = dot_tn(d_out[lo:], mixs[of(j), cols])
             parts = slice(SPAN * step, SPAN * step + SPAN)
@@ -258,9 +260,9 @@
             half, at = j // HALVES, j % HALVES
             send(outs.at[half, where[u], at], term_outs[2 * u + half].at[at])
 
-    dq[:, :, :HALF] = (wide[:, :HALF] * SCALE).astype(jnp.bfloat16).reshape(SLICES, STRIPE, HALF)
+    dq[:, :, :HALF] = (wide[:, :HALF] * (inv1 * SCALE)).astype(jnp.bfloat16).reshape(SLICES, STRIPE, HALF)
     dq[:, :, HALF:] = (
-        (wide[:, HALF:] * (-SCALE * weight)).astype(jnp.bfloat16).reshape(SLICES, STRIPE, HALF)
+        (wide[:, HALF:] * (inv2 * (-SCALE * weight))).astype(jnp.bfloat16).reshape(SLICES, STRIPE, HALF)
     )
     send(dq, dq_out)
     for copy in out_copies:

time: 111 us -> 111 us (level)
  no operation moved by 1% of the time
where the time goes in v6:
time: 111 us; the launch traced here: 110 us
  starting transfers between devices  33 us (30%)
  waiting for transfers between devices  31 us (28%)
  Pallas kernels  21.8 us (20%)
  blocking collectives  18.1 us (16%)
  other arithmetic  2.98 us (3%)
  local copies, waits for them, and re-layouts  2.31 us (2%)
  between operations  1.15 us (1%)
    all_to_all x1, blocking collectives, shards(): return unpack(lax.all_to_all(total, SECTION, 0, 0, tiled=True))  18.1 us
    ppermute x12, waiting for transfers between devices, along_z(): return lax.ppermute(x, 'z', [(i, (i + d) % 4) for i in range(4)])  17.8 us
    ppermute x12, starting transfers between devices, along_z(): return lax.ppermute(x, 'z', [(i, (i + d) % 4) for i in range(4)])  16.9 us
    pallas_call x1, Pallas kernels, core(): pl.pallas_call(core_kernel, out_shape=(jax.ShapeDtypeStruct((SLICES, STRI...  13.4 us
    all_to_all x1, waiting for transfers between devices, shards(): kv = lax.all_to_all(pack(keys, values), SECTION, 0, 0, tiled=True)  8.19 us
    all_to_all x1, starting transfers between devices, shards(): kv = lax.all_to_all(pack(keys, values), SECTION, 0, 0, tiled=True)  7.12 us
    all_to_all x1, starting transfers between devices, shards(): qg = lax.all_to_all(qg, SECTION, 0, 0, tiled=True)  4.87 us
    pallas_call x2, Pallas kernels, pack(): pl.pallas_call(pack_kernel, out_shape=jax.ShapeDtypeStruct((SLICES, 2, ST...  3.76 us
  transfers between devices with their start and end apart: 31, of which 12 were waited for; matrix products, arithmetic and copies ran while one was open for 2% of the time, Pallas kernels for 4%

profile of v6, /device:TPU:0, one launch (start us, length us, event | category | flops | bytes accessed | tf_op | source)
XLA Modules:
  0.0 110.3 jit_solution(8259898277621408243)
XLA Ops:
  0.6 1.9 %pack.2 = bf16[16,2,32,256]{3,2,1,0:T(8,128)(2,1)} custom-call(bf16[32,4096]{1,0:T(8,128)(2,1)} %a_ref.2, bf16[32,4096]{1,0:T(8,128)(2,1)} %b_ref.2), custom_call_target="tpu_custom_call" | custom-call | tf_op jit(solution)/shard_map/pack/pallas_call | solution.py:44
  2.5 7.1 %all-to-all-start = ((bf16[16,2,32,256]{3,2,1,0:T(8,128)(2,1)}), bf16[16,2,32,256]{3,2,1,0:T(8,128)(2,1)S(1)}, u32[]{:S(2)}, u32[]{:S(2)}) async-start(bf16[16,2,32,256]{3,2,1,0:T(8,128)(2,1)} %pack.2), calls=%async_computation | async-start | bytes 1048576 | tf_op jit(solution)/shard_map/all_to_all | solution.py:347
  9.7 0.7 collective-permute-start
  10.4 1.9 %pack.3 = bf16[16,2,32,256]{3,2,1,0:T(8,128)(2,1)} custom-call(bf16[32,4096]{1,0:T(8,128)(2,1)} %a_ref.3, bf16[32,4096]{1,0:T(8,128)(2,1)} %b_ref.3), custom_call_target="tpu_custom_call" | custom-call | tf_op jit(solution)/shard_map/pack/pallas_call | solution.py:44
  12.3 0.7 stack.39.where
  13.0 8.2 %all-to-all-done = bf16[16,2,32,256]{3,2,1,0:T(8,128)(2,1)S(1)} async-done(((bf16[16,2,32,256]{3,2,1,0:T(8,128)(2,1)}), bf16[16,2,32,256]{3,2,1,0:T(8,128)(2,1)S(1)}, u32[]{:S(2)}, u32[]{:S(2)}) %all-to-all-start) | async-done | bytes 524320 | tf_op jit(solution)/shard_map/all_to_all | solution.py:347
  21.2 0.0 copy-start.1
  21.2 0.0 copy-start.2
  21.2 4.1 %collective-permute-start.5 = (bf16[8,2,32,256]{3,2,1,0:T(8,128)(2,1)S(1)}, bf16[8,2,32,256]{3,2,1,0:T(8,128)(2,1)S(1)}, u32[]{:S(2)}, u32[]{:S(2)}) collective-permute-start(bf16[8,2,32,256]{3,2,1,0:T(8,128)(2,1)S(1)} %get-tuple-element.32), channel_id=1, source_target_pairs={{0,6},{2,0},{4,2},{6,4},{1,7},{3,1},{5,3},{7,5},{8,14},{10,8},{12,... | collective-permute-start | bytes 786440 | tf_op jit(solution)/shard_map/ppermute | solution.py:331
  25.3 0.0 collective-permute-start.3
  25.3 3.3 %collective-permute-start.2 = (bf16[8,2,32,256]{3,2,1,0:T(8,128)(2,1)S(1)}, bf16[8,2,32,256]{3,2,1,0:T(8,128)(2,1)S(1)}, u32[]{:S(2)}, u32[]{:S(2)}) collective-permute-start(bf16[8,2,32,256]{3,2,1,0:T(8,128)(2,1)S(1)} %get-tuple-element.33), channel_id=1, source_target_pairs={{0,6},{2,0},{4,2},{6,4},{1,7},{3,1},{5,3},{7,5},{8,14},{10,8},{12,... | collective-permute-start | bytes 786440 | tf_op jit(solution)/shard_map/ppermute | solution.py:331
  28.6 4.9 %all-to-all-start.1 = ((bf16[16,2,32,256]{3,2,1,0:T(8,128)(2,1)}), bf16[16,2,32,256]{3,2,1,0:T(8,128)(2,1)S(1)}, u32[]{:S(2)}, u32[]{:S(2)}) async-start(bf16[16,2,32,256]{3,2,1,0:T(8,128)(2,1)} %pack.3), calls=%async_computation.1 | async-start | bytes 1048576 | tf_op jit(solution)/shard_map/all_to_all | solution.py:356
  33.5 0.1 collective-permute-start.8
  33.6 0.5 collective-permute-start.7
  34.1 1.7 %collective-permute-done.1 = bf16[8,2,32,256]{3,2,1,0:T(8,128)(2,1)S(1)} collective-permute-done((bf16[8,2,32,256]{3,2,1,0:T(8,128)(2,1)S(1)}, bf16[8,2,32,256]{3,2,1,0:T(8,128)(2,1)S(1)}, u32[]{:S(2)}, u32[]{:S(2)}) %collective-permute-start.1) | collective-permute-done | bytes 262176 | tf_op jit(solution)/shard_map/ppermute | solution.py:331
  35.8 2.9 %collective-permute-done.3 = bf16[8,2,32,256]{3,2,1,0:T(8,128)(2,1)S(1)} collective-permute-done((bf16[8,2,32,256]{3,2,1,0:T(8,128)(2,1)S(1)}, bf16[8,2,32,256]{3,2,1,0:T(8,128)(2,1)S(1)}, u32[]{:S(2)}, u32[]{:S(2)}) %collective-permute-start.3) | collective-permute-done | bytes 262176 | tf_op jit(solution)/shard_map/ppermute | solution.py:331
  38.7 0.0 collective-permute-start.6
  38.7 2.0 %collective-permute-start.4 = (bf16[8,2,32,256]{3,2,1,0:T(8,128)(2,1)S(1)}, bf16[8,2,32,256]{3,2,1,0:T(8,128)(2,1)S(1)}, u32[]{:S(2)}, u32[]{:S(2)}) collective-permute-start(bf16[8,2,32,256]{3,2,1,0:T(8,128)(2,1)S(1)} %collective-permute-done.3), channel_id=1, source_target_pairs={{0,2},{2,4},{4,6},{6,0},{1,3},{3,5},{5,7},{7,1},{8,10},{10,12},{12... | collective-permute-start | bytes 786440 | tf_op jit(solution)/shard_map/ppermute | solution.py:331
  40.7 2.9 %all-to-all-done.1.qg_in = bf16[16,2,32,256]{3,2,1,0:T(8,128)(2,1)S(1)} async-done(((bf16[16,2,32,256]{3,2,1,0:T(8,128)(2,1)}), bf16[16,2,32,256]{3,2,1,0:T(8,128)(2,1)S(1)}, u32[]{:S(2)}, u32[]{:S(2)}) %all-to-all-start.1) | async-done | bytes 524320 | tf_op jit(solution)/shard_map/all_to_all | solution.py:356
  43.6 0.1 collective-permute-start.9
  43.7 0.5 collective-permute-start.10
  44.2 0.1 collective-permute-start.13
  44.3 0.8 collective-permute-done.6
  45.0 1.3 %collective-permute-done.4 = bf16[8,2,32,256]{3,2,1,0:T(8,128)(2,1)S(1)} collective-permute-done((bf16[8,2,32,256]{3,2,1,0:T(8,128)(2,1)S(1)}, bf16[8,2,32,256]{3,2,1,0:T(8,128)(2,1)S(1)}, u32[]{:S(2)}, u32[]{:S(2)}) %collective-permute-start.4) | collective-permute-done | bytes 262176 | tf_op jit(solution)/shard_map/ppermute | solution.py:331
  46.3 0.0 collective-permute-start.11
  46.3 0.0 collective-permute-done.9
  46.4 0.0 collective-permute-done.10
  46.4 0.2 collective-permute-done.12
  46.6 1.3 %collective-permute-done.11 = bf16[8,2,32,256]{3,2,1,0:T(8,128)(2,1)S(1)} collective-permute-done((bf16[8,2,32,256]{3,2,1,0:T(8,128)(2,1)S(1)}, bf16[8,2,32,256]{3,2,1,0:T(8,128)(2,1)S(1)}, u32[]{:S(2)}, u32[]{:S(2)}) %collective-permute-start.11) | collective-permute-done | bytes 262176 | tf_op jit(solution)/shard_map/ppermute | solution.py:335
  47.9 0.7 copy-done.21
  48.7 13.4 %attention.1 = (bf16[16,32,256]{2,1,0:T(8,128)(2,1)}, bf16[4,2,2,32,256]{4,3,2,1,0:T(8,128)(2,1)}, bf16[4,2,2,32,256]{4,3,2,1,0:T(8,128)(2,1)}, bf16[4,2,2,32,25...) custom-call(s32[16]{0:T(128)} %lengths.1, ...), custom_call_target="tpu_custom_call" | custom-call | tf_op jit(solution)/shard_map/attention/pallas_call | solution.py:277
  62.2 0.2 collective-permute-start.17
  62.4 0.4 collective-permute-start.22
  62.8 0.1 collective-permute-start.15
  62.9 0.4 collective-permute-start.19
  63.3 0.1 collective-permute-start.21
  63.4 0.6 collective-permute-done.17
  64.0 0.1 collective-permute-start.26
  64.1 1.1 fusion.10
  65.2 0.0 collective-permute-done.22
  65.2 0.7 collective-permute-start.25
  65.9 0.1 fusion.6
  66.0 0.3 collective-permute-start.23
  66.4 0.1 fusion.3
  66.5 1.8 %collective-permute-start.27 = (bf16[8,2,32,256]{3,2,1,0:T(8,128)(2,1)S(1)}, bf16[8,2,32,256]{3,2,1,0:T(8,128)(2,1)S(1)}, u32[]{:S(2)}, u32[]{:S(2)}) collective-permute-start(bf16[8,2,32,256]{3,2,1,0:T(8,128)(2,1)S(1)} %fusion.3), channel_id=1, source_target_pairs={{0,2},{2,4},{4,6},{6,0},{1,3},{3,5},{5,7},{7,1},{8,10},{10,12},{12... | collective-permute-start | bytes 786440 | tf_op jit(solution)/shard_map/ppermute | solution.py:331
  68.3 0.1 fusion.9
  68.5 0.1 collective-permute-start.16
  68.6 5.9 %collective-permute-done.23 = bf16[8,2,32,256]{3,2,1,0:T(8,128)(2,1)S(1)} collective-permute-done((bf16[8,2,32,256]{3,2,1,0:T(8,128)(2,1)S(1)}, bf16[8,2,32,256]{3,2,1,0:T(8,128)(2,1)S(1)}, u32[]{:S(2)}, u32[]{:S(2)}) %collective-permute-start.23) | collective-permute-done | bytes 262176 | tf_op jit(solution)/shard_map/ppermute | solution.py:331
  74.5 0.7 collective-permute-start.18
  75.2 0.1 fusion.8
  75.3 2.6 %collective-permute-start.20 = (bf16[8,2,32,256]{3,2,1,0:T(8,128)(2,1)S(1)}, bf16[8,2,32,256]{3,2,1,0:T(8,128)(2,1)S(1)}, u32[]{:S(2)}, u32[]{:S(2)}) collective-permute-start(bf16[8,2,32,256]{3,2,1,0:T(8,128)(2,1)S(1)} %fusion.9), channel_id=1, source_target_pairs={{0,6},{2,0},{4,2},{6,4},{1,7},{3,1},{5,3},{7,5},{8,14},{10,8},{12,... | collective-permute-start | bytes 786440 | tf_op jit(solution)/shard_map/ppermute | solution.py:331
  77.9 0.3 collective-permute-start.24
  78.2 0.1 fusion.5
  78.4 0.0 copy-start.7
  78.4 1.8 %collective-permute-start.28 = (bf16[8,2,32,256]{3,2,1,0:T(8,128)(2,1)S(1)}, bf16[8,2,32,256]{3,2,1,0:T(8,128)(2,1)S(1)}, u32[]{:S(2)}, u32[]{:S(2)}) collective-permute-start(bf16[8,2,32,256]{3,2,1,0:T(8,128)(2,1)S(1)} %fusion.5), channel_id=1, source_target_pairs={{0,2},{2,4},{4,6},{6,0},{1,3},{3,5},{5,7},{7,1},{8,10},{10,12},{12... | collective-permute-start | bytes 786440 | tf_op jit(solution)/shard_map/ppermute | solution.py:331
  80.2 4.7 %collective-permute-done.18.refs_4_ = bf16[8,2,32,256]{3,2,1,0:T(8,128)(2,1)S(1)} collective-permute-done((bf16[8,2,32,256]{3,2,1,0:T(8,128)(2,1)S(1)}, bf16[8,2,32,256]{3,2,1,0:T(8,128)(2,1)S(1)}, u32[]{:S(2)}, u32[]{:S(2)}) %collective-permute-start.18) | collective-permute-done | bytes 262176 | tf_op jit(solution)/shard_map/ppermute | solution.py:331
  84.9 0.7 copy-done.22
  85.6 0.1 copy-done.23
  85.7 2.5 %gather.1 = bf16[16,3,32,256]{3,2,1,0:T(8,128)(2,1)} custom-call(bf16[16,32,256]{2,1,0:T(8,128)(2,1)} %get-tuple-element.38.d_query, bf16[8,2,32,256]{3,2,1,0:T(8,128)(2,1)} %bitcast.55, bf16[8,2,32,256]{3,2,1,0:T(8,128)(2,1)} %bitcast.56, bf16[8,2,32,256]{3,2,1,0:T(8,128)(2,1)} %copy-done.7, bf16[8,2,32,256]{3,2,1,0:T(8,128)(2,1)} %copy-done.19, ...), custom_call_target="tpu_custom_call" | custom-call | flops 1000000 | bytes 3000000 | tf_op jit(solution)/shard_map/gather/pallas_call | solution.py:320
  88.3 0.0 collective-permute-done.24
  88.3 0.5 collective-permute-done.28
  88.8 1.3 %add_convert_fusion = bf16[16,3,32,256]{3,2,1,0:T(8,128)(2,1)S(1)} fusion(bf16[16,3,32,256]{3,2,1,0:T(8,128)(2,1)} %gather.1, bf16[8,2,32,256]{3,2,1,0:T(8,128)(2,1)S(1)} %collective-permute-done.28, bf16[8,2,32,256]{3,2,1,0:T(8,128)(2,1)S(1)} %collective-permute-done.24), kind=kLoop, calls=%fused_computation.3 | loop fusion | flops 3932160 | bytes 2097152 | tf_op jit(solution)/shard_map/convert_element_type | solution.py:363
  90.1 18.1 %all_to_all.15.in_ref = bf16[16,3,32,256]{3,2,1,0:T(8,128)(2,1)} all-to-all(bf16[16,3,32,256]{3,2,1,0:T(8,128)(2,1)S(1)} %add_convert_fusion), channel_id=1, replica_groups=mesh['x'=4,'y'=4,'z'=4,'core'=2] {'x','y'}, dimensions={0} | all-to-all | bytes 1572864 | tf_op jit(solution)/shard_map/all_to_all | solution.py:377
  108.2 2.0 %unpack.1 = (bf16[32,4096]{1,0:T(8,128)(2,1)}, bf16[32,4096]{1,0:T(8,128)(2,1)}, bf16[32,4096]{1,0:T(8,128)(2,1)}) custom-call(bf16[16,3,32,256]{3,2,1,0:T(8,128)(2,1)} %all_to_all.15.in_ref), custom_call_target="tpu_custom_call" | custom-call | tf_op jit(solution)/shard_map/unpack/pallas_call | solution.py:61
  (73 shorter events, 0.2 us)
Async XLA Ops:
  0.6 9.0 %copy-start.29 = (f32[2]{0:T(128)S(1)}, f32[2]{0:T(128)}, u32[]{:S(2)}) copy-start(f32[2]{0:T(128)} %param.10) | copy-start | bytes 28
  2.5 18.6 %all-to-all-start = ((bf16[16,2,32,256]{3,2,1,0:T(8,128)(2,1)}), bf16[16,2,32,256]{3,2,1,0:T(8,128)(2,1)S(1)}, u32[]{:S(2)}, u32[]{:S(2)}) async-start(bf16[16,2,32,256]{3,2,1,0:T(8,128)(2,1)} %pack.2), calls=%async_computation | async-start | bytes 1048576 | tf_op jit(solution)/shard_map/all_to_all | solution.py:347
  9.7 3.3 %collective-permute-start = (f32[2]{0:T(128)S(1)}, f32[2]{0:T(128)S(1)}, u32[]{:S(2)}, u32[]{:S(2)}) collective-permute-start(f32[2]{0:T(128)S(1)} %copy-done.29), channel_id=1, source_target_pairs={{0,0},{1,16},{2,32},{3,48},{4,64},{5,80},{6,96},{7,112},{8,1},{9,1... | collective-permute-start | bytes 32 | tf_op jit(solution)/shard_map/ppermute | solution.py:348
  13.0 15.6 %copy-start.26 = (f32[2]{0:T(128)}, f32[2]{0:T(128)S(1)}, u32[]{:S(2)}) copy-start(f32[2]{0:T(128)S(1)} %collective-permute-done.lams) | copy-start | bytes 28
  21.2 27.4 %copy-start.1 = (bf16[8,2,32,256]{3,2,1,0:T(8,128)(2,1)}, bf16[8,2,32,256]{3,2,1,0:T(8,128)(2,1)S(1)}, u32[]{:S(2)}) copy-start(bf16[8,2,32,256]{3,2,1,0:T(8,128)(2,1)S(1)} %get-tuple-element.32) | copy-start | bytes 786436
  21.2 27.4 %copy-start.2 = (bf16[8,2,32,256]{3,2,1,0:T(8,128)(2,1)}, bf16[8,2,32,256]{3,2,1,0:T(8,128)(2,1)S(1)}, u32[]{:S(2)}) copy-start(bf16[8,2,32,256]{3,2,1,0:T(8,128)(2,1)S(1)} %get-tuple-element.33) | copy-start | bytes 786436
  21.2 12.3 %collective-permute-start.5 = (bf16[8,2,32,256]{3,2,1,0:T(8,128)(2,1)S(1)}, bf16[8,2,32,256]{3,2,1,0:T(8,128)(2,1)S(1)}, u32[]{:S(2)}, u32[]{:S(2)}) collective-permute-start(bf16[8,2,32,256]{3,2,1,0:T(8,128)(2,1)S(1)} %get-tuple-element.32), channel_id=1, source_target_pairs={{0,6},{2,0},{4,2},{6,4},{1,7},{3,1},{5,3},{7,5},{8,14},{10,8},{12,... | collective-permute-start | bytes 786440 | tf_op jit(solution)/shard_map/ppermute | solution.py:331
  25.3 10.5 %collective-permute-start.1 = (bf16[8,2,32,256]{3,2,1,0:T(8,128)(2,1)S(1)}, bf16[8,2,32,256]{3,2,1,0:T(8,128)(2,1)S(1)}, u32[]{:S(2)}, u32[]{:S(2)}) collective-permute-start(bf16[8,2,32,256]{3,2,1,0:T(8,128)(2,1)S(1)} %get-tuple-element.32), channel_id=1, source_target_pairs={{0,2},{2,4},{4,6},{6,0},{1,3},{3,5},{5,7},{7,1},{8,10},{10,12},{12... | collective-permute-start | bytes 786440 | tf_op jit(solution)/shard_map/ppermute | solution.py:331
  25.3 13.3 %collective-permute-start.3 = (bf16[8,2,32,256]{3,2,1,0:T(8,128)(2,1)S(1)}, bf16[8,2,32,256]{3,2,1,0:T(8,128)(2,1)S(1)}, u32[]{:S(2)}, u32[]{:S(2)}) collective-permute-start(bf16[8,2,32,256]{3,2,1,0:T(8,128)(2,1)S(1)} %get-tuple-element.33), channel_id=1, source_target_pairs={{0,2},{2,4},{4,6},{6,0},{1,3},{3,5},{5,7},{7,1},{8,10},{10,12},{12... | collective-permute-start | bytes 786440 | tf_op jit(solution)/shard_map/ppermute | solution.py:331
  25.3 13.3 %collective-permute-start.2 = (bf16[8,2,32,256]{3,2,1,0:T(8,128)(2,1)S(1)}, bf16[8,2,32,256]{3,2,1,0:T(8,128)(2,1)S(1)}, u32[]{:S(2)}, u32[]{:S(2)}) collective-permute-start(bf16[8,2,32,256]{3,2,1,0:T(8,128)(2,1)S(1)} %get-tuple-element.33), channel_id=1, source_target_pairs={{0,6},{2,0},{4,2},{6,4},{1,7},{3,1},{5,3},{7,5},{8,14},{10,8},{12,... | collective-permute-start | bytes 786440 | tf_op jit(solution)/shard_map/ppermute | solution.py:331
  28.6 15.0 %all-to-all-start.1 = ((bf16[16,2,32,256]{3,2,1,0:T(8,128)(2,1)}), bf16[16,2,32,256]{3,2,1,0:T(8,128)(2,1)S(1)}, u32[]{:S(2)}, u32[]{:S(2)}) async-start(bf16[16,2,32,256]{3,2,1,0:T(8,128)(2,1)} %pack.3), calls=%async_computation.1 | async-start | bytes 1048576 | tf_op jit(solution)/shard_map/all_to_all | solution.py:356
  33.5 10.1 %collective-permute-start.8 = (bf16[8,2,32,256]{3,2,1,0:T(8,128)(2,1)S(1)}, bf16[8,2,32,256]{3,2,1,0:T(8,128)(2,1)S(1)}, u32[]{:S(2)}, u32[]{:S(2)}) collective-permute-start(bf16[8,2,32,256]{3,2,1,0:T(8,128)(2,1)S(1)} %get-tuple-element.32), channel_id=1, source_target_pairs={{0,1},{1,0},{2,3},{3,2},{4,5},{5,4},{6,7},{7,6},{8,9},{9,8},{10,11... | collective-permute-start | bytes 786440 | tf_op jit(solution)/shard_map/ppermute | solution.py:335
  33.6 15.0 %copy-start.3 = (bf16[8,2,32,256]{3,2,1,0:T(8,128)(2,1)}, bf16[8,2,32,256]{3,2,1,0:T(8,128)(2,1)S(1)}, u32[]{:S(2)}) copy-start(bf16[8,2,32,256]{3,2,1,0:T(8,128)(2,1)S(1)} %collective-permute-done.5) | copy-start | bytes 786436
  33.6 10.1 %collective-permute-start.7 = (bf16[8,2,32,256]{3,2,1,0:T(8,128)(2,1)S(1)}, bf16[8,2,32,256]{3,2,1,0:T(8,128)(2,1)S(1)}, u32[]{:S(2)}, u32[]{:S(2)}) collective-permute-start(bf16[8,2,32,256]{3,2,1,0:T(8,128)(2,1)S(1)} %get-tuple-element.33), channel_id=1, source_target_pairs={{0,1},{1,0},{2,3},{3,2},{4,5},{5,4},{6,7},{7,6},{8,9},{9,8},{10,11... | collective-permute-start | bytes 786440 | tf_op jit(solution)/shard_map/ppermute | solution.py:335
  35.8 12.8 %copy-start.4 = (bf16[8,2,32,256]{3,2,1,0:T(8,128)(2,1)}, bf16[8,2,32,256]{3,2,1,0:T(8,128)(2,1)S(1)}, u32[]{:S(2)}) copy-start(bf16[8,2,32,256]{3,2,1,0:T(8,128)(2,1)S(1)} %collective-permute-done.1) | copy-start | bytes 786436
  35.8 8.4 %collective-permute-start.14 = (bf16[8,2,32,256]{3,2,1,0:T(8,128)(2,1)S(1)}, bf16[8,2,32,256]{3,2,1,0:T(8,128)(2,1)S(1)}, u32[]{:S(2)}, u32[]{:S(2)}) collective-permute-start(bf16[8,2,32,256]{3,2,1,0:T(8,128)(2,1)S(1)} %collective-permute-done.5), channel_id=1, source_target_pairs={{0,1},{1,0},{2,3},{3,2},{4,5},{5,4},{6,7},{7,6},{8,9},{9,8},{10,11... | collective-permute-start | bytes 786440 | tf_op jit(solution)/shard_map/ppermute | solution.py:335
  38.7 9.9 %copy-start.5 = (bf16[8,2,32,256]{3,2,1,0:T(8,128)(2,1)}, bf16[8,2,32,256]{3,2,1,0:T(8,128)(2,1)S(1)}, u32[]{:S(2)}) copy-start(bf16[8,2,32,256]{3,2,1,0:T(8,128)(2,1)S(1)} %collective-permute-done.3) | copy-start | bytes 786436
  38.7 6.4 %collective-permute-start.6 = (bf16[8,2,32,256]{3,2,1,0:T(8,128)(2,1)S(1)}, bf16[8,2,32,256]{3,2,1,0:T(8,128)(2,1)S(1)}, u32[]{:S(2)}, u32[]{:S(2)}) collective-permute-start(bf16[8,2,32,256]{3,2,1,0:T(8,128)(2,1)S(1)} %collective-permute-done.5), channel_id=1, source_target_pairs={{0,6},{2,0},{4,2},{6,4},{1,7},{3,1},{5,3},{7,5},{8,14},{10,8},{12,... | collective-permute-start | bytes 786440 | tf_op jit(solution)/shard_map/ppermute | solution.py:331
  38.7 9.9 %copy-start.6 = (bf16[8,2,32,256]{3,2,1,0:T(8,128)(2,1)}, bf16[8,2,32,256]{3,2,1,0:T(8,128)(2,1)S(1)}, u32[]{:S(2)}) copy-start(bf16[8,2,32,256]{3,2,1,0:T(8,128)(2,1)S(1)} %collective-permute-done.2) | copy-start | bytes 786436
  38.7 7.7 %collective-permute-start.4 = (bf16[8,2,32,256]{3,2,1,0:T(8,128)(2,1)S(1)}, bf16[8,2,32,256]{3,2,1,0:T(8,128)(2,1)S(1)}, u32[]{:S(2)}, u32[]{:S(2)}) collective-permute-start(bf16[8,2,32,256]{3,2,1,0:T(8,128)(2,1)S(1)} %collective-permute-done.3), channel_id=1, source_target_pairs={{0,2},{2,4},{4,6},{6,0},{1,3},{3,5},{5,7},{7,1},{8,10},{10,12},{12... | collective-permute-start | bytes 786440 | tf_op jit(solution)/shard_map/ppermute | solution.py:331
  43.6 5.1 %copy-start = (bf16[16,2,32,256]{3,2,1,0:T(8,128)(2,1)}, bf16[16,2,32,256]{3,2,1,0:T(8,128)(2,1)S(1)}, u32[]{:S(2)}) copy-start(bf16[16,2,32,256]{3,2,1,0:T(8,128)(2,1)S(1)} %all-to-all-done.1.qg_in) | copy-start | bytes 1572868
  43.6 5.1 %copy-start.8 = (bf16[8,2,32,256]{3,2,1,0:T(8,128)(2,1)}, bf16[8,2,32,256]{3,2,1,0:T(8,128)(2,1)S(1)}, u32[]{:S(2)}) copy-start(bf16[8,2,32,256]{3,2,1,0:T(8,128)(2,1)S(1)} %collective-permute-done.8) | copy-start | bytes 786436
  43.6 2.8 %collective-permute-start.9 = (bf16[8,2,32,256]{3,2,1,0:T(8,128)(2,1)S(1)}, bf16[8,2,32,256]{3,2,1,0:T(8,128)(2,1)S(1)}, u32[]{:S(2)}, u32[]{:S(2)}) collective-permute-start(bf16[8,2,32,256]{3,2,1,0:T(8,128)(2,1)S(1)} %collective-permute-done.3), channel_id=1, source_target_pairs={{0,1},{1,0},{2,3},{3,2},{4,5},{5,4},{6,7},{7,6},{8,9},{9,8},{10,11... | collective-permute-start | bytes 786440 | tf_op jit(solution)/shard_map/ppermute | solution.py:335
  43.7 5.0 %copy-start.9 = (bf16[8,2,32,256]{3,2,1,0:T(8,128)(2,1)}, bf16[8,2,32,256]{3,2,1,0:T(8,128)(2,1)S(1)}, u32[]{:S(2)}) copy-start(bf16[8,2,32,256]{3,2,1,0:T(8,128)(2,1)S(1)} %collective-permute-done.7) | copy-start | bytes 786436
  43.7 2.7 %collective-permute-start.10 = (bf16[8,2,32,256]{3,2,1,0:T(8,128)(2,1)S(1)}, bf16[8,2,32,256]{3,2,1,0:T(8,128)(2,1)S(1)}, u32[]{:S(2)}, u32[]{:S(2)}) collective-permute-start(bf16[8,2,32,256]{3,2,1,0:T(8,128)(2,1)S(1)} %collective-permute-done.1), channel_id=1, source_target_pairs={{0,1},{1,0},{2,3},{3,2},{4,5},{5,4},{6,7},{7,6},{8,9},{9,8},{10,11... | collective-permute-start | bytes 786440 | tf_op jit(solution)/shard_map/ppermute | solution.py:335
  44.2 4.5 %copy-start.10 = (bf16[8,2,32,256]{3,2,1,0:T(8,128)(2,1)}, bf16[8,2,32,256]{3,2,1,0:T(8,128)(2,1)S(1)}, u32[]{:S(2)}) copy-start(bf16[8,2,32,256]{3,2,1,0:T(8,128)(2,1)S(1)} %collective-permute-done.14) | copy-start | bytes 786436
  44.2 2.2 %collective-permute-start.13 = (bf16[8,2,32,256]{3,2,1,0:T(8,128)(2,1)S(1)}, bf16[8,2,32,256]{3,2,1,0:T(8,128)(2,1)S(1)}, u32[]{:S(2)}, u32[]{:S(2)}) collective-permute-start(bf16[8,2,32,256]{3,2,1,0:T(8,128)(2,1)S(1)} %collective-permute-done.2), channel_id=1, source_target_pairs={{0,1},{1,0},{2,3},{3,2},{4,5},{5,4},{6,7},{7,6},{8,9},{9,8},{10,11... | collective-permute-start | bytes 786440 | tf_op jit(solution)/shard_map/ppermute | solution.py:335
  45.0 3.6 %copy-start.11 = (bf16[8,2,32,256]{3,2,1,0:T(8,128)(2,1)}, bf16[8,2,32,256]{3,2,1,0:T(8,128)(2,1)S(1)}, u32[]{:S(2)}) copy-start(bf16[8,2,32,256]{3,2,1,0:T(8,128)(2,1)S(1)} %collective-permute-done.6) | copy-start | bytes 786436
  45.0 1.5 %collective-permute-start.12 = (bf16[8,2,32,256]{3,2,1,0:T(8,128)(2,1)S(1)}, bf16[8,2,32,256]{3,2,1,0:T(8,128)(2,1)S(1)}, u32[]{:S(2)}, u32[]{:S(2)}) collective-permute-start(bf16[8,2,32,256]{3,2,1,0:T(8,128)(2,1)S(1)} %collective-permute-done.6), channel_id=1, source_target_pairs={{0,1},{1,0},{2,3},{3,2},{4,5},{5,4},{6,7},{7,6},{8,9},{9,8},{10,11... | collective-permute-start | bytes 786440 | tf_op jit(solution)/shard_map/ppermute | solution.py:335
  46.3 2.3 %copy-start.13 = (bf16[8,2,32,256]{3,2,1,0:T(8,128)(2,1)}, bf16[8,2,32,256]{3,2,1,0:T(8,128)(2,1)S(1)}, u32[]{:S(2)}) copy-start(bf16[8,2,32,256]{3,2,1,0:T(8,128)(2,1)S(1)} %collective-permute-done.4) | copy-start | bytes 786436
  46.3 1.5 %collective-permute-start.11 = (bf16[8,2,32,256]{3,2,1,0:T(8,128)(2,1)S(1)}, bf16[8,2,32,256]{3,2,1,0:T(8,128)(2,1)S(1)}, u32[]{:S(2)}, u32[]{:S(2)}) collective-permute-start(bf16[8,2,32,256]{3,2,1,0:T(8,128)(2,1)S(1)} %collective-permute-done.4), channel_id=1, source_target_pairs={{0,1},{1,0},{2,3},{3,2},{4,5},{5,4},{6,7},{7,6},{8,9},{9,8},{10,11... | collective-permute-start | bytes 786440 | tf_op jit(solution)/shard_map/ppermute | solution.py:335
  46.3 2.3 %copy-start.15 = (bf16[8,2,32,256]{3,2,1,0:T(8,128)(2,1)}, bf16[8,2,32,256]{3,2,1,0:T(8,128)(2,1)S(1)}, u32[]{:S(2)}) copy-start(bf16[8,2,32,256]{3,2,1,0:T(8,128)(2,1)S(1)} %collective-permute-done.9) | copy-start | bytes 786436
  46.4 2.3 %copy-start.17 = (bf16[8,2,32,256]{3,2,1,0:T(8,128)(2,1)}, bf16[8,2,32,256]{3,2,1,0:T(8,128)(2,1)S(1)}, u32[]{:S(2)}) copy-start(bf16[8,2,32,256]{3,2,1,0:T(8,128)(2,1)S(1)} %collective-permute-done.10) | copy-start | bytes 786436
  46.4 1.5 %copy-start.18 = (bf16[8,2,32,256]{3,2,1,0:T(8,128)(2,1)}, bf16[8,2,32,256]{3,2,1,0:T(8,128)(2,1)S(1)}, u32[]{:S(2)}) copy-start(bf16[8,2,32,256]{3,2,1,0:T(8,128)(2,1)S(1)} %collective-permute-done.13) | copy-start | bytes 786436
  46.6 1.3 %copy-start.20 = (bf16[8,2,32,256]{3,2,1,0:T(8,128)(2,1)}, bf16[8,2,32,256]{3,2,1,0:T(8,128)(2,1)S(1)}, u32[]{:S(2)}) copy-start(bf16[8,2,32,256]{3,2,1,0:T(8,128)(2,1)S(1)} %collective-permute-done.12) | copy-start | bytes 786436
  47.9 0.7 copy-start.21
  62.2 3.1 %copy-start.28 = (bf16[4,2,2,32,256]{4,3,2,1,0:T(8,128)(2,1)S(1)}, bf16[4,2,2,32,256]{4,3,2,1,0:T(8,128)(2,1)}, u32[]{:S(2)}) copy-start(bf16[4,2,2,32,256]{4,3,2,1,0:T(8,128)(2,1)} %get-tuple-element.52) | copy-start | bytes 786436
  62.2 3.8 %copy-start.16 = (bf16[4,2,2,32,256]{4,3,2,1,0:T(8,128)(2,1)S(1)}, bf16[4,2,2,32,256]{4,3,2,1,0:T(8,128)(2,1)}, u32[]{:S(2)}) copy-start(bf16[4,2,2,32,256]{4,3,2,1,0:T(8,128)(2,1)} %get-tuple-element.49) | copy-start | bytes 786436
  62.2 1.8 %collective-permute-start.17 = (bf16[8,2,32,256]{3,2,1,0:T(8,128)(2,1)}, bf16[8,2,32,256]{3,2,1,0:T(8,128)(2,1)S(1)}, u32[]{:S(2)}, u32[]{:S(2)}) collective-permute-start(bf16[8,2,32,256]{3,2,1,0:T(8,128)(2,1)} %bitcast.78), channel_id=1, source_target_pairs={{0,1},{1,0},{2,3},{3,2},{4,5},{5,4},{6,7},{7,6},{8,9},{9,8},{10,11... | collective-permute-start | bytes 786440 | tf_op jit(solution)/shard_map/ppermute | solution.py:335
  62.4 2.8 %collective-permute-start.22 = (bf16[8,2,32,256]{3,2,1,0:T(8,128)(2,1)}, bf16[8,2,32,256]{3,2,1,0:T(8,128)(2,1)S(1)}, u32[]{:S(2)}, u32[]{:S(2)}) collective-permute-start(bf16[8,2,32,256]{3,2,1,0:T(8,128)(2,1)} %bitcast.77), channel_id=1, source_target_pairs={{0,1},{1,0},{2,3},{3,2},{4,5},{5,4},{6,7},{7,6},{8,9},{9,8},{10,11... | collective-permute-start | bytes 786440 | tf_op jit(solution)/shard_map/ppermute | solution.py:335
  62.8 15.6 %collective-permute-start.15 = (bf16[8,2,32,256]{3,2,1,0:T(8,128)(2,1)}, bf16[8,2,32,256]{3,2,1,0:T(8,128)(2,1)S(1)}, u32[]{:S(2)}, u32[]{:S(2)}) collective-permute-start(bf16[8,2,32,256]{3,2,1,0:T(8,128)(2,1)} %bitcast.72), channel_id=1, source_target_pairs={{0,1},{1,0},{2,3},{3,2},{4,5},{5,4},{6,7},{7,6},{8,9},{9,8},{10,11... | collective-permute-start | bytes 786440 | tf_op jit(solution)/shard_map/ppermute | solution.py:335
  62.9 3.6 %collective-permute-start.19 = (bf16[8,2,32,256]{3,2,1,0:T(8,128)(2,1)}, bf16[8,2,32,256]{3,2,1,0:T(8,128)(2,1)S(1)}, u32[]{:S(2)}, u32[]{:S(2)}) collective-permute-start(bf16[8,2,32,256]{3,2,1,0:T(8,128)(2,1)} %bitcast.75), channel_id=1, source_target_pairs={{0,1},{1,0},{2,3},{3,2},{4,5},{5,4},{6,7},{7,6},{8,9},{9,8},{10,11... | collective-permute-start | bytes 786440 | tf_op jit(solution)/shard_map/ppermute | solution.py:335
  63.3 5.2 %collective-permute-start.21 = (bf16[8,2,32,256]{3,2,1,0:T(8,128)(2,1)}, bf16[8,2,32,256]{3,2,1,0:T(8,128)(2,1)S(1)}, u32[]{:S(2)}, u32[]{:S(2)}) collective-permute-start(bf16[8,2,32,256]{3,2,1,0:T(8,128)(2,1)} %bitcast.74), channel_id=1, source_target_pairs={{0,1},{1,0},{2,3},{3,2},{4,5},{5,4},{6,7},{7,6},{8,9},{9,8},{10,11... | collective-permute-start | bytes 786440 | tf_op jit(solution)/shard_map/ppermute | solution.py:335
  64.0 2.0 %collective-permute-start.26 = (bf16[8,2,32,256]{3,2,1,0:T(8,128)(2,1)}, bf16[8,2,32,256]{3,2,1,0:T(8,128)(2,1)S(1)}, u32[]{:S(2)}, u32[]{:S(2)}) collective-permute-start(bf16[8,2,32,256]{3,2,1,0:T(8,128)(2,1)} %bitcast.76), channel_id=1, source_target_pairs={{0,1},{1,0},{2,3},{3,2},{4,5},{5,4},{6,7},{7,6},{8,9},{9,8},{10,11... | collective-permute-start | bytes 786440 | tf_op jit(solution)/shard_map/ppermute | solution.py:335
  64.1 2.3 %copy-start.14 = (bf16[4,2,2,32,256]{4,3,2,1,0:T(8,128)(2,1)S(1)}, bf16[4,2,2,32,256]{4,3,2,1,0:T(8,128)(2,1)}, u32[]{:S(2)}) copy-start(bf16[4,2,2,32,256]{4,3,2,1,0:T(8,128)(2,1)} %get-tuple-element.53) | copy-start | bytes 786436
  65.2 10.1 %collective-permute-start.25 = (bf16[8,2,32,256]{3,2,1,0:T(8,128)(2,1)S(1)}, bf16[8,2,32,256]{3,2,1,0:T(8,128)(2,1)S(1)}, u32[]{:S(2)}, u32[]{:S(2)}) collective-permute-start(bf16[8,2,32,256]{3,2,1,0:T(8,128)(2,1)S(1)} %bitcast.73), channel_id=1, source_target_pairs={{0,1},{1,0},{2,3},{3,2},{4,5},{5,4},{6,7},{7,6},{8,9},{9,8},{10,11... | collective-permute-start | bytes 786440 | tf_op jit(solution)/shard_map/ppermute | solution.py:335
  65.9 2.4 %copy-start.12 = (bf16[4,2,2,32,256]{4,3,2,1,0:T(8,128)(2,1)S(1)}, bf16[4,2,2,32,256]{4,3,2,1,0:T(8,128)(2,1)}, u32[]{:S(2)}) copy-start(bf16[4,2,2,32,256]{4,3,2,1,0:T(8,128)(2,1)} %get-tuple-element.45) | copy-start | bytes 786436
  66.0 8.4 %collective-permute-start.23 = (bf16[8,2,32,256]{3,2,1,0:T(8,128)(2,1)S(1)}, bf16[8,2,32,256]{3,2,1,0:T(8,128)(2,1)S(1)}, u32[]{:S(2)}, u32[]{:S(2)}) collective-permute-start(bf16[8,2,32,256]{3,2,1,0:T(8,128)(2,1)S(1)} %fusion.6), channel_id=1, source_target_pairs={{0,6},{2,0},{4,2},{6,4},{1,7},{3,1},{5,3},{7,5},{8,14},{10,8},{12,... | collective-permute-start | bytes 786440 | tf_op jit(solution)/shard_map/ppermute | solution.py:331
  66.4 2.1 %copy-start.27 = (bf16[4,2,2,32,256]{4,3,2,1,0:T(8,128)(2,1)S(1)}, bf16[4,2,2,32,256]{4,3,2,1,0:T(8,128)(2,1)}, u32[]{:S(2)}) copy-start(bf16[4,2,2,32,256]{4,3,2,1,0:T(8,128)(2,1)} %get-tuple-element.42) | copy-start | bytes 786436
  66.4 8.8 %copy-start.25 = (bf16[4,2,2,32,256]{4,3,2,1,0:T(8,128)(2,1)S(1)}, bf16[4,2,2,32,256]{4,3,2,1,0:T(8,128)(2,1)}, u32[]{:S(2)}) copy-start(bf16[4,2,2,32,256]{4,3,2,1,0:T(8,128)(2,1)} %get-tuple-element.47) | copy-start | bytes 786436
  66.5 11.4 %collective-permute-start.27 = (bf16[8,2,32,256]{3,2,1,0:T(8,128)(2,1)S(1)}, bf16[8,2,32,256]{3,2,1,0:T(8,128)(2,1)S(1)}, u32[]{:S(2)}, u32[]{:S(2)}) collective-permute-start(bf16[8,2,32,256]{3,2,1,0:T(8,128)(2,1)S(1)} %fusion.3), channel_id=1, source_target_pairs={{0,2},{2,4},{4,6},{6,0},{1,3},{3,5},{5,7},{7,1},{8,10},{10,12},{12... | collective-permute-start | bytes 786440 | tf_op jit(solution)/shard_map/ppermute | solution.py:331
  68.3 9.9 %copy-start.24 = (bf16[4,2,2,32,256]{4,3,2,1,0:T(8,128)(2,1)S(1)}, bf16[4,2,2,32,256]{4,3,2,1,0:T(8,128)(2,1)}, u32[]{:S(2)}) copy-start(bf16[4,2,2,32,256]{4,3,2,1,0:T(8,128)(2,1)} %get-tuple-element.51) | copy-start | bytes 786436
  68.5 11.7 %collective-permute-start.16 = (bf16[8,2,32,256]{3,2,1,0:T(8,128)(2,1)S(1)}, bf16[8,2,32,256]{3,2,1,0:T(8,128)(2,1)S(1)}, u32[]{:S(2)}, u32[]{:S(2)}) collective-permute-start(bf16[8,2,32,256]{3,2,1,0:T(8,128)(2,1)S(1)} %bitcast.71), channel_id=1, source_target_pairs={{0,1},{1,0},{2,3},{3,2},{4,5},{5,4},{6,7},{7,6},{8,9},{9,8},{10,11... | collective-permute-start | bytes 786440 | tf_op jit(solution)/shard_map/ppermute | solution.py:335
  74.5 10.5 %collective-permute-start.18 = (bf16[8,2,32,256]{3,2,1,0:T(8,128)(2,1)S(1)}, bf16[8,2,32,256]{3,2,1,0:T(8,128)(2,1)S(1)}, u32[]{:S(2)}, u32[]{:S(2)}) collective-permute-start(bf16[8,2,32,256]{3,2,1,0:T(8,128)(2,1)S(1)} %fusion.10), channel_id=1, source_target_pairs={{0,2},{2,4},{4,6},{6,0},{1,3},{3,5},{5,7},{7,1},{8,10},{10,12},{12... | collective-permute-start | bytes 786440 | tf_op jit(solution)/shard_map/ppermute | solution.py:331
  75.3 9.6 %collective-permute-start.20 = (bf16[8,2,32,256]{3,2,1,0:T(8,128)(2,1)S(1)}, bf16[8,2,32,256]{3,2,1,0:T(8,128)(2,1)S(1)}, u32[]{:S(2)}, u32[]{:S(2)}) collective-permute-start(bf16[8,2,32,256]{3,2,1,0:T(8,128)(2,1)S(1)} %fusion.9), channel_id=1, source_target_pairs={{0,6},{2,0},{4,2},{6,4},{1,7},{3,1},{5,3},{7,5},{8,14},{10,8},{12,... | collective-permute-start | bytes 786440 | tf_op jit(solution)/shard_map/ppermute | solution.py:331
  77.9 10.4 %collective-permute-start.24 = (bf16[8,2,32,256]{3,2,1,0:T(8,128)(2,1)S(1)}, bf16[8,2,32,256]{3,2,1,0:T(8,128)(2,1)S(1)}, u32[]{:S(2)}, u32[]{:S(2)}) collective-permute-start(bf16[8,2,32,256]{3,2,1,0:T(8,128)(2,1)S(1)} %fusion.8), channel_id=1, source_target_pairs={{0,6},{2,0},{4,2},{6,4},{1,7},{3,1},{5,3},{7,5},{8,14},{10,8},{12,... | collective-permute-start | bytes 786440 | tf_op jit(solution)/shard_map/ppermute | solution.py:331
  78.4 6.5 %copy-start.7 = (bf16[8,2,32,256]{3,2,1,0:T(8,128)(2,1)}, bf16[8,2,32,256]{3,2,1,0:T(8,128)(2,1)S(1)}, u32[]{:S(2)}) copy-start(bf16[8,2,32,256]{3,2,1,0:T(8,128)(2,1)S(1)} %collective-permute-done.15.refs_2_) | copy-start | bytes 786436
  78.4 10.4 %collective-permute-start.28 = (bf16[8,2,32,256]{3,2,1,0:T(8,128)(2,1)S(1)}, bf16[8,2,32,256]{3,2,1,0:T(8,128)(2,1)S(1)}, u32[]{:S(2)}, u32[]{:S(2)}) collective-permute-start(bf16[8,2,32,256]{3,2,1,0:T(8,128)(2,1)S(1)} %fusion.5), channel_id=1, source_target_pairs={{0,2},{2,4},{4,6},{6,0},{1,3},{3,5},{5,7},{7,1},{8,10},{10,12},{12... | collective-permute-start | bytes 786440 | tf_op jit(solution)/shard_map/ppermute | solution.py:331
  80.2 4.7 %copy-start.19 = (bf16[8,2,32,256]{3,2,1,0:T(8,128)(2,1)}, bf16[8,2,32,256]{3,2,1,0:T(8,128)(2,1)S(1)}, u32[]{:S(2)}) copy-start(bf16[8,2,32,256]{3,2,1,0:T(8,128)(2,1)S(1)} %collective-permute-done.16.refs_3_) | copy-start | bytes 786436
  84.9 0.7 copy-start.22
  84.9 0.8 copy-start.23
